TPU v7x, 32 devices: a whole 2x2x4 slice. The times are simulated.
32 devices in a mesh: blk: 8 (over z, x), rep: 4 (over y, core).
Axes of the slice: x: 2, y: 2, z: 4, core: 2. Of those that a mesh axis runs over, the one named last changes fastest.
Arguments:
- amplitudes: float32 [64, 64, 16, 512], P('blk', None, 'rep'), may hold values from -6 to 6
- cycle_integrals: float32 [32, 64, 64, 512], P('rep', None, 'blk'), may hold values from -0.046875 to 0.046875
- cross_integrals: float32 [32, 64, 64, 512], P('rep', None, 'blk'), may hold values from -0.046875 to 0.046875
- occ_energy: float32 [64], replicated, may hold values from -2 to -0.5
- vir_energy_a: float32 [32], replicated, may hold values from 0.2 to 3
- vir_energy_b: float32 [16], replicated, may hold values from 0.2 to 3
Outputs:
- update: float32 [64, 32, 16, 64], P('blk', 'rep')
- residual_rms: float32 [], replicated
All inputs are finite; a program needn't handle non-finite values.
Results may differ from a plain program's by a relative error of at most 0.0006.
Values sent between devices are 32-bit elements; how exact they have to be, the bound alone decides.
No kernel may reach another device: no remote copies, remote signals or barrier semaphores. Data moves between devices by JAX's collectives and lax.ppermute only.
A program may use at most 128 MiB of HBM per device.

v0:
```python
import jax
import jax.numpy as jnp
from jax import lax
from jax.sharding import PartitionSpec as P


def per_device(
    amplitudes, cycle_integrals, cross_integrals, occ_energy, vir_energy_a, vir_energy_b
):
    highest = lax.Precision.HIGHEST
    whole = lax.all_gather(amplitudes, "rep", axis=2, tiled=True)
    moved = lax.all_to_all(whole, "blk", split_axis=1, concat_axis=0, tiled=True)
    crossed = jnp.swapaxes(moved, 0, 1)
    rows = amplitudes.shape[0]
    part = cycle_integrals
    cycle = lax.psum_scatter(
        jnp.einsum("aikc,kjbc->iabj", part, whole, precision=highest),
        "blk",
        scatter_dimension=0,
        tiled=True,
    )
    part = cross_integrals
    cross = lax.psum_scatter(
        jnp.einsum("aikc,kjbc->iabj", part, crossed, precision=highest),
        "blk",
        scatter_dimension=0,
        tiled=True,
    )
    residual = cycle + cross
    a_count = cycle_integrals.shape[0]
    occ_local = lax.dynamic_slice_in_dim(occ_energy, lax.axis_index("blk") * rows, rows, 0)
    vir_local = lax.dynamic_slice_in_dim(vir_energy_a, lax.axis_index("rep") * a_count, a_count, 0)
    denom = (
        occ_local[:, None, None, None]
        + occ_energy[None, None, None, :]
        - vir_local[None, :, None, None]
        - vir_energy_b[None, None, :, None]
    )
    update = residual / denom
    squares = lax.psum(jnp.sum(residual * residual), ("blk", "rep"))
    total_count = (
        occ_energy.shape[0] * occ_energy.shape[0] * vir_energy_a.shape[0] * vir_energy_b.shape[0]
    )
    residual_rms = jnp.sqrt(squares / total_count)
    return (update, residual_rms)


def solution(mesh):
    return jax.shard_map(
        per_device,
        mesh=mesh,
        in_specs=(
            P("blk", None, "rep", None),
            P("rep", None, "blk", None),
            P("rep", None, "blk", None),
            P(),
            P(),
            P(),
        ),
        out_specs=(P("blk", "rep", None, None), P()),
        check_vma=False,
    )
```

profile of v0, /device:TPU:0, one launch (start us, length us, event | category | flops | bytes accessed | tf_op | source)
XLA Modules:
  0.0 777.8 jit_solution(626042047397392422)
XLA Ops:
  7.2 0.0 all-gather.2.cloned.1.call-start
  7.2 5.5 copy.19
  12.7 0.0 all-gather.2.cloned.1.call-update
  12.7 0.0 reduce-scatter.2.cloned.1.call-start
  12.8 108.7 %all-gather.2.cloned.1.call-done = f32[8,64,16,512]{3,1,0,2:T(8,128)} async-done(((f32[8,64,4,512]{3,1,0,2:T(8,128)}), f32[8,64,16,512]{3,1,0,2:T(8,128)}) %all-gather.2.cloned.1.call-update) | async-done | bytes 16777232 | tf_op jit(solution)/shard_map/all_gather | solution.py:11
  121.5 15.2 %copy.21 = f32[8,64,16,512]{3,0,2,1:T(8,128)S(1)} copy(f32[8,64,16,512]{3,1,0,2:T(8,128)} %all-gather.2.cloned.1.call-done) | data formatting | bytes 33554432 | tf_op jit(solution)/shard_map/all_gather | solution.py:11
  136.7 368.5 %all_to_all.18 = f32[8,64,16,512]{3,0,2,1:T(8,128)S(1)} all-to-all(f32[8,64,16,512]{3,0,2,1:T(8,128)S(1)} %copy.21), channel_id=1, replica_groups=mesh['blk'=8,'rep'=4] {'blk'}, dimensions={1} | all-to-all | bytes 33554432 | tf_op jit(solution)/shard_map/all_to_all | solution.py:12
  505.3 11.7 %copy.22 = f32[8,8,8,16,512]{4,3,2,0,1:T(8,128)} copy(f32[8,8,8,16,512]{4,0,3,2,1:T(8,128)S(1)} %bitcast.38) | data formatting | bytes 33554432 | tf_op jit(solution)/shard_map/all_to_all | solution.py:12
  516.9 58.6 %fusion.8 = f32[64,16,8,64]{3,1,2,0:T(8,128)S(1)} fusion(f32[8,64,16,512,1]{3,2,0,4,1:T(8,128)} %bitcast.41, f32[8,64,8,512]{3,2,1,0:T(8,128)} %param.8), kind=kOutput, calls=%fused_computation.9 | convolution fusion | flops 25769803776 | bytes 27262976 | tf_op jit(solution)/shard_map/aikc,kjbc->iabj/dot_general | solution.py:24
  575.5 0.0 slice-done
  575.5 0.0 slice-done.1
  575.6 0.0 slice-done.2
  575.6 0.0 slice-done.3
  575.6 58.2 %fusion.7 = f32[64,8,16,64]{0,3,1,2:T(8,128)} fusion(f32[64,16,8,64]{3,1,2,0:T(8,128)S(1)} %fusion.8, f32[8,64,8,512]{3,2,1,0:T(8,128)} %param.7, f32[8,64,16,512]{3,1,0,2:T(8,128)S(1)} %bitcast.40), kind=kOutput, calls=%fused_computation.8 | convolution fusion | flops 25770328064 | bytes 29360128 | tf_op jit(solution)/shard_map/aikc,kjbc->iabj/dot_general | solution.py:17
  633.8 5.8 copy.25
  639.6 0.0 reduce-scatter.2.cloned.1.call-update
  639.6 0.1 dynamic_slice.7
  639.7 0.1 dynamic_slice.6
  639.8 0.1 broadcast_add_fusion
  639.9 0.1 broadcast_subtract_fusion
  639.9 86.0 %reduce-scatter.2.cloned.1.call-done = f32[8,8,16,64]{3,2,1,0:T(8,128)} async-done(((f32[64,8,16,64]{3,2,1,0:T(8,128)}), f32[8,8,16,64]{3,2,1,0:T(8,128)}) %reduce-scatter.2.cloned.1.call-update) | async-done | bytes 262160 | tf_op jit(solution)/shard_map/reduce_scatter | solution.py:16
  726.0 0.0 copy-done
  726.0 2.6 multiply_reduce_fusion
  728.6 40.5 %psum.7 = f32[]{:T(128)} all-reduce(f32[]{:T(128)} %get-tuple-element.4), channel_id=1, replica_groups=mesh['blk'=8,'rep'=4] {'blk','rep'}, use_global_device_ids=true, to_apply=%region_3.0 | all-reduce | flops 1 | bytes 8 | tf_op jit(solution)/shard_map/psum | solution.py:40
  (10 shorter events, 0.0 us)
Async XLA Ops:
  7.2 114.3 %all-gather.2.cloned.1.call-start = ((), (), s32[]{:S(2)}) async-start(), calls=%async_computation.2 | async-start | bytes 20971520 | tf_op jit(solution)/shard_map/all_gather | solution.py:11
  12.7 713.3 %reduce-scatter.2.cloned.1.call-start = ((), (), s32[]{:S(2)}) async-start(), calls=%async_computation.3 | async-start | bytes 4718592 | tf_op jit(solution)/shard_map/reduce_scatter | solution.py:16
  505.3 70.3 %slice-start = ((s8[16777216]{0:T(1024)(128)(4,1)}), s8[4194304]{0:T(1024)(128)(4,1)S(1)}, s32[]{:S(2)}) async-start(s8[16777216]{0:T(1024)(128)(4,1)} %bitcast.39), calls=%async_computation.4 | async-start | bytes 8388608
  505.3 70.3 %slice-start.1 = ((s8[16777216]{0:T(1024)(128)(4,1)}), s8[4194304]{0:T(1024)(128)(4,1)S(1)}, s32[]{:S(2)}) async-start(s8[16777216]{0:T(1024)(128)(4,1)} %bitcast.39), calls=%async_computation.5 | async-start | bytes 8388608
  516.9 58.6 %slice-start.2 = ((s8[16777216]{0:T(1024)(128)(4,1)}), s8[4194304]{0:T(1024)(128)(4,1)S(1)}, s32[]{:S(2)}) async-start(s8[16777216]{0:T(1024)(128)(4,1)} %bitcast.39), calls=%async_computation.6 | async-start | bytes 8388608
  516.9 58.6 %slice-start.3 = ((s8[16777216]{0:T(1024)(128)(4,1)}), s8[4194304]{0:T(1024)(128)(4,1)S(1)}, s32[]{:S(2)}) async-start(s8[16777216]{0:T(1024)(128)(4,1)} %bitcast.39), calls=%async_computation.7 | async-start | bytes 8388608
  633.8 5.8 copy-start.2
  633.8 5.9 copy-start.1
  633.8 92.2 %copy-start = (f32[16]{0:T(128)S(1)}, f32[16]{0:T(128)}, u32[]{:S(2)}) copy-start(f32[16]{0:T(128)} %param.11) | copy-start | bytes 196
Sparse Core Ops, SparseCore 0:
  12.8 108.6 all-gather.1
  639.7 86.1 reduce-scatter.1
where the time goes:
time: 778 us
  blocking collectives  409 us (53%)
  waiting for transfers between devices  195 us (25%)
  matrix products  117 us (15%)
  local copies, waits for them, and re-layouts  38.3 us (5%)
  between operations  15.9 us (2%)
    all_to_all x1, blocking collectives, per_device(): lax.all_to_all(whole, 'blk', split_axis=1, concat_axis=0, tiled=True)  369 us
    all_gather x1, waiting for transfers between devices, per_device(): whole = lax.all_gather(amplitudes, 'rep', axis=2, tiled=True)  109 us
    reduce_scatter x1, waiting for transfers between devices, per_device(): lax.psum_scatter(jnp.einsum('aikc,kjbc->iabj', part, whole, precision=hig...  86 us
    dot_general x1, matrix products, per_device(): jnp.einsum('aikc,kjbc->iabj', part, crossed, precision=highest)  58.6 us
    dot_general x1, matrix products, per_device(): jnp.einsum('aikc,kjbc->iabj', part, whole, precision=highest)  58.2 us
    psum x1, blocking collectives, per_device(): squares = lax.psum(jnp.sum(residual * residual), ('blk', 'rep'))  40.5 us
  transfers between devices with their start and end apart: 2, of which 2 were waited for; matrix products, arithmetic and copies ran while one was open for 0% of the time, Pallas kernels for 0%

commit v1 on v0

v1 whole, which is shorter than its diff:
```python
import functools

import jax
import jax.numpy as jnp
from jax import lax
from jax.experimental import pallas as pl
from jax.experimental.pallas import tpu as pltpu
from jax.sharding import PartitionSpec as P

VMEM = 48 * 2**20


def split(x):
    high = x.astype(jnp.bfloat16)
    return high, (x - high.astype(jnp.float32)).astype(jnp.bfloat16)


def split_kernel(in_ref, high_ref, low_ref):
    high_ref[...], low_ref[...] = split(jnp.swapaxes(in_ref[...], 0, 1))


def split_integrals(integrals):
    a, i, k, c = integrals.shape
    tile = 64
    half = jax.ShapeDtypeStruct((k, a * i, c), jnp.bfloat16)
    return pl.pallas_call(
        split_kernel,
        grid=(a * i // tile,),
        in_specs=[pl.BlockSpec((tile, k, c), lambda n: (n, 0, 0))],
        out_specs=[pl.BlockSpec((k, tile, c), lambda n: (0, n, 0))] * 2,
        out_shape=[half, half],
        compiler_params=pltpu.CompilerParams(vmem_limit_bytes=VMEM),
        cost_estimate=pl.CostEstimate(
            flops=4 * integrals.size, bytes_accessed=8 * integrals.size, transcendentals=0
        ),
    )(integrals.reshape(a * i, k, c))


def take_kernel(groups, count, where_ref, in_ref, *out_refs):
    for n in range(count):

        @pl.when(pl.program_id(0) == n)
        def _(n=n):
            for group, out_ref in zip(groups, out_refs):
                if n in group:
                    out_ref[0] = in_ref[:, 0]


def take_blocks(array, where, groups):
    k, q, j, b, c = array.shape
    count = where.shape[0]

    def at(group):
        first, last = group[0], group[-1]
        return lambda n, where: (jnp.clip(n, first, last) - first, 0, 0, 0, 0)

    return pl.pallas_call(
        functools.partial(take_kernel, groups, count),
        grid_spec=pltpu.PrefetchScalarGridSpec(
            num_scalar_prefetch=1,
            grid=(count,),
            in_specs=[pl.BlockSpec((k, 1, j, b, c), lambda n, where: (0, where[n], 0, 0, 0))],
            out_specs=[pl.BlockSpec((1, k, j, b, c), at(group)) for group in groups],
        ),
        out_shape=[
            jax.ShapeDtypeStruct((len(group), k, j, b, c), array.dtype) for group in groups
        ],
        compiler_params=pltpu.CompilerParams(vmem_limit_bytes=VMEM),
        cost_estimate=pl.CostEstimate(
            flops=0, bytes_accessed=12 * count * k * j * b * c, transcendentals=0
        ),
    )(where, array)


def product_kernel(places, first, p_ref, high_ref, low_ref, *refs):
    n = len(places)
    out_ref, t_high, t_low = refs[-3:]
    for ref, (crossed, e, width, ds) in zip(refs, places):
        for at, d in enumerate(ds):
            x = ref[at, :, 0] if crossed else ref[at, 0]
            rows = x.shape[0] * x.shape[1]
            high, low = split(x.reshape(rows, x.shape[2]))
            start = e * width
            if d is not None:
                start = pl.multiple_of(start + (p_ref[0] ^ d) * rows, 32)
            t_high[pl.ds(start, rows), :] = high
            t_low[pl.ds(start, rows), :] = low

    @pl.when(pl.program_id(0) == 0)
    def _():
        out_ref[...] = jnp.zeros_like(out_ref) if first else refs[n][...]

    dot = functools.partial(
        lax.dot_general,
        dimension_numbers=(((1,), (1,)), ((), ())),
        preferred_element_type=jnp.float32,
    )
    out_ref[...] += (
        dot(high_ref[0], t_high[...])
        + dot(high_ref[0], t_low[...])
        + dot(low_ref[0], t_high[...])
    )


def product(halves, sources, start, p, width, columns):
    high, low = halves
    steps, m, c = high.shape
    specs = [pl.BlockSpec((1, m, c), lambda k, p: (k, 0, 0))] * 2
    operands = [high, low]
    places = []
    for stack, crossed, e, ds in sources:
        s = stack.shape
        n = len(ds)
        if crossed:
            specs.append(pl.BlockSpec((n, s[1], 1, s[3], c), lambda k, p: (0, 0, k, 0, 0)))
        else:
            specs.append(pl.BlockSpec((n, 1, s[2], s[3], c), lambda k, p: (0, k, 0, 0, 0)))
        operands.append(stack)
        places.append((crossed, e, width, ds))
    whole = pl.BlockSpec((m, columns), lambda k, p: (0, 0))
    if start is not None:
        specs.append(whole)
        operands.append(start)
    return pl.pallas_call(
        functools.partial(product_kernel, places, start is None),
        grid_spec=pltpu.PrefetchScalarGridSpec(
            num_scalar_prefetch=1,
            grid=(steps,),
            in_specs=specs,
            out_specs=whole,
            scratch_shapes=[pltpu.VMEM((columns, c), jnp.bfloat16)] * 2,
        ),
        out_shape=jax.ShapeDtypeStruct((m, columns), jnp.float32),
        compiler_params=pltpu.CompilerParams(vmem_limit_bytes=VMEM),
        cost_estimate=pl.CostEstimate(
            flops=6 * steps * m * c * columns,
            bytes_accessed=4 * steps * c * (m + columns) + 8 * m * columns,
            transcendentals=0,
        ),
    )(p, *operands)


def shift(value, axis, d):
    size = lax.axis_size(axis)
    return lax.ppermute(value, axis, [(i, i ^ d) for i in range(size)])


def after(value, *others):
    return lax.optimization_barrier((value,) + others)[0]


def scatter_sum(part, bits):
    size, p = lax.axis_size("blk"), lax.axis_index("blk")
    a, i, n = part.shape
    top = size.bit_length() - 1
    part = part.reshape((a,) + (2,) * top + (i // size, n))
    left = list(range(top - 1, -1, -1))
    for bit in bits:
        axis = 1 + left.index(bit)
        mine = (p >> bit) & 1
        away = lax.dynamic_index_in_dim(part, 1 - mine, axis, keepdims=False)
        keep = lax.dynamic_index_in_dim(part, mine, axis, keepdims=False)
        part = keep + shift(away, "blk", 1 << bit)
        left.remove(bit)
    return part


def all_sum(value):
    value = value.reshape(1, 1)
    for axis in ("rep", "blk"):
        d = 1
        while d < lax.axis_size(axis):
            value = value + shift(value, axis, d)
            d *= 2
    return value[0, 0]


def parts_small(amplitudes, cyc, crs, p1, m, width):
    nb = lax.axis_size("blk")
    rows = amplitudes.shape[0]
    mine = amplitudes.reshape((rows, nb, rows) + amplitudes.shape[2:])
    own_a, own_x, t2, t4 = take_blocks(
        mine, p1 ^ jnp.array([1, 3, 2, 4], jnp.int32), [(0, 1, 2, 3), (0, 1), (2,), (3,)]
    )
    own_b, t5, t6, t7 = take_blocks(
        mine, p1 ^ jnp.array([5, 6, 7, 0], jnp.int32), [(0, 1, 2, 3), (0,), (1,), (2,)]
    )
    y_a = shift(own_a, "rep", 2)
    c5 = shift(t5, "blk", 5)
    c6 = shift(t6, "blk", 6)
    row1 = shift(amplitudes[None], "rep", 1)
    u = shift(own_x, "blk", 1)
    c7 = shift(after(t7, c5), "blk", 7)
    y_b = shift(after(own_b, row1), "rep", 2)
    v = shift(jnp.concatenate([t2, u[1:]]), "blk", 2)
    c4 = shift(after(t4, c6), "blk", 4)
    late0 = jnp.concatenate([c5, c6, c7])
    late2 = shift(late0, "rep", 2)
    zu = shift(after(y_a[:2], v), "blk", 1)
    zv = shift(jnp.concatenate([y_a[2:3], zu[1:]]), "blk", 2)
    z4 = shift(after(y_a[3:4], c4), "blk", 4)
    early2 = jnp.concatenate([zu[:1], zv, z4])
    col0 = jnp.concatenate([own_b[3:], u[:1], v, c4, late0])
    col1 = shift(col0, "rep", 1)
    row3a = shift(y_a, "rep", 1)
    row3b = shift(y_b, "rep", 1)
    early3 = shift(early2, "rep", 1)
    late3 = shift(late2, "rep", 1)

    columns = 2 * width
    natural = (None,)
    part0 = product(
        cyc,
        [(amplitudes[None], False, 0, natural), (row1, False, 1, natural)],
        None,
        p1,
        width,
        columns,
    )
    order = (0, 1, 2, 3, 4, 5, 6, 7)
    part0 = product(
        crs, [(col0, True, 0, order), (col1, True, 1, order)], part0, p1, width, columns
    )
    first, second, early, late = (1, 3, 2, 4), (5, 6, 7, 0), (1, 2, 3, 4), (5, 6, 7)
    part1 = product(
        cyc,
        [
            (y_a, False, 0, first),
            (y_b, False, 0, second),
            (row3a, False, 1, first),
            (row3b, False, 1, second),
        ],
        None,
        p1,
        width,
        columns,
    )
    part1 = product(
        crs,
        [
            (y_b[3:], True, 0, (0,)),
            (early2, True, 0, early),
            (late2, True, 0, late),
            (row3b[3:], True, 1, (0,)),
            (early3, True, 1, early),
            (late3, True, 1, late),
        ],
        part1,
        p1,
        width,
        columns,
    )
    return [((0, 1), part0), ((2, 3), part1)]


def parts_large(amplitudes, cyc, crs, p1, m, width):
    nr = lax.axis_size("rep")
    column = lax.all_to_all(amplitudes, "blk", split_axis=1, concat_axis=0, tiled=True)
    parts = []
    for e in range(nr):
        row, col = amplitudes, column
        if e:
            row, col = shift(row, "rep", e), shift(col, "rep", e)
        part = product(cyc, [(row[None], False, 0, (None,))], None, p1, width, width)
        part = product(crs, [(col[None], True, 0, (None,))], part, p1, width, width)
        parts.append(((e,), part))
    return parts


def per_device(
    amplitudes, cycle_integrals, cross_integrals, occ_energy, vir_energy_a, vir_energy_b
):
    nb, nr = lax.axis_size("blk"), lax.axis_size("rep")
    p, r = lax.axis_index("blk"), lax.axis_index("rep")
    rows, o_count, b_count, _ = amplitudes.shape
    a_count = cycle_integrals.shape[0]
    cyc = split_integrals(cycle_integrals)
    crs = split_integrals(cross_integrals)
    p1 = p.astype(jnp.int32).reshape(1)
    width = o_count * b_count
    make = parts_small if (nb, nr, rows) == (8, 4, 8) else parts_large
    residual = jnp.zeros((rows, a_count, nr * b_count, o_count), jnp.float32)
    top = nb.bit_length() - 1
    for es, part in make(amplitudes, cyc, crs, p1, a_count * o_count, width):
        part = scatter_sum(part.reshape(a_count, o_count, -1), range(top))
        part = part.reshape(a_count, rows, len(es), o_count, b_count)
        for at, e in enumerate(es):
            residual = lax.dynamic_update_slice_in_dim(
                residual,
                jnp.transpose(part[:, :, at], (1, 0, 3, 2)),
                (r ^ e) * b_count,
                2,
            )
    occ_local = lax.dynamic_slice_in_dim(occ_energy, p * rows, rows, 0)
    vir_local = lax.dynamic_slice_in_dim(vir_energy_a, r * a_count, a_count, 0)
    denom = (
        occ_local[:, None, None, None]
        + occ_energy[None, None, None, :]
        - vir_local[None, :, None, None]
        - vir_energy_b[None, None, :, None]
    )
    update = residual / denom
    squares = all_sum(jnp.sum(residual * residual))
    total_count = (
        occ_energy.shape[0] * occ_energy.shape[0] * vir_energy_a.shape[0] * vir_energy_b.shape[0]
    )
    residual_rms = jnp.sqrt(squares / total_count)
    return (update, residual_rms)


def solution(mesh):
    return jax.shard_map(
        per_device,
        mesh=mesh,
        in_specs=(
            P("blk", None, "rep", None),
            P("rep", None, "blk", None),
            P("rep", None, "blk", None),
            P(),
            P(),
            P(),
        ),
        out_specs=(P("blk", "rep", None, None), P()),
        check_vma=False,
    )
```

time: 778 us -> 336 us (0.43)
  blocking collectives: 409 us -> 0 us
  matrix products: 117 us -> 0 us
  Pallas kernels: 0 us -> 75.2 us
  starting transfers between devices: 0.08 us -> 46.7 us
  waiting for transfers between devices: 195 us -> 163 us
  other arithmetic: 2.75 us -> 14.2 us
  between operations: 15.9 us -> 5.88 us
  local copies, waits for them, and re-layouts: 38.3 us -> 28.6 us
    all_to_all x1 -> x0, blocking collectives: 369 us -> none  [per_device(): lax.all_to_all(whole, 'blk', split_axis=1, concat_axis=0, tiled=True)]
    ppermute x0 -> x29, waiting for transfers between devices: none -> 163 us  [shift(): return lax.ppermute(value, axis, [(i, i ^ d) for i in range(size)])]
    dot_general x2 -> x0, matrix products: 117 us -> none  [the longest x1 58.6 us: per_device(): jnp.einsum('aikc,kjbc->iabj', part, crossed, precision=highest)]
    all_gather x1 -> x0, waiting for transfers between devices: 109 us -> none  [per_device(): whole = lax.all_gather(amplitudes, 'rep', axis=2, tiled=True)]
    reduce_scatter x1 -> x0, waiting for transfers between devices: 86 us -> none  [per_device(): lax.psum_scatter(jnp.einsum('aikc,kjbc->iabj', part, whole, precision=hig...]
    pallas_call x0 -> x8, Pallas kernels: none -> 75.2 us  [the longest x4 49.1 us: product(): pl.pallas_call(functools.partial(product_kernel, places, start is None),...]
    ppermute x0 -> x29, starting transfers between devices: none -> 46.7 us  [shift(): return lax.ppermute(value, axis, [(i, i ^ d) for i in range(size)])]
    psum x1 -> x0, blocking collectives: 40.5 us -> none  [per_device(): squares = lax.psum(jnp.sum(residual * residual), ('blk', 'rep'))]
  transfers between devices with their start and end apart: 2 -> 29, of which waited for: 2 -> 18; matrix products, arithmetic and copies ran while one was open for 0% -> 9% of each run, Pallas kernels for 0% -> 18%
where the time goes in v1:
time: 336 us; the launch traced here: 334 us
  waiting for transfers between devices  163 us (49%)
  Pallas kernels  75.2 us (22%)
  starting transfers between devices  46.7 us (14%)
  local copies, waits for them, and re-layouts  28.6 us (9%)
  other arithmetic  14.2 us (4%)
  between operations  5.88 us (2%)
    ppermute x29, waiting for transfers between devices, shift(): return lax.ppermute(value, axis, [(i, i ^ d) for i in range(size)])  163 us
    pallas_call x4, Pallas kernels, product(): pl.pallas_call(functools.partial(product_kernel, places, start is None),...  49.1 us
    ppermute x29, starting transfers between devices, shift(): return lax.ppermute(value, axis, [(i, i ^ d) for i in range(size)])  46.7 us
    pallas_call x2, Pallas kernels, split_integrals(): pl.pallas_call(split_kernel, grid=(a * i // tile,), in_specs=[pl.BlockSpe...  18.6 us
    unnamed x25, local copies, waits for them, and re-layouts  7.52 us
    pallas_call x2, Pallas kernels, take_blocks(): pl.pallas_call(functools.partial(take_kernel, groups, count), grid_spec=p...  7.43 us
    transpose x6, local copies, waits for them, and re-layouts, per_device(): jnp.transpose(part[:, :, at], (1, 0, 3, 2))  7.35 us
  transfers between devices with their start and end apart: 29, of which 18 were waited for; matrix products, arithmetic and copies ran while one was open for 9% of the time, Pallas kernels for 18%

profile of v1, /device:TPU:0, one launch (start us, length us, event | category | flops | bytes accessed | tf_op | source)
XLA Modules:
  0.0 333.8 jit_solution(6724134923618808110)
XLA Ops:
  1.5 3.0 shard_map.97
  7.5 4.4 %shard_map.96 = (f32[4,8,8,4,512]{4,3,2,1,0:T(4,128)}, f32[1,8,8,4,512]{4,3,2,1,0:T(4,128)S(1)}, f32[1,8,8,4,512]{4,3,2,1,0:T(4,128)S(1)}, f32[1,8,8,4,512]{4,3,2,1,0:T(4,128)S(1)}) custom-call(s32[4]{0:T(128)S(1)} %get-tuple-element.49.where_ref, f32[8,8,8,4,512]{4,3,2,1,0:T(4,128)} %bitcast.64), custom_call_target="tpu_custom_call" | custom-call | bytes 6291456 | tf_op jit(solution)/shard_map/pallas_call | solution.py:57
  13.8 16.9 %collective-permute-done = f32[2,8,8,4,512]{4,3,2,1,0:T(4,128)S(1)} collective-permute-done((f32[2,8,8,4,512]{4,3,2,1,0:T(4,128)S(1)}, f32[2,8,8,4,512]{4,3,2,1,0:T(4,128)S(1)}, u32[]{:S(2)}, u32[]{:S(2)}) %collective-permute-start) | collective-permute-done | bytes 1048608 | tf_op jit(solution)/shard_map/ppermute | solution.py:145
  38.8 32.8 %collective-permute-done.2 = f32[1,8,8,4,512]{4,3,2,1,0:T(4,128)S(1)} collective-permute-done((f32[1,8,8,4,512]{4,3,2,1,0:T(4,128)S(1)}, f32[1,8,8,4,512]{4,3,2,1,0:T(4,128)S(1)}, u32[]{:S(2)}, u32[]{:S(2)}) %collective-permute-start.2) | collective-permute-done | bytes 524320 | tf_op jit(solution)/shard_map/ppermute | solution.py:145
  71.6 27.0 %collective-permute-done.4 = f32[1,8,8,4,512]{4,3,2,1,0:T(4,128)S(1)} collective-permute-done((f32[1,8,8,4,512]{4,3,2,1,0:T(4,128)S(1)}, f32[1,8,8,4,512]{4,3,2,1,0:T(4,128)S(1)}, u32[]{:S(2)}, u32[]{:S(2)}) %collective-permute-start.4) | collective-permute-done | bytes 524320 | tf_op jit(solution)/shard_map/ppermute | solution.py:145
  98.6 3.9 %collective-permute-start.5 = (f32[1,8,8,4,512]{4,3,2,1,0:T(4,128)S(1)}, f32[1,8,8,4,512]{4,3,2,1,0:T(4,128)S(1)}, u32[]{:S(2)}, u32[]{:S(2)}) collective-permute-start(f32[1,8,8,4,512]{4,3,2,1,0:T(4,128)S(1)} %get-tuple-element.29), channel_id=1, source_target_pairs={{0,28},{4,24},{8,20},{12,16},{16,12},{20,8},{24,4},{28,0},{1,29},{... | collective-permute-start | bytes 1572872 | tf_op jit(solution)/shard_map/ppermute | solution.py:145
  103.6 10.9 %collective-permute-done.3 = f32[1,8,8,4,512]{4,3,2,1,0:T(4,128)S(1)} collective-permute-done((f32[1,8,8,4,512]{4,3,2,1,0:T(4,128)S(1)}, f32[1,8,8,4,512]{4,3,2,1,0:T(4,128)S(1)}, u32[]{:S(2)}, u32[]{:S(2)}) %collective-permute-start.3) | collective-permute-done | bytes 524320 | tf_op jit(solution)/shard_map/ppermute | solution.py:145
  122.2 21.5 %collective-permute-done.13 = f32[2,8,8,4,512]{4,3,2,1,0:T(4,128)S(1)} collective-permute-done((f32[2,8,8,4,512]{4,3,2,1,0:T(4,128)S(1)}, f32[2,8,8,4,512]{4,3,2,1,0:T(4,128)S(1)}, u32[]{:S(2)}, u32[]{:S(2)}) %collective-permute-start.13) | collective-permute-done | bytes 1048608 | tf_op jit(solution)/shard_map/ppermute | solution.py:145
  145.8 10.2 %collective-permute-start.14 = (f32[2,8,8,4,512]{4,3,2,1,0:T(4,128)}, f32[2,8,8,4,512]{4,3,2,1,0:T(4,128)}, u32[]{:S(2)}, u32[]{:S(2)}) collective-permute-start(f32[2,8,8,4,512]{4,3,2,1,0:T(4,128)} %pad_maximum_fusion.3), channel_id=1, source_target_pairs={{0,8},{4,12},{8,0},{12,4},{16,24},{20,28},{24,16},{28,20},{1,9},{5... | collective-permute-start | bytes 3145736 | tf_op jit(solution)/shard_map/ppermute | solution.py:145
  157.2 8.7 %shard_map.98 = (bf16[8,512,512]{2,1,0:T(8,128)(2,1)S(1)}, bf16[8,512,512]{2,1,0:T(8,128)(2,1)}) custom-call(f32[512,8,512]{2,1,0:T(8,128)} %bitcast.67), custom_call_target="tpu_custom_call" | custom-call | flops 8388608 | bytes 16777216 | tf_op jit(solution)/shard_map/pallas_call | solution.py:26
  165.9 9.9 %shard_map.95 = (bf16[8,512,512]{2,1,0:T(8,128)(2,1)S(1)}, bf16[8,512,512]{2,1,0:T(8,128)(2,1)}) custom-call(f32[512,8,512]{2,1,0:T(8,128)} %bitcast.68), custom_call_target="tpu_custom_call" | custom-call | flops 8388608 | bytes 16777216 | tf_op jit(solution)/shard_map/pallas_call | solution.py:26
  179.8 10.0 %collective-permute-done.15 = f32[1,8,8,4,512]{4,3,2,1,0:T(4,128)} collective-permute-done((f32[1,8,8,4,512]{4,3,2,1,0:T(4,128)}, f32[1,8,8,4,512]{4,3,2,1,0:T(4,128)}, u32[]{:S(2)}, u32[]{:S(2)}) %collective-permute-start.15) | collective-permute-done | bytes 524320 | tf_op jit(solution)/shard_map/ppermute | solution.py:145
  190.5 3.6 %pad_maximum_fusion.refs_1_ = f32[4,8,8,4,512]{4,3,2,1,0:T(4,128)} fusion(f32[1,8,8,4,512]{4,3,2,1,0:T(4,128)} %collective-permute-done.15, f32[2,8,8,4,512]{4,3,2,1,0:T(4,128)} %collective-permute-done.14, f32[1,8,8,4,512]{4,3,2,1,0:T(4,128)S(1)} %copy-done.6), kind=kLoop, calls=%fused_computation | loop fusion | flops 1048576 | bytes 4194304 | tf_op jit(solution)/shard_map/concatenate | solution.py:202
  194.2 11.9 %shard_map.99.refs_2_ = f32[512,512]{1,0:T(8,128)S(1)} custom-call(s32[1]{0:T(128)} %bitcast.p_ref, bf16[8,512,512]{2,1,0:T(8,128)(2,1)S(1)} %get-tuple-element.30.high_ref, bf16[8,512,512]{2,1,0:T(8,128)(2,1)} %get-tuple-element.31.low_ref, f32[1,8,64,4,512]{4,3,2,1,0:T(4,128)} %bitcast.65, f32[1,8,64,4,512]{4,3,2,1,0:T(4,128)} %collective-permute-done.7.refs_1_), custom_call_target="tpu_custom_call" | custom-call | flops 6442450944 | bytes 18874368 | tf_op jit(solution)/shard_map/pallas_call | solution.py:124
  206.7 12.6 %shard_map.100 = f32[512,512]{1,0:T(8,128)S(1)} custom-call(s32[1]{0:T(128)} %bitcast.p_ref, bf16[8,512,512]{2,1,0:T(8,128)(2,1)} %copy-done, bf16[8,512,512]{2,1,0:T(8,128)(2,1)} %get-tuple-element.20.low_ref, f32[8,8,8,4,512]{4,3,2,1,0:T(4,128)} %constant_dynamic-update-slice_fusion.refs_0_, f32[8,8,8,4,512]{4,3,2,1,0:T(4,128)} %collective-permute-done.6.refs_1_, ...), custom_call_target="tpu_custom_call" | custom-call | flops 6442450944 | bytes 18874368 | tf_op jit(solution)/shard_map/pallas_call | solution.py:124
  220.7 13.6 %collective-permute-done.8 = f32[8,2,2,8,512]{4,3,2,1,0:T(8,128)} collective-permute-done((f32[8,2,2,8,512]{4,3,2,1,0:T(8,128)}, f32[8,2,2,8,512]{4,3,2,1,0:T(8,128)}, u32[]{:S(2)}, u32[]{:S(2)}) %collective-permute-start.8) | collective-permute-done | bytes 524320 | tf_op jit(solution)/shard_map/ppermute | solution.py:145
  237.2 3.6 %collective-permute-start.9 = (f32[8,2,8,512]{3,2,1,0:T(8,128)S(1)}, f32[8,2,8,512]{3,2,1,0:T(8,128)S(1)}, u32[]{:S(2)}, u32[]{:S(2)}) collective-permute-start(f32[8,2,8,512]{3,2,1,0:T(8,128)S(1)} %dynamic-slice_bitcast_fusion.3), channel_id=1, source_target_pairs={{0,8},{4,12},{8,0},{12,4},{16,24},{20,28},{24,16},{28,20},{1,9},{5... | collective-permute-start | bytes 786440 | tf_op jit(solution)/shard_map/ppermute | solution.py:145
  242.2 4.9 %collective-permute-done.9 = f32[8,2,8,512]{3,2,1,0:T(8,128)S(1)} collective-permute-done((f32[8,2,8,512]{3,2,1,0:T(8,128)S(1)}, f32[8,2,8,512]{3,2,1,0:T(8,128)S(1)}, u32[]{:S(2)}, u32[]{:S(2)}) %collective-permute-start.9) | collective-permute-done | bytes 262176 | tf_op jit(solution)/shard_map/ppermute | solution.py:145
  249.1 12.1 %shard_map.101.refs_6_ = f32[512,512]{1,0:T(8,128)S(1)} custom-call(s32[1]{0:T(128)} %bitcast.p_ref, bf16[8,512,512]{2,1,0:T(8,128)(2,1)} %copy-done.1, bf16[8,512,512]{2,1,0:T(8,128)(2,1)} %get-tuple-element.31.low_ref, f32[4,8,8,4,512]{4,3,2,1,0:T(4,128)S(1)} %collective-permute-done.12.refs_0_, f32[4,8,8,4,512]{4,3,2,1,0:T(4,128)} %collective-permute-done.11.refs_1_, ...), custom_call_target="tpu_custom_call" | custom-call | flops 6442450944 | bytes 18874368 | tf_op jit(solution)/shard_map/pallas_call | solution.py:124
  261.3 12.5 %shard_map.102 = f32[512,512]{1,0:T(8,128)S(1)} custom-call(s32[1]{0:T(128)} %bitcast.p_ref, bf16[8,512,512]{2,1,0:T(8,128)(2,1)} %copy-done, bf16[8,512,512]{2,1,0:T(8,128)(2,1)} %get-tuple-element.20.low_ref, f32[1,8,8,4,512]{4,3,2,1,0:T(4,128)S(1)} %slice.60.refs_0_, f32[4,8,8,4,512]{4,3,2,1,0:T(4,128)} %pad_maximum_fusion.refs_1_, ...), custom_call_target="tpu_custom_call" | custom-call | flops 6442450944 | bytes 18874368 | tf_op jit(solution)/shard_map/pallas_call | solution.py:124
  276.6 6.6 %collective-permute-done.10 = f32[8,8,512]{2,1,0:T(8,128)S(1)} collective-permute-done((f32[8,8,512]{2,1,0:T(8,128)S(1)}, f32[8,8,512]{2,1,0:T(8,128)S(1)}, u32[]{:S(2)}, u32[]{:S(2)}) %collective-permute-start.10) | collective-permute-done | bytes 131104 | tf_op jit(solution)/shard_map/ppermute | solution.py:145
  283.9 4.0 %collective-permute-done.21 = f32[8,2,2,8,512]{4,3,2,1,0:T(8,128)} collective-permute-done((f32[8,2,2,8,512]{4,3,2,1,0:T(8,128)}, f32[8,2,2,8,512]{4,3,2,1,0:T(8,128)}, u32[]{:S(2)}, u32[]{:S(2)}) %collective-permute-start.21) | collective-permute-done | bytes 524320 | tf_op jit(solution)/shard_map/ppermute | solution.py:145
  300.6 3.4 %collective-permute-done.23 = f32[8,8,512]{2,1,0:T(8,128)S(1)} collective-permute-done((f32[8,8,512]{2,1,0:T(8,128)S(1)}, f32[8,8,512]{2,1,0:T(8,128)S(1)}, u32[]{:S(2)}, u32[]{:S(2)}) %collective-permute-start.23) | collective-permute-done | bytes 131104 | tf_op jit(solution)/shard_map/ppermute | solution.py:145
  328.9 3.1 collective-permute-done.28
  (109 shorter events, 76.7 us)
Async XLA Ops:
  4.5 26.2 %collective-permute-start = (f32[2,8,8,4,512]{4,3,2,1,0:T(4,128)S(1)}, f32[2,8,8,4,512]{4,3,2,1,0:T(4,128)S(1)}, u32[]{:S(2)}, u32[]{:S(2)}) collective-permute-start(f32[2,8,8,4,512]{4,3,2,1,0:T(4,128)S(1)} %get-tuple-element.22), channel_id=1, source_target_pairs={{0,4},{4,0},{8,12},{12,8},{16,20},{20,16},{24,28},{28,24},{1,5},{5... | collective-permute-start | bytes 3145736 | tf_op jit(solution)/shard_map/ppermute | solution.py:145
  7.5 113.2 %collective-permute-start.7 = (f32[1,8,64,4,512]{4,3,2,1,0:T(4,128)S(1)}, f32[1,8,64,4,512]{4,3,2,1,0:T(4,128)}, u32[]{:S(2)}, u32[]{:S(2)}) collective-permute-start(f32[1,8,64,4,512]{4,3,2,1,0:T(4,128)S(1)} %bitcast.66), channel_id=1, source_target_pairs={{0,1},{1,0},{2,3},{3,2},{4,5},{5,4},{6,7},{7,6},{8,9},{9,8},{10,11... | collective-permute-start | bytes 12582920 | tf_op jit(solution)/shard_map/ppermute | solution.py:145
  31.9 70.7 %collective-permute-start.1 = (f32[2,8,8,4,512]{4,3,2,1,0:T(4,128)S(1)}, f32[2,8,8,4,512]{4,3,2,1,0:T(4,128)S(1)}, u32[]{:S(2)}, u32[]{:S(2)}) collective-permute-start(f32[2,8,8,4,512]{4,3,2,1,0:T(4,128)S(1)} %pad_maximum_fusion.2), channel_id=1, source_target_pairs={{0,8},{4,12},{8,0},{12,4},{16,24},{20,28},{24,16},{28,20},{1,9},{5... | collective-permute-start | bytes 3145736 | tf_op jit(solution)/shard_map/ppermute | solution.py:145
  33.7 37.9 %collective-permute-start.2 = (f32[1,8,8,4,512]{4,3,2,1,0:T(4,128)S(1)}, f32[1,8,8,4,512]{4,3,2,1,0:T(4,128)S(1)}, u32[]{:S(2)}, u32[]{:S(2)}) collective-permute-start(f32[1,8,8,4,512]{4,3,2,1,0:T(4,128)S(1)} %get-tuple-element.25), channel_id=1, source_target_pairs={{0,24},{4,28},{8,16},{12,20},{16,8},{20,12},{24,0},{28,4},{1,25},{... | collective-permute-start | bytes 1572872 | tf_op jit(solution)/shard_map/ppermute | solution.py:145
  36.2 62.4 %collective-permute-start.4 = (f32[1,8,8,4,512]{4,3,2,1,0:T(4,128)S(1)}, f32[1,8,8,4,512]{4,3,2,1,0:T(4,128)S(1)}, u32[]{:S(2)}, u32[]{:S(2)}) collective-permute-start(f32[1,8,8,4,512]{4,3,2,1,0:T(4,128)S(1)} %get-tuple-element.27), channel_id=1, source_target_pairs={{0,20},{4,16},{8,28},{12,24},{16,4},{20,0},{24,12},{28,8},{1,21},{... | collective-permute-start | bytes 1572872 | tf_op jit(solution)/shard_map/ppermute | solution.py:145
  37.3 80.9 %collective-permute-start.12 = (f32[4,8,8,4,512]{4,3,2,1,0:T(4,128)S(1)}, f32[4,8,8,4,512]{4,3,2,1,0:T(4,128)S(1)}, u32[]{:S(2)}, u32[]{:S(2)}) collective-permute-start(f32[4,8,8,4,512]{4,3,2,1,0:T(4,128)S(1)} %get-tuple-element.33), channel_id=1, source_target_pairs={{0,2},{1,3},{2,0},{3,1},{4,6},{5,7},{6,4},{7,5},{8,10},{9,11},{10,... | collective-permute-start | bytes 6291464 | tf_op jit(solution)/shard_map/ppermute | solution.py:145
  71.6 42.9 %collective-permute-start.3 = (f32[1,8,8,4,512]{4,3,2,1,0:T(4,128)S(1)}, f32[1,8,8,4,512]{4,3,2,1,0:T(4,128)S(1)}, u32[]{:S(2)}, u32[]{:S(2)}) collective-permute-start(f32[1,8,8,4,512]{4,3,2,1,0:T(4,128)S(1)} %get-tuple-element.26), channel_id=1, source_target_pairs={{0,16},{4,20},{8,24},{12,28},{16,0},{20,4},{24,8},{28,12},{1,17},{... | collective-permute-start | bytes 1572872 | tf_op jit(solution)/shard_map/ppermute | solution.py:145
  98.6 18.5 %collective-permute-start.5 = (f32[1,8,8,4,512]{4,3,2,1,0:T(4,128)S(1)}, f32[1,8,8,4,512]{4,3,2,1,0:T(4,128)S(1)}, u32[]{:S(2)}, u32[]{:S(2)}) collective-permute-start(f32[1,8,8,4,512]{4,3,2,1,0:T(4,128)S(1)} %get-tuple-element.29), channel_id=1, source_target_pairs={{0,28},{4,24},{8,20},{12,16},{16,12},{20,8},{24,4},{28,0},{1,29},{... | collective-permute-start | bytes 1572872 | tf_op jit(solution)/shard_map/ppermute | solution.py:145
  118.0 88.7 %collective-permute-start.6 = (f32[8,8,8,4,512]{4,3,2,1,0:T(4,128)}, f32[8,8,8,4,512]{4,3,2,1,0:T(4,128)}, u32[]{:S(2)}, u32[]{:S(2)}) collective-permute-start(f32[8,8,8,4,512]{4,3,2,1,0:T(4,128)} %constant_dynamic-update-slice_fusion.refs_0_), channel_id=1, source_target_pairs={{0,1},{1,0},{2,3},{3,2},{4,5},{5,4},{6,7},{7,6},{8,9},{9,8},{10,11... | collective-permute-start | bytes 12582920 | tf_op jit(solution)/shard_map/ppermute | solution.py:145
  118.2 25.5 %collective-permute-start.13 = (f32[2,8,8,4,512]{4,3,2,1,0:T(4,128)S(1)}, f32[2,8,8,4,512]{4,3,2,1,0:T(4,128)S(1)}, u32[]{:S(2)}, u32[]{:S(2)}) collective-permute-start(f32[2,8,8,4,512]{4,3,2,1,0:T(4,128)S(1)} %slice.61), channel_id=1, source_target_pairs={{0,4},{4,0},{8,12},{12,8},{16,20},{20,16},{24,28},{28,24},{1,5},{5... | collective-permute-start | bytes 3145736 | tf_op jit(solution)/shard_map/ppermute | solution.py:145
  120.7 85.4 %collective-permute-start.11 = (f32[4,8,8,4,512]{4,3,2,1,0:T(4,128)}, f32[4,8,8,4,512]{4,3,2,1,0:T(4,128)}, u32[]{:S(2)}, u32[]{:S(2)}) collective-permute-start(f32[4,8,8,4,512]{4,3,2,1,0:T(4,128)} %get-tuple-element.32), channel_id=1, source_target_pairs={{0,2},{1,3},{2,0},{3,1},{4,6},{5,7},{6,4},{7,5},{8,10},{9,11},{10,... | collective-permute-start | bytes 6291464 | tf_op jit(solution)/shard_map/ppermute | solution.py:145
  145.8 44.7 %collective-permute-start.14 = (f32[2,8,8,4,512]{4,3,2,1,0:T(4,128)}, f32[2,8,8,4,512]{4,3,2,1,0:T(4,128)}, u32[]{:S(2)}, u32[]{:S(2)}) collective-permute-start(f32[2,8,8,4,512]{4,3,2,1,0:T(4,128)} %pad_maximum_fusion.3), channel_id=1, source_target_pairs={{0,8},{4,12},{8,0},{12,4},{16,24},{20,28},{24,16},{28,20},{1,9},{5... | collective-permute-start | bytes 3145736 | tf_op jit(solution)/shard_map/ppermute | solution.py:145
  156.0 33.8 %collective-permute-start.15 = (f32[1,8,8,4,512]{4,3,2,1,0:T(4,128)}, f32[1,8,8,4,512]{4,3,2,1,0:T(4,128)}, u32[]{:S(2)}, u32[]{:S(2)}) collective-permute-start(f32[1,8,8,4,512]{4,3,2,1,0:T(4,128)} %get-tuple-element.35), channel_id=1, source_target_pairs={{0,16},{4,20},{8,24},{12,28},{16,0},{20,4},{24,8},{28,12},{1,17},{... | collective-permute-start | bytes 1572872 | tf_op jit(solution)/shard_map/ppermute | solution.py:145
  178.2 42.5 %collective-permute-start.16 = (f32[3,8,8,4,512]{4,3,2,1,0:T(4,128)S(1)}, f32[3,8,8,4,512]{4,3,2,1,0:T(4,128)}, u32[]{:S(2)}, u32[]{:S(2)}) collective-permute-start(f32[3,8,8,4,512]{4,3,2,1,0:T(4,128)S(1)} %pad_maximum_fusion.1), channel_id=1, source_target_pairs={{0,2},{1,3},{2,0},{3,1},{4,6},{5,7},{6,4},{7,5},{8,10},{9,11},{10,... | collective-permute-start | bytes 4718600 | tf_op jit(solution)/shard_map/ppermute | solution.py:145
  189.8 59.3 %collective-permute-start.20 = (f32[4,8,8,4,512]{4,3,2,1,0:T(4,128)S(1)}, f32[4,8,8,4,512]{4,3,2,1,0:T(4,128)}, u32[]{:S(2)}, u32[]{:S(2)}) collective-permute-start(f32[4,8,8,4,512]{4,3,2,1,0:T(4,128)S(1)} %collective-permute-done.12.refs_0_), channel_id=1, source_target_pairs={{0,1},{1,0},{2,3},{3,2},{4,5},{5,4},{6,7},{7,6},{8,9},{9,8},{10,11... | collective-permute-start | bytes 6291464 | tf_op jit(solution)/shard_map/ppermute | solution.py:145
  194.1 67.1 %collective-permute-start.18 = (f32[4,8,8,4,512]{4,3,2,1,0:T(4,128)}, f32[4,8,8,4,512]{4,3,2,1,0:T(4,128)}, u32[]{:S(2)}, u32[]{:S(2)}) collective-permute-start(f32[4,8,8,4,512]{4,3,2,1,0:T(4,128)} %pad_maximum_fusion.refs_1_), channel_id=1, source_target_pairs={{0,1},{1,0},{2,3},{3,2},{4,5},{5,4},{6,7},{7,6},{8,9},{9,8},{10,11... | collective-permute-start | bytes 6291464 | tf_op jit(solution)/shard_map/ppermute | solution.py:145
  206.1 41.9 %collective-permute-start.17 = (f32[4,8,8,4,512]{4,3,2,1,0:T(4,128)}, f32[4,8,8,4,512]{4,3,2,1,0:T(4,128)}, u32[]{:S(2)}, u32[]{:S(2)}) collective-permute-start(f32[4,8,8,4,512]{4,3,2,1,0:T(4,128)} %collective-permute-done.11.refs_1_), channel_id=1, source_target_pairs={{0,1},{1,0},{2,3},{3,2},{4,5},{5,4},{6,7},{7,6},{8,9},{9,8},{10,11... | collective-permute-start | bytes 6291464 | tf_op jit(solution)/shard_map/ppermute | solution.py:145
  220.1 14.2 %collective-permute-start.8 = (f32[8,2,2,8,512]{4,3,2,1,0:T(8,128)}, f32[8,2,2,8,512]{4,3,2,1,0:T(8,128)}, u32[]{:S(2)}, u32[]{:S(2)}) collective-permute-start(f32[8,2,2,8,512]{4,3,2,1,0:T(8,128)} %dynamic-slice_bitcast_fusion.1), channel_id=1, source_target_pairs={{0,4},{4,0},{8,12},{12,8},{16,20},{20,16},{24,28},{28,24},{1,5},{5... | collective-permute-start | bytes 1572872 | tf_op jit(solution)/shard_map/ppermute | solution.py:145
  220.7 40.6 %collective-permute-start.19 = (f32[3,8,8,4,512]{4,3,2,1,0:T(4,128)}, f32[3,8,8,4,512]{4,3,2,1,0:T(4,128)}, u32[]{:S(2)}, u32[]{:S(2)}) collective-permute-start(f32[3,8,8,4,512]{4,3,2,1,0:T(4,128)} %collective-permute-done.16.refs_2_), channel_id=1, source_target_pairs={{0,1},{1,0},{2,3},{3,2},{4,5},{5,4},{6,7},{7,6},{8,9},{9,8},{10,11... | collective-permute-start | bytes 4718600 | tf_op jit(solution)/shard_map/ppermute | solution.py:145
  237.2 9.8 %collective-permute-start.9 = (f32[8,2,8,512]{3,2,1,0:T(8,128)S(1)}, f32[8,2,8,512]{3,2,1,0:T(8,128)S(1)}, u32[]{:S(2)}, u32[]{:S(2)}) collective-permute-start(f32[8,2,8,512]{3,2,1,0:T(8,128)S(1)} %dynamic-slice_bitcast_fusion.3), channel_id=1, source_target_pairs={{0,8},{4,12},{8,0},{12,4},{16,24},{20,28},{24,16},{28,20},{1,9},{5... | collective-permute-start | bytes 786440 | tf_op jit(solution)/shard_map/ppermute | solution.py:145
  274.6 13.3 %collective-permute-start.21 = (f32[8,2,2,8,512]{4,3,2,1,0:T(8,128)}, f32[8,2,2,8,512]{4,3,2,1,0:T(8,128)}, u32[]{:S(2)}, u32[]{:S(2)}) collective-permute-start(f32[8,2,2,8,512]{4,3,2,1,0:T(8,128)} %dynamic-slice_bitcast_fusion), channel_id=1, source_target_pairs={{0,4},{4,0},{8,12},{12,8},{16,20},{20,16},{24,28},{28,24},{1,5},{5... | collective-permute-start | bytes 1572872 | tf_op jit(solution)/shard_map/ppermute | solution.py:145
  275.1 8.0 %collective-permute-start.10 = (f32[8,8,512]{2,1,0:T(8,128)S(1)}, f32[8,8,512]{2,1,0:T(8,128)S(1)}, u32[]{:S(2)}, u32[]{:S(2)}) collective-permute-start(f32[8,8,512]{2,1,0:T(8,128)S(1)} %dynamic-slice_bitcast_fusion.5), channel_id=1, source_target_pairs={{0,16},{4,20},{8,24},{12,28},{16,0},{20,4},{24,8},{28,12},{1,17},{... | collective-permute-start | bytes 393224 | tf_op jit(solution)/shard_map/ppermute | solution.py:145
  289.1 6.6 %collective-permute-start.22 = (f32[8,2,8,512]{3,2,1,0:T(8,128)S(1)}, f32[8,2,8,512]{3,2,1,0:T(8,128)}, u32[]{:S(2)}, u32[]{:S(2)}) collective-permute-start(f32[8,2,8,512]{3,2,1,0:T(8,128)S(1)} %dynamic-slice_bitcast_fusion.2), channel_id=1, source_target_pairs={{0,8},{4,12},{8,0},{12,4},{16,24},{20,28},{24,16},{28,20},{1,9},{5... | collective-permute-start | bytes 786440 | tf_op jit(solution)/shard_map/ppermute | solution.py:145
  296.7 7.3 %collective-permute-start.23 = (f32[8,8,512]{2,1,0:T(8,128)S(1)}, f32[8,8,512]{2,1,0:T(8,128)S(1)}, u32[]{:S(2)}, u32[]{:S(2)}) collective-permute-start(f32[8,8,512]{2,1,0:T(8,128)S(1)} %dynamic-slice_bitcast_fusion.4), channel_id=1, source_target_pairs={{0,16},{4,20},{8,24},{12,28},{16,0},{20,4},{24,8},{28,12},{1,17},{... | collective-permute-start | bytes 393224 | tf_op jit(solution)/shard_map/ppermute | solution.py:145
  (15 other events, 194.4 us)

commit v2 on v1

v2 whole, which is shorter than its diff:
```python
import functools

import jax
import jax.numpy as jnp
from jax import lax
from jax.experimental import pallas as pl
from jax.experimental.pallas import tpu as pltpu
from jax.sharding import PartitionSpec as P

VMEM = 48 * 2**20
QUICK = pl.CostEstimate(flops=2**10, bytes_accessed=2**10, transcendentals=0)


def split(x):
    high = x.astype(jnp.bfloat16)
    return high, (x - high.astype(jnp.float32)).astype(jnp.bfloat16)


def split_kernel(in_ref, high_ref, low_ref):
    high_ref[...], low_ref[...] = split(jnp.swapaxes(in_ref[...], 0, 1))


def split_integrals(integrals):
    a, i, k, c = integrals.shape
    tile = 64
    half = jax.ShapeDtypeStruct((k, a * i, c), jnp.bfloat16)
    return pl.pallas_call(
        split_kernel,
        grid=(a * i // tile,),
        in_specs=[pl.BlockSpec((tile, k, c), lambda n: (n, 0, 0))],
        out_specs=[pl.BlockSpec((k, tile, c), lambda n: (0, n, 0))] * 2,
        out_shape=[half, half],
        compiler_params=pltpu.CompilerParams(vmem_limit_bytes=VMEM),
        cost_estimate=QUICK,
    )(integrals.reshape(a * i, k, c))


def take_kernel(count, where_ref, in_ref, out_ref, held, in_sem, out_sem):
    reads = [
        pltpu.make_async_copy(in_ref.at[:, where_ref[n]], held.at[n], in_sem.at[n])
        for n in range(count)
    ]
    writes = [
        pltpu.make_async_copy(held.at[n], out_ref.at[n], out_sem.at[n]) for n in range(count)
    ]
    for read in reads:
        read.start()
    for read, write in zip(reads, writes):
        read.wait()
        write.start()
    for write in writes:
        write.wait()


def take_blocks(array, where, count):
    k, q, j, b, c = array.shape
    blocks = jax.ShapeDtypeStruct((count, k, j, b, c), array.dtype)
    return pl.pallas_call(
        functools.partial(take_kernel, count),
        grid_spec=pltpu.PrefetchScalarGridSpec(
            num_scalar_prefetch=1,
            grid=(),
            in_specs=[pl.BlockSpec(memory_space=pl.ANY)],
            out_specs=pl.BlockSpec(memory_space=pl.ANY),
            scratch_shapes=[
                pltpu.VMEM(blocks.shape, array.dtype),
                pltpu.SemaphoreType.DMA((count,)),
                pltpu.SemaphoreType.DMA((count,)),
            ],
        ),
        out_shape=blocks,
        compiler_params=pltpu.CompilerParams(vmem_limit_bytes=VMEM),
        cost_estimate=QUICK,
    )(where, array)


def product_kernel(places, first, p_ref, high_ref, low_ref, *refs):
    n = len(places)
    out_ref, t_high, t_low = refs[-3:]
    for ref, (crossed, base, ds) in zip(refs, places):
        for at, d in enumerate(ds):
            x = ref[at, :, 0] if crossed else ref[at, 0]
            rows = x.shape[0] * x.shape[1]
            high, low = split(x.reshape(rows, x.shape[2]))
            start = base
            if d is not None:
                q = d(p_ref[0]) if callable(d) else p_ref[0] ^ d
                start = pl.multiple_of(base + q * rows, 16)
            t_high[pl.ds(start, rows), :] = high
            t_low[pl.ds(start, rows), :] = low

    @pl.when(pl.program_id(0) == 0)
    def _():
        out_ref[...] = jnp.zeros_like(out_ref) if first else refs[n][...]

    dot = functools.partial(
        lax.dot_general,
        dimension_numbers=(((1,), (1,)), ((), ())),
        preferred_element_type=jnp.float32,
    )
    out_ref[...] += (
        dot(high_ref[0], t_high[...])
        + dot(high_ref[0], t_low[...])
        + dot(low_ref[0], t_high[...])
    )


def product(halves, sources, start, p, columns):
    high, low = halves
    steps, m, c = high.shape
    specs = [pl.BlockSpec((1, m, c), lambda k, p: (k, 0, 0))] * 2
    operands = [high, low]
    places = []
    for stack, crossed, base, ds, part, skip in sources:
        b = stack.shape[3]
        n, h = part or (stack.shape[1 if crossed else 2], 0)
        if crossed:
            specs.append(pl.BlockSpec((len(ds), n, 1, b, c), lambda k, p, h=h, skip=skip: (skip, h, k, 0, 0)))
        else:
            specs.append(pl.BlockSpec((len(ds), 1, n, b, c), lambda k, p, h=h, skip=skip: (skip, k, h, 0, 0)))
        operands.append(stack)
        places.append((crossed, base, ds))
    if start is not None:
        specs.append(pl.BlockSpec((m, columns), lambda k, p: (0, start[1])))
        operands.append(start[0])
    return pl.pallas_call(
        functools.partial(product_kernel, places, start is None),
        grid_spec=pltpu.PrefetchScalarGridSpec(
            num_scalar_prefetch=1,
            grid=(steps,),
            in_specs=specs,
            out_specs=pl.BlockSpec((m, columns), lambda k, p: (0, 0)),
            scratch_shapes=[pltpu.VMEM((columns, c), jnp.bfloat16)] * 2,
        ),
        out_shape=jax.ShapeDtypeStruct((m, columns), jnp.float32),
        compiler_params=pltpu.CompilerParams(vmem_limit_bytes=VMEM),
        cost_estimate=QUICK,
    )(p, *operands)


def shift(value, axis, d):
    size = lax.axis_size(axis)
    return lax.ppermute(value, axis, [(i, i ^ d) for i in range(size)])


def after(value, *others):
    return lax.optimization_barrier((value,) + others)[0]


def scatter_sum(part, bits, holds):
    size, p = lax.axis_size("blk"), lax.axis_index("blk")
    a, i, n = part.shape
    top = size.bit_length() - 1
    part = part.reshape((a,) + (2,) * top + (i // size, n))
    left = list(range(top - 1, -1, -1))
    for at, bit in enumerate(bits):
        for hold in holds[: at + len(holds) - len(bits) + 1]:
            part = after(part, hold)
        axis = 1 + left.index(bit)
        mine = (p >> bit) & 1
        away = lax.dynamic_index_in_dim(part, 1 - mine, axis, keepdims=False)
        keep = lax.dynamic_index_in_dim(part, mine, axis, keepdims=False)
        part = keep + shift(away, "blk", 1 << bit)
        left.remove(bit)
    return part


def all_sum(copies):
    return jnp.sum(lax.all_to_all(copies, ("blk", "rep"), 0, 0, tiled=True)[:, 0, 0])


def parts_small(amplitudes, cycle_integrals, cross_integrals, p1):
    nb = lax.axis_size("blk")
    rows, o_count, b_count = amplitudes.shape[:3]
    mine = amplitudes.reshape((rows, nb, rows) + amplitudes.shape[2:])
    own = take_blocks(mine, jnp.arange(nb, dtype=jnp.int32), nb)
    whole = amplitudes[None]
    columns = 2 * o_count * b_count
    half = columns // 2

    def natural(stack):
        return stack.reshape((1, -1) + stack.shape[2:])

    row2 = shift(whole, "rep", 2)
    row1 = shift(whole, "rep", 1)
    col0 = lax.all_to_all(own, "blk", 0, 0, tiled=True)
    cyc = split_integrals(cycle_integrals)
    part0 = product(
        cyc,
        [(whole, False, 0, (None,), None, 0), (row1, False, half, (None,), None, 0)],
        None,
        p1,
        columns,
    )
    crs = split_integrals(after(cross_integrals, part0))

    col0, row2 = after(col0, crs[0]), after(row2, crs[0])
    late0 = take_blocks(
        col0.reshape((1, nb, rows * rows) + amplitudes.shape[2:]),
        p1 ^ jnp.array([5, 6, 7], jnp.int32),
        3,
    )
    late2 = shift(late0.reshape((3,) + col0.shape[1:]), "rep", 2)
    col1 = shift(col0, "rep", 1)
    row3 = shift(row2, "rep", 1)
    rows_in = after(row2, late0).reshape(mine.shape)
    near0 = take_blocks(rows_in, (p1 & 4) | jnp.arange(4, dtype=jnp.int32), 4)
    far0 = take_blocks(rows_in, p1 ^ 4, 1)
    groups = [[0, 1, 2, 3], [4, 5, 6, 7]]
    near2 = lax.all_to_all(near0, "blk", 0, 0, axis_index_groups=groups, tiled=True)
    far2 = shift(far0, "blk", 4)

    sources = [
        (natural(col0), True, 0, (None,), None, 0),
        (natural(col1), True, half, (None,), None, 0),
    ]
    part0 = product(crs, sources, (part0, 0), p1, columns)
    sources = [(row2, False, 0, (None,), None, 0), (row3, False, half, (None,), None, 0)]
    part1 = product(cyc, sources, None, after(p1, part0), columns)

    near3 = shift(after(near2, part1, late2), "rep", 1)
    far3 = shift(after(far2, part1), "rep", 1)
    late3 = shift(after(late2, far3), "rep", 1)
    places = tuple((lambda p, g=g: (p & 4) | g) for g in range(4))
    sources = []
    for base, near, far, late in ((0, near2, far2, late2), (half, near3, far3, late3)):
        sources.append((near, True, base, places, None, 0))
        sources.append((far, True, base, (4,), None, 0))
        sources.append((late, True, base, (5, 6, 7), None, 0))
    part1 = product(crs, sources, (part1, 0), p1, columns)
    return [((0, 1), part0, (late3, part1)), ((2, 3), part1, ())]


def parts_large(amplitudes, cycle_integrals, cross_integrals, p1):
    column = lax.all_to_all(amplitudes, "blk", split_axis=1, concat_axis=0, tiled=True)
    cyc, crs = split_integrals(cycle_integrals), split_integrals(cross_integrals)
    columns = amplitudes.shape[1] * amplitudes.shape[2]
    parts = []
    for e in range(lax.axis_size("rep")):
        row, col = amplitudes, column
        if e:
            row, col = shift(row, "rep", e), shift(col, "rep", e)
        part = product(cyc, [(row[None], False, 0, (None,), None, 0)], None, p1, columns)
        part = product(crs, [(col[None], True, 0, (None,), None, 0)], (part, 0), p1, columns)
        parts.append(((e,), part, ()))
    return parts


def per_device(
    amplitudes, cycle_integrals, cross_integrals, occ_energy, vir_energy_a, vir_energy_b
):
    nb, nr = lax.axis_size("blk"), lax.axis_size("rep")
    p, r = lax.axis_index("blk"), lax.axis_index("rep")
    rows, o_count, b_count, _ = amplitudes.shape
    a_count = cycle_integrals.shape[0]
    p1 = p.astype(jnp.int32).reshape(1)
    make = parts_small if (nb, nr, rows) == (8, 4, 8) else parts_large
    bits = tuple(range(nb.bit_length() - 1))
    squares = jnp.float32(0)
    residual = jnp.zeros((rows, a_count, nr * b_count, o_count), jnp.float32)
    found = []
    for es, part, holds in make(amplitudes, cycle_integrals, cross_integrals, p1):
        part = part.reshape(a_count, o_count, -1)
        half = part.shape[2] // 2
        part = [
            scatter_sum(part[:, :, :half], bits, holds),
            scatter_sum(part[:, :, half:], bits[1:] + bits[:1], holds),
        ]
        squares += jnp.sum(part[0] * part[0]) + jnp.sum(part[1] * part[1])
        found.append((es, part))
    copies = jnp.broadcast_to(squares, (nb * nr, 8, 128))
    es, part = found[-1]
    found[-1] = es, [after(piece, copies) for piece in part]
    for es, part in found:
        part = jnp.concatenate(part, axis=2)
        part = part.reshape(a_count, rows, len(es), o_count, b_count)
        for at, e in enumerate(es):
            residual = lax.dynamic_update_slice_in_dim(
                residual, jnp.transpose(part[:, :, at], (1, 0, 3, 2)), (r ^ e) * b_count, 2
            )
    occ_local = lax.dynamic_slice_in_dim(occ_energy, p * rows, rows, 0)
    vir_local = lax.dynamic_slice_in_dim(vir_energy_a, r * a_count, a_count, 0)
    denom = (
        occ_local[:, None, None, None]
        + occ_energy[None, None, None, :]
        - vir_local[None, :, None, None]
        - vir_energy_b[None, None, :, None]
    )
    update = residual / denom
    squares = all_sum(copies)
    total_count = (
        occ_energy.shape[0] * occ_energy.shape[0] * vir_energy_a.shape[0] * vir_energy_b.shape[0]
    )
    residual_rms = jnp.sqrt(squares / total_count)
    return (update, residual_rms)


def solution(mesh):
    return jax.shard_map(
        per_device,
        mesh=mesh,
        in_specs=(
            P("blk", None, "rep", None),
            P("rep", None, "blk", None),
            P("rep", None, "blk", None),
            P(),
            P(),
            P(),
        ),
        out_specs=(P("blk", "rep", None, None), P()),
        check_vma=False,
    )
```

time: 336 us -> 237 us (0.71)
  waiting for transfers between devices: 163 us -> 75.6 us
  local copies, waits for them, and re-layouts: 28.6 us -> 22.7 us
  other arithmetic: 14.2 us -> 9.43 us
    ppermute x29 -> x21, waiting for transfers between devices: 163 us -> 19 us  [shift(): return lax.ppermute(value, axis, [(i, i ^ d) for i in range(size)])]
    all_to_all x0 -> x3, waiting for transfers between devices: none -> 56.5 us  [the longest x1 55.9 us: parts_small(): col0 = lax.all_to_all(own, 'blk', 0, 0, tiled=True)]
    ppermute x29 -> x21, starting transfers between devices: 46.7 us -> 28.7 us  [shift(): return lax.ppermute(value, axis, [(i, i ^ d) for i in range(size)])]
    all_to_all x0 -> x3, starting transfers between devices: none -> 16.7 us  [the longest x1 7.25 us: parts_small(): col0 = lax.all_to_all(own, 'blk', 0, 0, tiled=True)]
    concatenate x4 -> x2, other arithmetic: 5.47 us -> 0.02 us  [per_device(): part = jnp.concatenate(part, axis=2)]
    slice x6 -> x2, local copies, waits for them, and re-layouts: 4.9 us -> 0.22 us  [per_device(): part[:, :, :half]]
    pallas_call x2 -> x4, Pallas kernels: 7.43 us -> 9.74 us  [take_blocks(): pl.pallas_call(functools.partial(take_kernel, count), grid_spec=pltpu.Pre...]
    unnamed x25 -> x28, local copies, waits for them, and re-layouts: 7.52 us -> 8.29 us
  transfers between devices with their start and end apart: 29 -> 24, of which waited for: 18 -> 11; matrix products, arithmetic and copies ran while one was open for 9% -> 9% of each run, Pallas kernels for 18% -> 31%
where the time goes in v2:
time: 237 us; the launch traced here: 235 us
  Pallas kernels  76.4 us (32%)
  waiting for transfers between devices  75.6 us (32%)
  starting transfers between devices  45.4 us (19%)
  local copies, waits for them, and re-layouts  22.7 us (10%)
  other arithmetic  9.43 us (4%)
  between operations  5.49 us (2%)
    all_to_all x1, waiting for transfers between devices, parts_small(): col0 = lax.all_to_all(own, 'blk', 0, 0, tiled=True)  55.9 us
    pallas_call x4, Pallas kernels, product(): pl.pallas_call(functools.partial(product_kernel, places, start is None),...  49.1 us
    ppermute x21, starting transfers between devices, shift(): return lax.ppermute(value, axis, [(i, i ^ d) for i in range(size)])  28.7 us
    ppermute x21, waiting for transfers between devices, shift(): return lax.ppermute(value, axis, [(i, i ^ d) for i in range(size)])  19 us
    pallas_call x2, Pallas kernels, split_integrals(): pl.pallas_call(split_kernel, grid=(a * i // tile,), in_specs=[pl.BlockSpe...  17.6 us
    pallas_call x4, Pallas kernels, take_blocks(): pl.pallas_call(functools.partial(take_kernel, count), grid_spec=pltpu.Pre...  9.74 us
    unnamed x28, local copies, waits for them, and re-layouts  8.29 us
    transpose x6, local copies, waits for them, and re-layouts, per_device(): jnp.transpose(part[:, :, at], (1, 0, 3, 2))  7.32 us
  transfers between devices with their start and end apart: 24, of which 11 were waited for; matrix products, arithmetic and copies ran while one was open for 9% of the time, Pallas kernels for 31%

profile of v2, /device:TPU:0, one launch (start us, length us, event | category | flops | bytes accessed | tf_op | source)
XLA Modules:
  0.0 234.9 jit_solution(1076221097945785762)
XLA Ops:
  0.6 2.9 %shard_map.89 = f32[8,8,8,4,512]{4,3,2,1,0:T(4,128)S(1)} custom-call(s32[8]{0:T(128)S(1)} %iota.6.where_ref, f32[8,8,8,4,512]{4,3,2,1,0:T(4,128)} %bitcast.89), custom_call_target="tpu_custom_call" | custom-call | flops 1024 | bytes 1024 | tf_op jit(solution)/shard_map/pallas_call | solution.py:58
  5.5 7.3 %all-to-all-start = ((f32[8,8,8,4,512]{4,3,2,1,0:T(4,128)}), f32[8,8,8,4,512]{4,3,2,1,0:T(4,128)}, u32[]{:S(2)}, u32[]{:S(2)}) async-start(f32[8,8,8,4,512]{4,3,2,1,0:T(4,128)} %copy-done.3), calls=%async_computation | async-start | bytes 8388608 | tf_op jit(solution)/shard_map/all_to_all | solution.py:186
  14.4 8.7 %shard_map.86 = (bf16[8,512,512]{2,1,0:T(8,128)(2,1)S(1)}, bf16[8,512,512]{2,1,0:T(8,128)(2,1)}) custom-call(f32[512,8,512]{2,1,0:T(8,128)} %bitcast.93), custom_call_target="tpu_custom_call" | custom-call | flops 1024 | bytes 1024 | tf_op jit(solution)/shard_map/pallas_call | solution.py:27
  25.2 2.2 copy-done.1
  27.3 11.9 %shard_map.87.refs_2_ = f32[512,512]{1,0:T(8,128)S(1)} custom-call(s32[1]{0:T(128)} %bitcast.p_ref, bf16[8,512,512]{2,1,0:T(8,128)(2,1)S(1)} %copy-done.1, bf16[8,512,512]{2,1,0:T(8,128)(2,1)} %get-tuple-element.23.low_ref, f32[1,8,64,4,512]{4,3,2,1,0:T(4,128)} %bitcast.92, f32[1,8,64,4,512]{4,3,2,1,0:T(4,128)} %collective-permute-done.refs_1_), custom_call_target="tpu_custom_call" | custom-call | flops 1024 | bytes 1024 | tf_op jit(solution)/shard_map/pallas_call | solution.py:126
  39.3 8.8 %shard_map.88 = (bf16[8,512,512]{2,1,0:T(8,128)(2,1)S(1)}, bf16[8,512,512]{2,1,0:T(8,128)(2,1)}) custom-call(f32[512,8,512]{2,1,0:T(8,128)} %bitcast.94), custom_call_target="tpu_custom_call" | custom-call | flops 1024 | bytes 1024 | tf_op jit(solution)/shard_map/pallas_call | solution.py:27
  50.2 55.9 %all-to-all-done = f32[8,8,8,4,512]{4,3,2,1,0:T(4,128)} async-done(((f32[8,8,8,4,512]{4,3,2,1,0:T(4,128)}), f32[8,8,8,4,512]{4,3,2,1,0:T(4,128)}, u32[]{:S(2)}, u32[]{:S(2)}) %all-to-all-start) | async-done | bytes 4194336 | tf_op jit(solution)/shard_map/all_to_all | solution.py:186
  106.6 2.8 %shard_map.91 = f32[3,1,64,4,512]{4,3,2,1,0:T(4,128)} custom-call(s32[3]{0:T(128)S(1)} %broadcast_xor_fusion.where_ref, f32[1,8,64,4,512]{4,3,2,1,0:T(4,128)} %bitcast.11.in_ref), custom_call_target="tpu_custom_call" | custom-call | flops 1024 | bytes 1024 | tf_op jit(solution)/shard_map/pallas_call | solution.py:58
  109.4 3.0 %shard_map.94 = f32[4,8,8,4,512]{4,3,2,1,0:T(4,128)} custom-call(s32[4]{0:T(128)S(1)} %iota_or_fusion.where_ref, f32[8,8,8,4,512]{4,3,2,1,0:T(4,128)} %bitcast.13.in_ref), custom_call_target="tpu_custom_call" | custom-call | flops 1024 | bytes 1024 | tf_op jit(solution)/shard_map/pallas_call | solution.py:58
  112.4 4.5 %all-to-all-start.1 = ((f32[4,8,8,4,512]{4,3,2,1,0:T(4,128)}), f32[4,8,8,4,512]{4,3,2,1,0:T(4,128)}, u32[]{:S(2)}, u32[]{:S(2)}) async-start(f32[4,8,8,4,512]{4,3,2,1,0:T(4,128)} %shard_map.94), calls=%async_computation.1 | async-start | bytes 4194304 | tf_op jit(solution)/shard_map/all_to_all | solution.py:210
  119.5 2.5 %collective-permute-start.5 = (f32[1,8,8,4,512]{4,3,2,1,0:T(4,128)S(1)}, f32[1,8,8,4,512]{4,3,2,1,0:T(4,128)S(1)}, u32[]{:S(2)}, u32[]{:S(2)}) collective-permute-start(f32[1,8,8,4,512]{4,3,2,1,0:T(4,128)S(1)} %shard_map.92), channel_id=1, source_target_pairs={{0,16},{4,20},{8,24},{12,28},{16,0},{20,4},{24,8},{28,12},{1,17},{... | collective-permute-start | bytes 1572872 | tf_op jit(solution)/shard_map/ppermute | solution.py:143
  122.1 12.9 %shard_map.90 = f32[512,512]{1,0:T(8,128)S(1)} custom-call(s32[1]{0:T(128)} %bitcast.p_ref, bf16[8,512,512]{2,1,0:T(8,128)(2,1)} %copy-done.4, bf16[8,512,512]{2,1,0:T(8,128)(2,1)} %get-tuple-element.26.low_ref, f32[1,64,8,4,512]{4,3,2,1,0:T(4,128)} %bitcast.5.refs_0_, f32[1,64,8,4,512]{4,3,2,1,0:T(4,128)} %bitcast.6.refs_1_, f32[512,512]{1,0:T(8,128)S(1)} %shard_map.87.refs_2_), custom_call_target="tpu_custom_call" | custom-call | flops 1024 | bytes 1024 | tf_op jit(solution)/shard_map/pallas_call | solution.py:126
  135.0 12.0 %shard_map.93.refs_6_ = f32[512,512]{1,0:T(8,128)S(1)} custom-call(s32[1]{0:T(128)} %bitcast.p_ref, bf16[8,512,512]{2,1,0:T(8,128)(2,1)S(1)} %copy-done.2, bf16[8,512,512]{2,1,0:T(8,128)(2,1)} %get-tuple-element.23.low_ref, f32[1,8,64,4,512]{4,3,2,1,0:T(4,128)} %collective-permute-done.4.refs_0_, f32[1,8,64,4,512]{4,3,2,1,0:T(4,128)} %collective-permute-done.6.refs_1_), custom_call_target="tpu_custom_call" | custom-call | flops 1024 | bytes 1024 | tf_op jit(solution)/shard_map/pallas_call | solution.py:126
  146.9 4.3 %collective-permute-done.5.refs_1_ = f32[1,8,8,4,512]{4,3,2,1,0:T(4,128)S(1)} collective-permute-done((f32[1,8,8,4,512]{4,3,2,1,0:T(4,128)S(1)}, f32[1,8,8,4,512]{4,3,2,1,0:T(4,128)S(1)}, u32[]{:S(2)}, u32[]{:S(2)}) %collective-permute-start.5) | collective-permute-done | bytes 524320 | tf_op jit(solution)/shard_map/ppermute | solution.py:143
  151.2 2.3 collective-permute-done.3.refs_2_
  154.7 4.2 %collective-permute-start.12 = (f32[8,2,2,8,256]{4,3,2,1,0:T(8,128)S(1)}, f32[8,2,2,8,256]{4,3,2,1,0:T(8,128)S(1)}, u32[]{:S(2)}, u32[]{:S(2)}) collective-permute-start(f32[8,2,2,8,256]{4,3,2,1,0:T(8,128)S(1)} %dynamic-slice_bitcast_fusion.2), channel_id=1, source_target_pairs={{0,8},{4,12},{8,0},{12,4},{16,24},{20,28},{24,16},{28,20},{1,9},{5... | collective-permute-start | bytes 786440 | tf_op jit(solution)/shard_map/ppermute | solution.py:143
  160.5 5.2 %collective-permute-done.12 = f32[8,2,2,8,256]{4,3,2,1,0:T(8,128)S(1)} collective-permute-done((f32[8,2,2,8,256]{4,3,2,1,0:T(8,128)S(1)}, f32[8,2,2,8,256]{4,3,2,1,0:T(8,128)S(1)}, u32[]{:S(2)}, u32[]{:S(2)}) %collective-permute-start.12) | collective-permute-done | bytes 262176 | tf_op jit(solution)/shard_map/ppermute | solution.py:143
  169.6 12.3 %shard_map.95 = f32[512,512]{1,0:T(8,128)S(1)} custom-call(s32[1]{0:T(128)} %bitcast.p_ref, bf16[8,512,512]{2,1,0:T(8,128)(2,1)} %copy-done.4, bf16[8,512,512]{2,1,0:T(8,128)(2,1)} %get-tuple-element.26.low_ref, f32[4,8,8,4,512]{4,3,2,1,0:T(4,128)} %all-to-all-done.1.refs_0_, f32[1,8,8,4,512]{4,3,2,1,0:T(4,128)S(1)} %collective-permute-done.5.refs_1_, ...), custom_call_target="tpu_custom_call" | custom-call | flops 1024 | bytes 1024 | tf_op jit(solution)/shard_map/pallas_call | solution.py:126
  186.0 3.0 %collective-permute-start.11 = (f32[8,8,256]{2,1,0:T(8,128)S(1)}, f32[8,8,256]{2,1,0:T(8,128)S(1)}, u32[]{:S(2)}, u32[]{:S(2)}) collective-permute-start(f32[8,8,256]{2,1,0:T(8,128)S(1)} %dynamic-slice_bitcast_fusion.11), channel_id=1, source_target_pairs={{0,16},{4,20},{8,24},{12,28},{16,0},{20,4},{24,8},{28,12},{1,17},{... | collective-permute-start | bytes 196616 | tf_op jit(solution)/shard_map/ppermute | solution.py:143
  188.9 3.1 %collective-permute-done.14 = f32[8,8,256]{2,1,0:T(8,128)S(1)} collective-permute-done((f32[8,8,256]{2,1,0:T(8,128)S(1)}, f32[8,8,256]{2,1,0:T(8,128)S(1)}, u32[]{:S(2)}, u32[]{:S(2)}) %collective-permute-start.14) | collective-permute-done | bytes 65568 | tf_op jit(solution)/shard_map/ppermute | solution.py:143
  202.4 2.7 %collective-permute-start.19 = (f32[8,2,8,256]{3,2,1,0:T(8,128)S(1)}, f32[8,2,8,256]{3,2,1,0:T(8,128)S(1)}, u32[]{:S(2)}, u32[]{:S(2)}) collective-permute-start(f32[8,2,8,256]{3,2,1,0:T(8,128)S(1)} %dynamic-slice_bitcast_fusion.4), channel_id=1, source_target_pairs={{0,16},{4,20},{8,24},{12,28},{16,0},{20,4},{24,8},{28,12},{1,17},{... | collective-permute-start | bytes 393224 | tf_op jit(solution)/shard_map/ppermute | solution.py:143
  208.4 2.9 %collective-permute-start.20 = (f32[8,8,256]{2,1,0:T(8,128)S(1)}, f32[8,8,256]{2,1,0:T(8,128)S(1)}, u32[]{:S(2)}, u32[]{:S(2)}) collective-permute-start(f32[8,8,256]{2,1,0:T(8,128)S(1)} %dynamic-slice_bitcast_fusion.8), channel_id=1, source_target_pairs={{0,4},{4,0},{8,12},{12,8},{16,20},{20,16},{24,28},{28,24},{1,5},{5... | collective-permute-start | bytes 196616 | tf_op jit(solution)/shard_map/ppermute | solution.py:143
  214.2 2.4 %collective-permute-done.17 = f32[8,8,256]{2,1,0:T(8,128)S(1)} collective-permute-done((f32[8,8,256]{2,1,0:T(8,128)S(1)}, f32[8,8,256]{2,1,0:T(8,128)S(1)}, u32[]{:S(2)}, u32[]{:S(2)}) %collective-permute-start.17) | collective-permute-done | bytes 65568 | tf_op jit(solution)/shard_map/ppermute | solution.py:143
  219.3 4.9 %all-to-all-start.2 = ((f32[32,8,128]{2,1,0:T(8,128)}), f32[32,8,128]{2,1,0:T(8,128)S(1)}, u32[]{:S(2)}, u32[]{:S(2)}) async-start(f32[32,8,128]{2,1,0:T(8,128)} %broadcast_in_dim.15), calls=%async_computation.2 | async-start | bytes 262144 | tf_op jit(solution)/shard_map/all_to_all | solution.py:169
  (113 shorter events, 46.8 us)
Async XLA Ops:
  5.5 100.5 %all-to-all-start = ((f32[8,8,8,4,512]{4,3,2,1,0:T(4,128)}), f32[8,8,8,4,512]{4,3,2,1,0:T(4,128)}, u32[]{:S(2)}, u32[]{:S(2)}) async-start(f32[8,8,8,4,512]{4,3,2,1,0:T(4,128)} %copy-done.3), calls=%async_computation | async-start | bytes 8388608 | tf_op jit(solution)/shard_map/all_to_all | solution.py:186
  12.8 12.4 %collective-permute-start = (f32[1,8,64,4,512]{4,3,2,1,0:T(4,128)}, f32[1,8,64,4,512]{4,3,2,1,0:T(4,128)}, u32[]{:S(2)}, u32[]{:S(2)}) collective-permute-start(f32[1,8,64,4,512]{4,3,2,1,0:T(4,128)} %bitcast.90), channel_id=1, source_target_pairs={{0,1},{1,0},{2,3},{3,2},{4,5},{5,4},{6,7},{7,6},{8,9},{9,8},{10,11... | collective-permute-start | bytes 12582920 | tf_op jit(solution)/shard_map/ppermute | solution.py:143
  12.8 93.3 %collective-permute-start.4 = (f32[1,8,64,4,512]{4,3,2,1,0:T(4,128)}, f32[1,8,64,4,512]{4,3,2,1,0:T(4,128)}, u32[]{:S(2)}, u32[]{:S(2)}) collective-permute-start(f32[1,8,64,4,512]{4,3,2,1,0:T(4,128)} %bitcast.91), channel_id=1, source_target_pairs={{0,2},{1,3},{2,0},{3,1},{4,6},{5,7},{6,4},{7,5},{8,10},{9,11},{10,... | collective-permute-start | bytes 12582920 | tf_op jit(solution)/shard_map/ppermute | solution.py:143
  106.1 16.0 %collective-permute-start.1 = (f32[8,8,8,4,512]{4,3,2,1,0:T(4,128)}, f32[8,8,8,4,512]{4,3,2,1,0:T(4,128)}, u32[]{:S(2)}, u32[]{:S(2)}) collective-permute-start(f32[8,8,8,4,512]{4,3,2,1,0:T(4,128)} %all-to-all-done), channel_id=1, source_target_pairs={{0,1},{1,0},{2,3},{3,2},{4,5},{5,4},{6,7},{7,6},{8,9},{9,8},{10,11... | collective-permute-start | bytes 12582920 | tf_op jit(solution)/shard_map/ppermute | solution.py:143
  106.1 28.8 %collective-permute-start.6 = (f32[1,8,64,4,512]{4,3,2,1,0:T(4,128)}, f32[1,8,64,4,512]{4,3,2,1,0:T(4,128)}, u32[]{:S(2)}, u32[]{:S(2)}) collective-permute-start(f32[1,8,64,4,512]{4,3,2,1,0:T(4,128)} %collective-permute-done.4.refs_0_), channel_id=1, source_target_pairs={{0,1},{1,0},{2,3},{3,2},{4,5},{5,4},{6,7},{7,6},{8,9},{9,8},{10,11... | collective-permute-start | bytes 12582920 | tf_op jit(solution)/shard_map/ppermute | solution.py:143
  112.4 41.4 %all-to-all-start.1 = ((f32[4,8,8,4,512]{4,3,2,1,0:T(4,128)}), f32[4,8,8,4,512]{4,3,2,1,0:T(4,128)}, u32[]{:S(2)}, u32[]{:S(2)}) async-start(f32[4,8,8,4,512]{4,3,2,1,0:T(4,128)} %shard_map.94), calls=%async_computation.1 | async-start | bytes 4194304 | tf_op jit(solution)/shard_map/all_to_all | solution.py:210
  116.9 36.7 %collective-permute-start.3 = (f32[3,8,8,4,512]{4,3,2,1,0:T(4,128)}, f32[3,8,8,4,512]{4,3,2,1,0:T(4,128)}, u32[]{:S(2)}, u32[]{:S(2)}) collective-permute-start(f32[3,8,8,4,512]{4,3,2,1,0:T(4,128)} %bitcast.12), channel_id=1, source_target_pairs={{0,2},{1,3},{2,0},{3,1},{4,6},{5,7},{6,4},{7,5},{8,10},{9,11},{10,... | collective-permute-start | bytes 4718600 | tf_op jit(solution)/shard_map/ppermute | solution.py:143
  119.5 31.7 %collective-permute-start.5 = (f32[1,8,8,4,512]{4,3,2,1,0:T(4,128)S(1)}, f32[1,8,8,4,512]{4,3,2,1,0:T(4,128)S(1)}, u32[]{:S(2)}, u32[]{:S(2)}) collective-permute-start(f32[1,8,8,4,512]{4,3,2,1,0:T(4,128)S(1)} %shard_map.92), channel_id=1, source_target_pairs={{0,16},{4,20},{8,24},{12,28},{16,0},{20,4},{24,8},{28,12},{1,17},{... | collective-permute-start | bytes 1572872 | tf_op jit(solution)/shard_map/ppermute | solution.py:143
  151.2 2.5 %collective-permute-start.7 = (f32[1,8,8,4,512]{4,3,2,1,0:T(4,128)S(1)}, f32[1,8,8,4,512]{4,3,2,1,0:T(4,128)S(1)}, u32[]{:S(2)}, u32[]{:S(2)}) collective-permute-start(f32[1,8,8,4,512]{4,3,2,1,0:T(4,128)S(1)} %collective-permute-done.5.refs_1_), channel_id=1, source_target_pairs={{0,1},{1,0},{2,3},{3,2},{4,5},{5,4},{6,7},{7,6},{8,9},{9,8},{10,11... | collective-permute-start | bytes 1572872 | tf_op jit(solution)/shard_map/ppermute | solution.py:143
  153.8 15.9 %collective-permute-start.10 = (f32[4,8,8,4,512]{4,3,2,1,0:T(4,128)}, f32[4,8,8,4,512]{4,3,2,1,0:T(4,128)}, u32[]{:S(2)}, u32[]{:S(2)}) collective-permute-start(f32[4,8,8,4,512]{4,3,2,1,0:T(4,128)} %all-to-all-done.1.refs_0_), channel_id=1, source_target_pairs={{0,1},{1,0},{2,3},{3,2},{4,5},{5,4},{6,7},{7,6},{8,9},{9,8},{10,11... | collective-permute-start | bytes 6291464 | tf_op jit(solution)/shard_map/ppermute | solution.py:143
  153.8 14.4 %collective-permute-start.8 = (f32[3,8,8,4,512]{4,3,2,1,0:T(4,128)}, f32[3,8,8,4,512]{4,3,2,1,0:T(4,128)}, u32[]{:S(2)}, u32[]{:S(2)}) collective-permute-start(f32[3,8,8,4,512]{4,3,2,1,0:T(4,128)} %collective-permute-done.3.refs_2_), channel_id=1, source_target_pairs={{0,1},{1,0},{2,3},{3,2},{4,5},{5,4},{6,7},{7,6},{8,9},{9,8},{10,11... | collective-permute-start | bytes 4718600 | tf_op jit(solution)/shard_map/ppermute | solution.py:143
  154.7 11.0 %collective-permute-start.12 = (f32[8,2,2,8,256]{4,3,2,1,0:T(8,128)S(1)}, f32[8,2,2,8,256]{4,3,2,1,0:T(8,128)S(1)}, u32[]{:S(2)}, u32[]{:S(2)}) collective-permute-start(f32[8,2,2,8,256]{4,3,2,1,0:T(8,128)S(1)} %dynamic-slice_bitcast_fusion.2), channel_id=1, source_target_pairs={{0,8},{4,12},{8,0},{12,4},{16,24},{20,28},{24,16},{28,20},{1,9},{5... | collective-permute-start | bytes 786440 | tf_op jit(solution)/shard_map/ppermute | solution.py:143
  158.9 8.4 %collective-permute-start.2 = (f32[8,2,2,8,256]{4,3,2,1,0:T(8,128)S(1)}, f32[8,2,2,8,256]{4,3,2,1,0:T(8,128)S(1)}, u32[]{:S(2)}, u32[]{:S(2)}) collective-permute-start(f32[8,2,2,8,256]{4,3,2,1,0:T(8,128)S(1)} %dynamic-slice_bitcast_fusion.3), channel_id=1, source_target_pairs={{0,4},{4,0},{8,12},{12,8},{16,20},{20,16},{24,28},{28,24},{1,5},{5... | collective-permute-start | bytes 786440 | tf_op jit(solution)/shard_map/ppermute | solution.py:143
  168.2 17.0 %collective-permute-start.13 = (f32[8,2,8,256]{3,2,1,0:T(8,128)S(1)}, f32[8,2,8,256]{3,2,1,0:T(8,128)S(1)}, u32[]{:S(2)}, u32[]{:S(2)}) collective-permute-start(f32[8,2,8,256]{3,2,1,0:T(8,128)S(1)} %dynamic-slice_bitcast_fusion.6), channel_id=1, source_target_pairs={{0,16},{4,20},{8,24},{12,28},{16,0},{20,4},{24,8},{28,12},{1,17},{... | collective-permute-start | bytes 393224 | tf_op jit(solution)/shard_map/ppermute | solution.py:143
  168.4 17.6 %collective-permute-start.9 = (f32[8,2,8,256]{3,2,1,0:T(8,128)S(1)}, f32[8,2,8,256]{3,2,1,0:T(8,128)S(1)}, u32[]{:S(2)}, u32[]{:S(2)}) collective-permute-start(f32[8,2,8,256]{3,2,1,0:T(8,128)S(1)} %dynamic-slice_bitcast_fusion.7), channel_id=1, source_target_pairs={{0,8},{4,12},{8,0},{12,4},{16,24},{20,28},{24,16},{28,20},{1,9},{5... | collective-permute-start | bytes 393224 | tf_op jit(solution)/shard_map/ppermute | solution.py:143
  182.9 18.5 %collective-permute-start.18 = (f32[8,2,2,8,256]{4,3,2,1,0:T(8,128)}, f32[8,2,2,8,256]{4,3,2,1,0:T(8,128)}, u32[]{:S(2)}, u32[]{:S(2)}) collective-permute-start(f32[8,2,2,8,256]{4,3,2,1,0:T(8,128)} %dynamic-slice_bitcast_fusion), channel_id=1, source_target_pairs={{0,8},{4,12},{8,0},{12,4},{16,24},{20,28},{24,16},{28,20},{1,9},{5... | collective-permute-start | bytes 786440 | tf_op jit(solution)/shard_map/ppermute | solution.py:143
  183.7 21.4 %collective-permute-start.15 = (f32[8,2,2,8,256]{4,3,2,1,0:T(8,128)S(1)}, f32[8,2,2,8,256]{4,3,2,1,0:T(8,128)}, u32[]{:S(2)}, u32[]{:S(2)}) collective-permute-start(f32[8,2,2,8,256]{4,3,2,1,0:T(8,128)S(1)} %dynamic-slice_bitcast_fusion.1), channel_id=1, source_target_pairs={{0,4},{4,0},{8,12},{12,8},{16,20},{20,16},{24,28},{28,24},{1,5},{5... | collective-permute-start | bytes 786440 | tf_op jit(solution)/shard_map/ppermute | solution.py:143
  185.3 6.8 %collective-permute-start.14 = (f32[8,8,256]{2,1,0:T(8,128)S(1)}, f32[8,8,256]{2,1,0:T(8,128)S(1)}, u32[]{:S(2)}, u32[]{:S(2)}) collective-permute-start(f32[8,8,256]{2,1,0:T(8,128)S(1)} %dynamic-slice_bitcast_fusion.10), channel_id=1, source_target_pairs={{0,4},{4,0},{8,12},{12,8},{16,20},{20,16},{24,28},{28,24},{1,5},{5... | collective-permute-start | bytes 196616 | tf_op jit(solution)/shard_map/ppermute | solution.py:143
  186.0 6.7 %collective-permute-start.11 = (f32[8,8,256]{2,1,0:T(8,128)S(1)}, f32[8,8,256]{2,1,0:T(8,128)S(1)}, u32[]{:S(2)}, u32[]{:S(2)}) collective-permute-start(f32[8,8,256]{2,1,0:T(8,128)S(1)} %dynamic-slice_bitcast_fusion.11), channel_id=1, source_target_pairs={{0,16},{4,20},{8,24},{12,28},{16,0},{20,4},{24,8},{28,12},{1,17},{... | collective-permute-start | bytes 196616 | tf_op jit(solution)/shard_map/ppermute | solution.py:143
  202.4 6.0 %collective-permute-start.19 = (f32[8,2,8,256]{3,2,1,0:T(8,128)S(1)}, f32[8,2,8,256]{3,2,1,0:T(8,128)S(1)}, u32[]{:S(2)}, u32[]{:S(2)}) collective-permute-start(f32[8,2,8,256]{3,2,1,0:T(8,128)S(1)} %dynamic-slice_bitcast_fusion.4), channel_id=1, source_target_pairs={{0,16},{4,20},{8,24},{12,28},{16,0},{20,4},{24,8},{28,12},{1,17},{... | collective-permute-start | bytes 393224 | tf_op jit(solution)/shard_map/ppermute | solution.py:143
  206.1 5.2 %collective-permute-start.16 = (f32[8,2,8,256]{3,2,1,0:T(8,128)S(1)}, f32[8,2,8,256]{3,2,1,0:T(8,128)S(1)}, u32[]{:S(2)}, u32[]{:S(2)}) collective-permute-start(f32[8,2,8,256]{3,2,1,0:T(8,128)S(1)} %dynamic-slice_bitcast_fusion.5), channel_id=1, source_target_pairs={{0,8},{4,12},{8,0},{12,4},{16,24},{20,28},{24,16},{28,20},{1,9},{5... | collective-permute-start | bytes 393224 | tf_op jit(solution)/shard_map/ppermute | solution.py:143
  208.4 5.1 %collective-permute-start.20 = (f32[8,8,256]{2,1,0:T(8,128)S(1)}, f32[8,8,256]{2,1,0:T(8,128)S(1)}, u32[]{:S(2)}, u32[]{:S(2)}) collective-permute-start(f32[8,8,256]{2,1,0:T(8,128)S(1)} %dynamic-slice_bitcast_fusion.8), channel_id=1, source_target_pairs={{0,4},{4,0},{8,12},{12,8},{16,20},{20,16},{24,28},{28,24},{1,5},{5... | collective-permute-start | bytes 196616 | tf_op jit(solution)/shard_map/ppermute | solution.py:143
  211.4 5.2 %collective-permute-start.17 = (f32[8,8,256]{2,1,0:T(8,128)S(1)}, f32[8,8,256]{2,1,0:T(8,128)S(1)}, u32[]{:S(2)}, u32[]{:S(2)}) collective-permute-start(f32[8,8,256]{2,1,0:T(8,128)S(1)} %dynamic-slice_bitcast_fusion.9), channel_id=1, source_target_pairs={{0,16},{4,20},{8,24},{12,28},{16,0},{20,4},{24,8},{28,12},{1,17},{... | collective-permute-start | bytes 196616 | tf_op jit(solution)/shard_map/ppermute | solution.py:143
  219.3 13.2 %all-to-all-start.2 = ((f32[32,8,128]{2,1,0:T(8,128)}), f32[32,8,128]{2,1,0:T(8,128)S(1)}, u32[]{:S(2)}, u32[]{:S(2)}) async-start(f32[32,8,128]{2,1,0:T(8,128)} %broadcast_in_dim.15), calls=%async_computation.2 | async-start | bytes 262144 | tf_op jit(solution)/shard_map/all_to_all | solution.py:169
  (14 other events, 173.8 us)

commit v3 on v2

v3 whole, which is shorter than its diff:
```python
import functools

import jax
import jax.numpy as jnp
from jax import lax
from jax.experimental import pallas as pl
from jax.experimental.pallas import tpu as pltpu
from jax.sharding import PartitionSpec as P

VMEM = 48 * 2**20
QUICK = pl.CostEstimate(flops=2**10, bytes_accessed=2**10, transcendentals=0)


def split(x):
    high = x.astype(jnp.bfloat16)
    return high, (x - high.astype(jnp.float32)).astype(jnp.bfloat16)


def split_kernel(in_ref, high_ref, low_ref):
    a = in_ref.shape[0]
    for i in range(in_ref.shape[1]):
        high, low = split(jnp.swapaxes(in_ref[:, i], 0, 1))
        high_ref[:, i * a : (i + 1) * a, :] = high
        low_ref[:, i * a : (i + 1) * a, :] = low


def split_integrals(integrals):
    a, i, k, c = integrals.shape
    tile = 8
    half = jax.ShapeDtypeStruct((k, i * a, c), jnp.bfloat16)
    return pl.pallas_call(
        split_kernel,
        grid=(i // tile,),
        in_specs=[pl.BlockSpec((a, tile, k, c), lambda n: (0, n, 0, 0))],
        out_specs=[pl.BlockSpec((k, tile * a, c), lambda n: (0, n, 0))] * 2,
        out_shape=[half, half],
        compiler_params=pltpu.CompilerParams(vmem_limit_bytes=VMEM),
        cost_estimate=QUICK,
    )(integrals)


def take_kernel(count, where_ref, in_ref, out_ref, held, in_sem, out_sem):
    reads = [
        pltpu.make_async_copy(in_ref.at[:, where_ref[n]], held.at[n], in_sem.at[n])
        for n in range(count)
    ]
    writes = [
        pltpu.make_async_copy(held.at[n], out_ref.at[n], out_sem.at[n]) for n in range(count)
    ]
    for read in reads:
        read.start()
    for read, write in zip(reads, writes):
        read.wait()
        write.start()
    for write in writes:
        write.wait()


def take_blocks(array, where, count):
    k, q, j, b, c = array.shape
    blocks = jax.ShapeDtypeStruct((count, k, j, b, c), array.dtype)
    return pl.pallas_call(
        functools.partial(take_kernel, count),
        grid_spec=pltpu.PrefetchScalarGridSpec(
            num_scalar_prefetch=1,
            grid=(),
            in_specs=[pl.BlockSpec(memory_space=pl.ANY)],
            out_specs=pl.BlockSpec(memory_space=pl.ANY),
            scratch_shapes=[
                pltpu.VMEM(blocks.shape, array.dtype),
                pltpu.SemaphoreType.DMA((count,)),
                pltpu.SemaphoreType.DMA((count,)),
            ],
        ),
        out_shape=blocks,
        compiler_params=pltpu.CompilerParams(vmem_limit_bytes=VMEM),
        cost_estimate=QUICK,
    )(where, array)


def product_kernel(places, first, width, p_ref, high_ref, low_ref, *refs):
    out_ref, *t_all = refs[len(places) + (not first) :]
    for ref, (crossed, base, ds) in zip(refs, places):
        for at, d in enumerate(ds):
            for k, t_ref in enumerate(t_all):
                x = ref[at, :, k] if crossed else ref[at, k]
                j, b, _ = x.shape
                q = 0 if d is None else p_ref[0] ^ d
                for n in range(b):
                    start = pl.multiple_of(base + n * width + q * j, 8)
                    t_ref[pl.ds(start, j), :] = x[:, n, :]

    @pl.when(pl.program_id(0) == 0)
    def _():
        out_ref[...] = jnp.zeros_like(out_ref) if first else refs[len(places)][...]

    dot = functools.partial(
        lax.dot_general,
        dimension_numbers=(((1,), (1,)), ((), ())),
        preferred_element_type=jnp.float32,
    )
    total = 0.0
    for k, t_ref in enumerate(t_all):
        t_high, t_low = split(t_ref[...])
        total += dot(high_ref[k], t_high) + dot(high_ref[k], t_low) + dot(low_ref[k], t_high)
    out_ref[...] += total


def product(halves, sources, start, p, width, columns):
    high, low = halves
    steps, m, c = high.shape
    ks = 2 if steps % 2 == 0 else 1
    specs = [pl.BlockSpec((ks, m, c), lambda k, p: (k, 0, 0))] * 2
    operands = [high, low]
    places = []
    for stack, crossed, base, ds, part, skip in sources:
        b = stack.shape[3]
        n, h = part or (stack.shape[1 if crossed else 2], 0)
        if crossed:
            specs.append(pl.BlockSpec((len(ds), n, ks, b, c), lambda k, p, h=h, skip=skip: (skip, h, k, 0, 0)))
        else:
            specs.append(pl.BlockSpec((len(ds), ks, n, b, c), lambda k, p, h=h, skip=skip: (skip, k, h, 0, 0)))
        operands.append(stack)
        places.append((crossed, base, ds))
    if start is not None:
        specs.append(pl.BlockSpec((m, columns), lambda k, p: (0, start[1])))
        operands.append(start[0])
    return pl.pallas_call(
        functools.partial(product_kernel, places, start is None, width),
        grid_spec=pltpu.PrefetchScalarGridSpec(
            num_scalar_prefetch=1,
            grid=(steps // ks,),
            in_specs=specs,
            out_specs=pl.BlockSpec((m, columns), lambda k, p: (0, 0)),
            scratch_shapes=[pltpu.VMEM((columns, c), jnp.float32)] * ks,
        ),
        out_shape=jax.ShapeDtypeStruct((m, columns), jnp.float32),
        compiler_params=pltpu.CompilerParams(vmem_limit_bytes=VMEM),
        cost_estimate=QUICK,
    )(p, *operands)


def shift(value, axis, d):
    size = lax.axis_size(axis)
    return lax.ppermute(value, axis, [(i, i ^ d) for i in range(size)])


def after(value, *others):
    return lax.optimization_barrier((value,) + others)[0]


def scatter_step(part, left, bit, hold=None):
    mine = (lax.axis_index("blk") >> bit) & 1
    axis = left.index(bit)
    away = lax.dynamic_index_in_dim(part, 1 - mine, axis, keepdims=False)
    keep = lax.dynamic_index_in_dim(part, mine, axis, keepdims=False)
    away = shift(away, "blk", 1 << bit)
    if hold is not None:
        away = after(away, hold)
    return keep + away, [other for other in left if other != bit]


def scatter_halves(part, pieces=2):
    size = lax.axis_size("blk")
    bits = tuple(range(size.bit_length() - 1))
    half = part.shape[1] // pieces
    left = list(reversed(bits))
    return [
        (part[:, at : at + half].reshape((2,) * len(bits) + (-1, half)), left, order)
        for at, order in ((0, bits), (half, bits[1:] + bits[:1]))[:pieces]
    ]


def scatter_rest(halves, holds=()):
    for step in range(len(halves[0][2])):
        hold = holds[step] if step < len(holds) else None
        halves = [
            scatter_step(part, left, order[0], hold) + (order[1:],)
            for part, left, order in halves
        ]
    return [part for part, _, _ in halves]


def all_sum(copies):
    return jnp.sum(lax.all_to_all(copies, ("blk", "rep"), 0, 0, tiled=True))


def parts_small(amplitudes, cycle_integrals, cross_integrals, p1):
    nb = lax.axis_size("blk")
    rows, o_count, b_count = amplitudes.shape[:3]
    mine = amplitudes.reshape((rows, nb, rows) + amplitudes.shape[2:])
    own = take_blocks(mine, jnp.arange(nb, dtype=jnp.int32), nb)
    whole = amplitudes[None]
    columns = 2 * o_count * b_count
    half = columns // 2

    def natural(stack):
        return stack.reshape((1, -1) + stack.shape[2:])

    row2 = shift(whole, "rep", 2)
    row1 = shift(whole, "rep", 1)
    col0 = lax.all_to_all(own, "blk", 0, 0, tiled=True)
    cyc = split_integrals(cycle_integrals)
    part0 = product(
        cyc,
        [(whole, False, 0, (None,), None, 0), (row1, False, half, (None,), None, 0)],
        None,
        p1,
        o_count,
        columns,
    )
    crs = split_integrals(after(cross_integrals, part0))

    row2 = after(row2, crs[0])
    row3 = shift(row2, "rep", 1)
    rows_in = row2.reshape(mine.shape)
    near = [take_blocks(rows_in, p1 ^ d, 1) for d in (0, 1, 2, 3, 4)]
    near[1] = shift(near[1], "blk", 1)
    col0 = after(col0, row3, *near)
    late0 = take_blocks(
        col0.reshape((1, nb, rows * rows) + amplitudes.shape[2:]),
        p1 ^ jnp.array([5, 6, 7], jnp.int32),
        3,
    )
    late2 = shift(late0.reshape((3,) + col0.shape[1:]), "rep", 2)
    col1 = shift(col0, "rep", 1)
    near[2] = shift(after(near[2], late0), "blk", 2)
    near[3] = shift(after(near[3], late0), "blk", 3)
    far2 = shift(after(near[4], late0), "blk", 4)

    sources = [(row2, False, 0, (None,), None, 0), (row3, False, half, (None,), None, 0)]
    part1 = product(cyc, sources, None, after(p1, late0), o_count, columns)
    sources = [
        (natural(col0), True, 0, (None,), None, 0),
        (natural(col1), True, half, (None,), None, 0),
    ]
    part0 = product(crs, sources, (part0, 0), after(p1, part1), o_count, columns)
    sums0 = scatter_halves(part0, 1)
    sums0 = [
        scatter_step(part, left, order[0]) + (order[1:],) for part, left, order in sums0
    ]

    begun = [part for part, _, _ in sums0]
    far3 = shift(after(far2, part0), "rep", 1)
    late3 = shift(after(late2, far3, *begun), "rep", 1)
    early2 = jnp.concatenate(near[:2] + [after(near[2], part0), after(near[3], part0)])
    early3 = shift(early2, "rep", 1)
    sources = []
    for base, early, far, late in ((0, early2, far2, late2), (half, early3, far3, late3)):
        sources.append((early, True, base, (0, 1, 2, 3), None, 0))
        sources.append((far, True, base, (4,), None, 0))
        sources.append((late, True, base, (5, 6, 7), None, 0))
    ready = after(p1, *begun)
    part1 = product(crs, sources, (part1, 0), ready, o_count, columns)
    done = scatter_rest(sums0, (part1,))
    return [((0, 1), done), ((2, 3), scatter_rest(scatter_halves(part1)))]


def parts_large(amplitudes, cycle_integrals, cross_integrals, p1):
    column = lax.all_to_all(amplitudes, "blk", split_axis=1, concat_axis=0, tiled=True)
    cyc, crs = split_integrals(cycle_integrals), split_integrals(cross_integrals)
    o_count = amplitudes.shape[1]
    columns = o_count * amplitudes.shape[2]
    parts = []
    for e in range(lax.axis_size("rep")):
        row, col = amplitudes, column
        if e:
            row, col = shift(row, "rep", e), shift(col, "rep", e)
        part = product(cyc, [(row[None], False, 0, (None,), None, 0)], None, p1, o_count, columns)
        part = product(crs, [(col[None], True, 0, (None,), None, 0)], (part, 0), p1, o_count, columns)
        parts.append(((e,), scatter_rest(scatter_halves(part))))
    return parts


def per_device(
    amplitudes, cycle_integrals, cross_integrals, occ_energy, vir_energy_a, vir_energy_b
):
    nb, nr = lax.axis_size("blk"), lax.axis_size("rep")
    p, r = lax.axis_index("blk"), lax.axis_index("rep")
    rows, o_count, b_count, _ = amplitudes.shape
    a_count = cycle_integrals.shape[0]
    p1 = p.astype(jnp.int32).reshape(1)
    make = parts_small if (nb, nr, rows) == (8, 4, 8) else parts_large
    residual = jnp.zeros((rows, a_count, nr * b_count, o_count), jnp.float32)
    found = make(amplitudes, cycle_integrals, cross_integrals, p1)
    squares = sum(
        jnp.sum((part * part).reshape(-1, o_count), axis=0) for _, parts in found for part in parts
    )
    copies = jnp.broadcast_to(squares, (nb * nr,) + squares.shape)
    es, parts = found[-1]
    found[-1] = es, [after(part, copies) for part in parts]
    for es, parts in found:
        part = jnp.concatenate(parts, axis=1) if len(parts) > 1 else parts[0]
        part = part.reshape(rows, a_count, len(es), b_count, o_count)
        for at, e in enumerate(es):
            residual = lax.dynamic_update_slice_in_dim(
                residual, part[:, :, at], (r ^ e) * b_count, 2
            )
    occ_local = lax.dynamic_slice_in_dim(occ_energy, p * rows, rows, 0)
    vir_local = lax.dynamic_slice_in_dim(vir_energy_a, r * a_count, a_count, 0)
    denom = (
        occ_local[:, None, None, None]
        + occ_energy[None, None, None, :]
        - vir_local[None, :, None, None]
        - vir_energy_b[None, None, :, None]
    )
    update = residual / denom
    squares = all_sum(copies)
    total_count = (
        occ_energy.shape[0] * occ_energy.shape[0] * vir_energy_a.shape[0] * vir_energy_b.shape[0]
    )
    residual_rms = jnp.sqrt(squares / total_count)
    return (update, residual_rms)


def solution(mesh):
    return jax.shard_map(
        per_device,
        mesh=mesh,
        in_specs=(
            P("blk", None, "rep", None),
            P("rep", None, "blk", None),
            P("rep", None, "blk", None),
            P(),
            P(),
            P(),
        ),
        out_specs=(P("blk", "rep", None, None), P()),
        check_vma=False,
    )
```

time: 237 us -> 221 us (0.932)
  starting transfers between devices: 45.4 us -> 33.2 us
  local copies, waits for them, and re-layouts: 22.7 us -> 13 us
  waiting for transfers between devices: 75.6 us -> 83.9 us
  Pallas kernels: 76.4 us -> 79.8 us
  other arithmetic: 9.43 us -> 6.82 us
  between operations: 5.49 us -> 2.91 us
    ppermute x21, waiting for transfers between devices: 19 us -> 77.8 us  [shift(): return lax.ppermute(value, axis, [(i, i ^ d) for i in range(size)])]
    all_to_all x1, waiting for transfers between devices: 55.9 us -> 0.01 us  [parts_small(): col0 = lax.all_to_all(own, 'blk', 0, 0, tiled=True)]
    transpose x6 -> x0, local copies, waits for them, and re-layouts: 7.32 us -> none  [per_device(): jnp.transpose(part[:, :, at], (1, 0, 3, 2))]
    all_to_all x2 -> x1, starting transfers between devices: 9.43 us -> 3.82 us  [all_sum(): return jnp.sum(lax.all_to_all(copies, ('blk', 'rep'), 0, 0, tiled=True))]
    all_to_all x2 -> x1, waiting for transfers between devices: 0.64 us -> 6.07 us  [all_sum(): return jnp.sum(lax.all_to_all(copies, ('blk', 'rep'), 0, 0, tiled=True))]
    ppermute x21, starting transfers between devices: 28.7 us -> 23.6 us  [shift(): return lax.ppermute(value, axis, [(i, i ^ d) for i in range(size)])]
    pallas_call x4 -> x7, Pallas kernels: 9.74 us -> 13.4 us  [take_blocks(): pl.pallas_call(functools.partial(take_kernel, count), grid_spec=pltpu.Pre...]
    concatenate x2, other arithmetic: 0.02 us -> 3.6 us  [the longest x1 3.59 us: parts_small(): jnp.concatenate(near[:2] + [after(near[2], part0), after(near[3], part0)])]
  transfers between devices with their start and end apart: 24 -> 23, of which waited for: 11 -> 11; matrix products, arithmetic and copies ran while one was open for 9% -> 3% of each run, Pallas kernels for 31% -> 36%
where the time goes in v3:
time: 221 us; the launch traced here: 220 us
  waiting for transfers between devices  83.9 us (38%)
  Pallas kernels  79.8 us (36%)
  starting transfers between devices  33.2 us (15%)
  local copies, waits for them, and re-layouts  13 us (6%)
  other arithmetic  6.82 us (3%)
  between operations  2.91 us (1%)
    ppermute x21, waiting for transfers between devices, shift(): return lax.ppermute(value, axis, [(i, i ^ d) for i in range(size)])  77.8 us
    pallas_call x4, Pallas kernels, product(): pl.pallas_call(functools.partial(product_kernel, places, start is None, w...  49 us
    ppermute x21, starting transfers between devices, shift(): return lax.ppermute(value, axis, [(i, i ^ d) for i in range(size)])  23.6 us
    pallas_call x2, Pallas kernels, split_integrals(): pl.pallas_call(split_kernel, grid=(i // tile,), in_specs=[pl.BlockSpec((a...  17.4 us
    pallas_call x7, Pallas kernels, take_blocks(): pl.pallas_call(functools.partial(take_kernel, count), grid_spec=pltpu.Pre...  13.4 us
    unnamed x22, local copies, waits for them, and re-layouts  11.2 us
    all_to_all x1, waiting for transfers between devices, all_sum(): return jnp.sum(lax.all_to_all(copies, ('blk', 'rep'), 0, 0, tiled=True))  6.07 us
    all_to_all x1, starting transfers between devices, parts_small(): col0 = lax.all_to_all(own, 'blk', 0, 0, tiled=True)  5.81 us
  transfers between devices with their start and end apart: 23, of which 11 were waited for; matrix products, arithmetic and copies ran while one was open for 3% of the time, Pallas kernels for 36%

profile of v3, /device:TPU:0, one launch (start us, length us, event | category | flops | bytes accessed | tf_op | source)
XLA Modules:
  0.0 219.7 jit_solution(2720021388911477023)
XLA Ops:
  1.1 2.6 %collective-permute-start = (f32[1,8,64,4,512]{4,3,2,1,0:T(4,128)}, f32[1,8,64,4,512]{4,3,2,1,0:T(4,128)}, u32[]{:S(2)}, u32[]{:S(2)}) collective-permute-start(f32[1,8,64,4,512]{4,3,2,1,0:T(4,128)} %bitcast.70), channel_id=1, source_target_pairs={{0,2},{1,3},{2,0},{3,1},{4,6},{5,7},{6,4},{7,5},{8,10},{9,11},{10,... | collective-permute-start | bytes 12582920 | tf_op jit(solution)/shard_map/ppermute | solution.py:145
  3.7 2.9 %shard_map.86 = f32[8,8,8,4,512]{4,3,2,1,0:T(4,128)S(1)} custom-call(s32[8]{0:T(128)S(1)} %iota.3.where_ref, f32[8,8,8,4,512]{4,3,2,1,0:T(4,128)} %bitcast.71), custom_call_target="tpu_custom_call" | custom-call | flops 1024 | bytes 1024 | tf_op jit(solution)/shard_map/pallas_call | solution.py:62
  8.6 5.8 %all-to-all-start = ((f32[8,8,8,4,512]{4,3,2,1,0:T(4,128)}), f32[8,8,8,4,512]{4,3,2,1,0:T(4,128)}, u32[]{:S(2)}, u32[]{:S(2)}) async-start(f32[8,8,8,4,512]{4,3,2,1,0:T(4,128)} %copy-done.3), calls=%async_computation | async-start | bytes 8388608 | tf_op jit(solution)/shard_map/all_to_all | solution.py:202
  14.4 8.7 %shard_map.87 = (bf16[8,512,512]{2,1,0:T(8,128)(2,1)S(1)}, bf16[8,512,512]{2,1,0:T(8,128)(2,1)}) custom-call(f32[8,64,8,512]{3,2,1,0:T(8,128)} %in_ref.1), custom_call_target="tpu_custom_call" | custom-call | flops 1024 | bytes 1024 | tf_op jit(solution)/shard_map/pallas_call | solution.py:31
  25.1 2.2 copy-done.1
  27.3 12.0 %shard_map.88.refs_2_ = f32[512,512]{1,0:T(8,128)S(1)} custom-call(s32[1]{0:T(128)} %bitcast.p_ref.where_ref, bf16[8,512,512]{2,1,0:T(8,128)(2,1)S(1)} %copy-done.1, bf16[8,512,512]{2,1,0:T(8,128)(2,1)} %get-tuple-element.23.low_ref, f32[1,8,64,4,512]{4,3,2,1,0:T(4,128)} %bitcast.72, f32[1,8,64,4,512]{4,3,2,1,0:T(4,128)} %collective-permute-done.1.refs_1_), custom_call_target="tpu_custom_call" | custom-call | flops 1024 | bytes 1024 | tf_op jit(solution)/shard_map/pallas_call | solution.py:128
  39.4 8.7 %shard_map.89 = (bf16[8,512,512]{2,1,0:T(8,128)(2,1)S(1)}, bf16[8,512,512]{2,1,0:T(8,128)(2,1)}) custom-call(f32[8,64,8,512]{3,2,1,0:T(8,128)} %in_ref.2), custom_call_target="tpu_custom_call" | custom-call | flops 1024 | bytes 1024 | tf_op jit(solution)/shard_map/pallas_call | solution.py:31
  50.1 45.1 %collective-permute-done.refs_0_ = f32[1,8,64,4,512]{4,3,2,1,0:T(4,128)} collective-permute-done((f32[1,8,64,4,512]{4,3,2,1,0:T(4,128)}, f32[1,8,64,4,512]{4,3,2,1,0:T(4,128)}, u32[]{:S(2)}, u32[]{:S(2)}) %collective-permute-start) | collective-permute-done | bytes 4194336 | tf_op jit(solution)/shard_map/ppermute | solution.py:145
  105.6 5.2 %collective-permute-done.3 = f32[1,8,8,4,512]{4,3,2,1,0:T(4,128)} collective-permute-done((f32[1,8,8,4,512]{4,3,2,1,0:T(4,128)S(1)}, f32[1,8,8,4,512]{4,3,2,1,0:T(4,128)}, u32[]{:S(2)}, u32[]{:S(2)}) %collective-permute-start.3) | collective-permute-done | bytes 524320 | tf_op jit(solution)/shard_map/ppermute | solution.py:145
  110.9 2.8 %shard_map.95 = f32[3,1,64,4,512]{4,3,2,1,0:T(4,128)} custom-call(s32[3]{0:T(128)S(1)} %broadcast_xor_fusion.where_ref, f32[1,8,64,4,512]{4,3,2,1,0:T(4,128)} %bitcast.4.in_ref), custom_call_target="tpu_custom_call" | custom-call | flops 1024 | bytes 1024 | tf_op jit(solution)/shard_map/pallas_call | solution.py:62
  115.5 2.5 %collective-permute-start.8 = (f32[1,8,8,4,512]{4,3,2,1,0:T(4,128)}, f32[1,8,8,4,512]{4,3,2,1,0:T(4,128)}, u32[]{:S(2)}, u32[]{:S(2)}) collective-permute-start(f32[1,8,8,4,512]{4,3,2,1,0:T(4,128)} %shard_map.93), channel_id=1, source_target_pairs={{0,12},{4,8},{8,4},{12,0},{16,28},{20,24},{24,20},{28,16},{1,13},{... | collective-permute-start | bytes 1572872 | tf_op jit(solution)/shard_map/ppermute | solution.py:145
  118.4 2.6 %collective-permute-start.9 = (f32[1,8,8,4,512]{4,3,2,1,0:T(4,128)}, f32[1,8,8,4,512]{4,3,2,1,0:T(4,128)}, u32[]{:S(2)}, u32[]{:S(2)}) collective-permute-start(f32[1,8,8,4,512]{4,3,2,1,0:T(4,128)} %shard_map.94), channel_id=1, source_target_pairs={{0,16},{4,20},{8,24},{12,28},{16,0},{20,4},{24,8},{28,12},{1,17},{... | collective-permute-start | bytes 1572872 | tf_op jit(solution)/shard_map/ppermute | solution.py:145
  123.2 12.0 %shard_map.96.refs_6_ = f32[512,512]{1,0:T(8,128)S(1)} custom-call(s32[1]{0:T(128)} %bitcast.p_ref.where_ref, bf16[8,512,512]{2,1,0:T(8,128)(2,1)S(1)} %copy-done.2, bf16[8,512,512]{2,1,0:T(8,128)(2,1)} %get-tuple-element.23.low_ref, f32[1,8,64,4,512]{4,3,2,1,0:T(4,128)} %collective-permute-done.refs_0_, f32[1,8,64,4,512]{4,3,2,1,0:T(4,128)} %collective-permute-done.2.refs_1_), custom_call_target="tpu_custom_call" | custom-call | flops 1024 | bytes 1024 | tf_op jit(solution)/shard_map/pallas_call | solution.py:128
  135.3 12.5 %shard_map.97 = f32[512,512]{1,0:T(8,128)S(1)} custom-call(s32[1]{0:T(128)} %bitcast.p_ref.where_ref, bf16[8,512,512]{2,1,0:T(8,128)(2,1)} %copy-done.4, bf16[8,512,512]{2,1,0:T(8,128)(2,1)} %get-tuple-element.30.low_ref, f32[1,64,8,4,512]{4,3,2,1,0:T(4,128)} %bitcast.5.refs_0_, f32[1,64,8,4,512]{4,3,2,1,0:T(4,128)} %bitcast.6.refs_1_, ...), custom_call_target="tpu_custom_call" | custom-call | flops 1024 | bytes 1024 | tf_op jit(solution)/shard_map/pallas_call | solution.py:128
  148.5 4.8 %collective-permute-done.7 = f32[1,8,8,4,512]{4,3,2,1,0:T(4,128)} collective-permute-done((f32[1,8,8,4,512]{4,3,2,1,0:T(4,128)}, f32[1,8,8,4,512]{4,3,2,1,0:T(4,128)}, u32[]{:S(2)}, u32[]{:S(2)}) %collective-permute-start.7) | collective-permute-done | bytes 524320 | tf_op jit(solution)/shard_map/ppermute | solution.py:145
  153.2 3.6 %pad_maximum_fusion.refs_0_ = f32[4,8,8,4,512]{4,3,2,1,0:T(4,128)} fusion(f32[1,8,8,4,512]{4,3,2,1,0:T(4,128)} %collective-permute-done.8, f32[1,8,8,4,512]{4,3,2,1,0:T(4,128)} %collective-permute-done.7, f32[1,8,8,4,512]{4,3,2,1,0:T(4,128)} %collective-permute-done.3, f32[1,8,8,4,512]{4,3,2,1,0:T(4,128)S(1)} %copy-done.6), kind=kLoop, calls=%fused_computation | loop fusion | flops 1572864 | bytes 4194304 | tf_op jit(solution)/shard_map/concatenate | solution.py:246
  157.3 3.9 %collective-permute-done.5 = f32[2,2,64,512]{3,2,1,0:T(8,128)} collective-permute-done((f32[2,2,64,512]{3,2,1,0:T(8,128)S(1)}, f32[2,2,64,512]{3,2,1,0:T(8,128)}, u32[]{:S(2)}, u32[]{:S(2)}) %collective-permute-start.5) | collective-permute-done | bytes 524320 | tf_op jit(solution)/shard_map/ppermute | solution.py:145
  166.2 12.4 %shard_map.98 = f32[512,512]{1,0:T(8,128)S(1)} custom-call(s32[1]{0:T(128)} %bitcast.p_ref.where_ref, bf16[8,512,512]{2,1,0:T(8,128)(2,1)} %copy-done.4, bf16[8,512,512]{2,1,0:T(8,128)(2,1)} %get-tuple-element.30.low_ref, f32[4,8,8,4,512]{4,3,2,1,0:T(4,128)} %pad_maximum_fusion.refs_0_, f32[1,8,8,4,512]{4,3,2,1,0:T(4,128)} %collective-permute-done.9.refs_1_, ...), custom_call_target="tpu_custom_call" | custom-call | flops 1024 | bytes 1024 | tf_op jit(solution)/shard_map/pallas_call | solution.py:128
  181.5 6.8 %collective-permute-done.14 = f32[64,512]{1,0:T(8,128)S(1)} collective-permute-done((f32[64,512]{1,0:T(8,128)S(1)}, f32[64,512]{1,0:T(8,128)S(1)}, u32[]{:S(2)}, u32[]{:S(2)}) %collective-permute-start.14) | collective-permute-done | bytes 131104 | tf_op jit(solution)/shard_map/ppermute | solution.py:145
  190.2 2.4 %collective-permute-start.19 = (f32[2,64,256]{2,1,0:T(8,128)S(1)}, f32[2,64,256]{2,1,0:T(8,128)S(1)}, u32[]{:S(2)}, u32[]{:S(2)}) collective-permute-start(f32[2,64,256]{2,1,0:T(8,128)S(1)} %dynamic-slice_bitcast_fusion.4), channel_id=1, source_target_pairs={{0,16},{4,20},{8,24},{12,28},{16,0},{20,4},{24,8},{28,12},{1,17},{... | collective-permute-start | bytes 393224 | tf_op jit(solution)/shard_map/ppermute | solution.py:145
  194.4 4.3 %collective-permute-done.19 = f32[2,64,256]{2,1,0:T(8,128)S(1)} collective-permute-done((f32[2,64,256]{2,1,0:T(8,128)S(1)}, f32[2,64,256]{2,1,0:T(8,128)S(1)}, u32[]{:S(2)}, u32[]{:S(2)}) %collective-permute-start.19) | collective-permute-done | bytes 131104 | tf_op jit(solution)/shard_map/ppermute | solution.py:145
  200.5 2.6 %collective-permute-done.20 = f32[64,256]{1,0:T(8,128)S(1)} collective-permute-done((f32[64,256]{1,0:T(8,128)S(1)}, f32[64,256]{1,0:T(8,128)S(1)}, u32[]{:S(2)}, u32[]{:S(2)}) %collective-permute-start.20) | collective-permute-done | bytes 65568 | tf_op jit(solution)/shard_map/ppermute | solution.py:145
  206.3 3.8 %all-to-all-start.1 = ((f32[32,1,64]{2,1,0:T(1,128)}), f32[32,1,64]{2,1,0:T(1,128)S(1)}, u32[]{:S(2)}, u32[]{:S(2)}) async-start(f32[32,1,64]{2,1,0:T(1,128)} %broadcast_in_dim.18), calls=%async_computation.1 | async-start | bytes 32768 | tf_op jit(solution)/shard_map/all_to_all | solution.py:185
  211.2 6.1 %all-to-all-done.1 = f32[32,1,64]{2,1,0:T(1,128)S(1)} async-done(((f32[32,1,64]{2,1,0:T(1,128)}), f32[32,1,64]{2,1,0:T(1,128)S(1)}, u32[]{:S(2)}, u32[]{:S(2)}) %all-to-all-start.1) | async-done | bytes 8224 | tf_op jit(solution)/shard_map/all_to_all | solution.py:185
  (101 shorter events, 40.5 us)
Async XLA Ops:
  0.6 24.5 %collective-permute-start.1 = (f32[1,8,64,4,512]{4,3,2,1,0:T(4,128)}, f32[1,8,64,4,512]{4,3,2,1,0:T(4,128)}, u32[]{:S(2)}, u32[]{:S(2)}) collective-permute-start(f32[1,8,64,4,512]{4,3,2,1,0:T(4,128)} %bitcast.69), channel_id=1, source_target_pairs={{0,1},{1,0},{2,3},{3,2},{4,5},{5,4},{6,7},{7,6},{8,9},{9,8},{10,11... | collective-permute-start | bytes 12582920 | tf_op jit(solution)/shard_map/ppermute | solution.py:145
  1.1 94.1 %collective-permute-start = (f32[1,8,64,4,512]{4,3,2,1,0:T(4,128)}, f32[1,8,64,4,512]{4,3,2,1,0:T(4,128)}, u32[]{:S(2)}, u32[]{:S(2)}) collective-permute-start(f32[1,8,64,4,512]{4,3,2,1,0:T(4,128)} %bitcast.70), channel_id=1, source_target_pairs={{0,2},{1,3},{2,0},{3,1},{4,6},{5,7},{6,4},{7,5},{8,10},{9,11},{10,... | collective-permute-start | bytes 12582920 | tf_op jit(solution)/shard_map/ppermute | solution.py:145
  8.6 102.2 %all-to-all-start = ((f32[8,8,8,4,512]{4,3,2,1,0:T(4,128)}), f32[8,8,8,4,512]{4,3,2,1,0:T(4,128)}, u32[]{:S(2)}, u32[]{:S(2)}) async-start(f32[8,8,8,4,512]{4,3,2,1,0:T(4,128)} %copy-done.3), calls=%async_computation | async-start | bytes 8388608 | tf_op jit(solution)/shard_map/all_to_all | solution.py:202
  95.2 15.6 %collective-permute-start.2 = (f32[1,8,64,4,512]{4,3,2,1,0:T(4,128)}, f32[1,8,64,4,512]{4,3,2,1,0:T(4,128)}, u32[]{:S(2)}, u32[]{:S(2)}) collective-permute-start(f32[1,8,64,4,512]{4,3,2,1,0:T(4,128)} %collective-permute-done.refs_0_), channel_id=1, source_target_pairs={{0,1},{1,0},{2,3},{3,2},{4,5},{5,4},{6,7},{7,6},{8,9},{9,8},{10,11... | collective-permute-start | bytes 12582920 | tf_op jit(solution)/shard_map/ppermute | solution.py:145
  96.3 14.5 %collective-permute-start.3 = (f32[1,8,8,4,512]{4,3,2,1,0:T(4,128)S(1)}, f32[1,8,8,4,512]{4,3,2,1,0:T(4,128)}, u32[]{:S(2)}, u32[]{:S(2)}) collective-permute-start(f32[1,8,8,4,512]{4,3,2,1,0:T(4,128)S(1)} %shard_map.91), channel_id=1, source_target_pairs={{0,4},{4,0},{8,12},{12,8},{16,20},{20,16},{24,28},{28,24},{1,5},{5... | collective-permute-start | bytes 1572872 | tf_op jit(solution)/shard_map/ppermute | solution.py:145
  110.8 24.4 %collective-permute-start.4 = (f32[8,8,8,4,512]{4,3,2,1,0:T(4,128)}, f32[8,8,8,4,512]{4,3,2,1,0:T(4,128)}, u32[]{:S(2)}, u32[]{:S(2)}) collective-permute-start(f32[8,8,8,4,512]{4,3,2,1,0:T(4,128)} %all-to-all-done), channel_id=1, source_target_pairs={{0,1},{1,0},{2,3},{3,2},{4,5},{5,4},{6,7},{7,6},{8,9},{9,8},{10,11... | collective-permute-start | bytes 12582920 | tf_op jit(solution)/shard_map/ppermute | solution.py:145
  113.7 48.7 %collective-permute-start.10 = (f32[3,8,8,4,512]{4,3,2,1,0:T(4,128)}, f32[3,8,8,4,512]{4,3,2,1,0:T(4,128)}, u32[]{:S(2)}, u32[]{:S(2)}) collective-permute-start(f32[3,8,8,4,512]{4,3,2,1,0:T(4,128)} %bitcast.12), channel_id=1, source_target_pairs={{0,2},{1,3},{2,0},{3,1},{4,6},{5,7},{6,4},{7,5},{8,10},{9,11},{10,... | collective-permute-start | bytes 4718600 | tf_op jit(solution)/shard_map/ppermute | solution.py:145
  115.5 33.0 %collective-permute-start.8 = (f32[1,8,8,4,512]{4,3,2,1,0:T(4,128)}, f32[1,8,8,4,512]{4,3,2,1,0:T(4,128)}, u32[]{:S(2)}, u32[]{:S(2)}) collective-permute-start(f32[1,8,8,4,512]{4,3,2,1,0:T(4,128)} %shard_map.93), channel_id=1, source_target_pairs={{0,12},{4,8},{8,4},{12,0},{16,28},{20,24},{24,20},{28,16},{1,13},{... | collective-permute-start | bytes 1572872 | tf_op jit(solution)/shard_map/ppermute | solution.py:145
  118.0 35.2 %collective-permute-start.7 = (f32[1,8,8,4,512]{4,3,2,1,0:T(4,128)}, f32[1,8,8,4,512]{4,3,2,1,0:T(4,128)}, u32[]{:S(2)}, u32[]{:S(2)}) collective-permute-start(f32[1,8,8,4,512]{4,3,2,1,0:T(4,128)} %shard_map.92), channel_id=1, source_target_pairs={{0,8},{4,12},{8,0},{12,4},{16,24},{20,28},{24,16},{28,20},{1,9},{5... | collective-permute-start | bytes 1572872 | tf_op jit(solution)/shard_map/ppermute | solution.py:145
  118.4 34.8 %collective-permute-start.9 = (f32[1,8,8,4,512]{4,3,2,1,0:T(4,128)}, f32[1,8,8,4,512]{4,3,2,1,0:T(4,128)}, u32[]{:S(2)}, u32[]{:S(2)}) collective-permute-start(f32[1,8,8,4,512]{4,3,2,1,0:T(4,128)} %shard_map.94), channel_id=1, source_target_pairs={{0,16},{4,20},{8,24},{12,28},{16,0},{20,4},{24,8},{28,12},{1,17},{... | collective-permute-start | bytes 1572872 | tf_op jit(solution)/shard_map/ppermute | solution.py:145
  147.9 13.4 %collective-permute-start.5 = (f32[2,2,64,512]{3,2,1,0:T(8,128)S(1)}, f32[2,2,64,512]{3,2,1,0:T(8,128)}, u32[]{:S(2)}, u32[]{:S(2)}) collective-permute-start(f32[2,2,64,512]{3,2,1,0:T(8,128)S(1)} %dynamic-slice_bitcast_fusion), channel_id=1, source_target_pairs={{0,4},{4,0},{8,12},{12,8},{16,20},{20,16},{24,28},{28,24},{1,5},{5... | collective-permute-start | bytes 1572872 | tf_op jit(solution)/shard_map/ppermute | solution.py:145
  153.2 9.1 %collective-permute-start.12 = (f32[1,8,8,4,512]{4,3,2,1,0:T(4,128)}, f32[1,8,8,4,512]{4,3,2,1,0:T(4,128)S(1)}, u32[]{:S(2)}, u32[]{:S(2)}) collective-permute-start(f32[1,8,8,4,512]{4,3,2,1,0:T(4,128)} %collective-permute-done.9.refs_1_), channel_id=1, source_target_pairs={{0,1},{1,0},{2,3},{3,2},{4,5},{5,4},{6,7},{7,6},{8,9},{9,8},{10,11... | collective-permute-start | bytes 1572872 | tf_op jit(solution)/shard_map/ppermute | solution.py:145
  156.8 7.6 %collective-permute-start.11 = (f32[4,8,8,4,512]{4,3,2,1,0:T(4,128)}, f32[4,8,8,4,512]{4,3,2,1,0:T(4,128)}, u32[]{:S(2)}, u32[]{:S(2)}) collective-permute-start(f32[4,8,8,4,512]{4,3,2,1,0:T(4,128)} %pad_maximum_fusion.refs_0_), channel_id=1, source_target_pairs={{0,1},{1,0},{2,3},{3,2},{4,5},{5,4},{6,7},{7,6},{8,9},{9,8},{10,11... | collective-permute-start | bytes 6291464 | tf_op jit(solution)/shard_map/ppermute | solution.py:145
  162.4 3.8 %collective-permute-start.13 = (f32[3,8,8,4,512]{4,3,2,1,0:T(4,128)}, f32[3,8,8,4,512]{4,3,2,1,0:T(4,128)}, u32[]{:S(2)}, u32[]{:S(2)}) collective-permute-start(f32[3,8,8,4,512]{4,3,2,1,0:T(4,128)} %collective-permute-done.10.refs_2_), channel_id=1, source_target_pairs={{0,1},{1,0},{2,3},{3,2},{4,5},{5,4},{6,7},{7,6},{8,9},{9,8},{10,11... | collective-permute-start | bytes 4718600 | tf_op jit(solution)/shard_map/ppermute | solution.py:145
  162.8 15.9 %collective-permute-start.6 = (f32[2,64,512]{2,1,0:T(8,128)S(1)}, f32[2,64,512]{2,1,0:T(8,128)S(1)}, u32[]{:S(2)}, u32[]{:S(2)}) collective-permute-start(f32[2,64,512]{2,1,0:T(8,128)S(1)} %dynamic-slice_bitcast_fusion.3), channel_id=1, source_target_pairs={{0,8},{4,12},{8,0},{12,4},{16,24},{20,28},{24,16},{28,20},{1,9},{5... | collective-permute-start | bytes 786440 | tf_op jit(solution)/shard_map/ppermute | solution.py:145
  178.8 9.5 %collective-permute-start.14 = (f32[64,512]{1,0:T(8,128)S(1)}, f32[64,512]{1,0:T(8,128)S(1)}, u32[]{:S(2)}, u32[]{:S(2)}) collective-permute-start(f32[64,512]{1,0:T(8,128)S(1)} %dynamic-slice_bitcast_fusion.6), channel_id=1, source_target_pairs={{0,16},{4,20},{8,24},{12,28},{16,0},{20,4},{24,8},{28,12},{1,17},{... | collective-permute-start | bytes 393224 | tf_op jit(solution)/shard_map/ppermute | solution.py:145
  179.2 10.9 %collective-permute-start.18 = (f32[2,2,64,256]{3,2,1,0:T(8,128)S(1)}, f32[2,2,64,256]{3,2,1,0:T(8,128)S(1)}, u32[]{:S(2)}, u32[]{:S(2)}) collective-permute-start(f32[2,2,64,256]{3,2,1,0:T(8,128)S(1)} %dynamic-slice_bitcast_fusion.1), channel_id=1, source_target_pairs={{0,8},{4,12},{8,0},{12,4},{16,24},{20,28},{24,16},{28,20},{1,9},{5... | collective-permute-start | bytes 786440 | tf_op jit(solution)/shard_map/ppermute | solution.py:145
  180.8 29.4 %copy-start.7 = (f32[16]{0:T(128)S(1)}, f32[16]{0:T(128)}, u32[]{:S(2)}) copy-start(f32[16]{0:T(128)} %param.12) | copy-start | bytes 196
  180.8 11.8 %collective-permute-start.15 = (f32[2,2,64,256]{3,2,1,0:T(8,128)S(1)}, f32[2,2,64,256]{3,2,1,0:T(8,128)S(1)}, u32[]{:S(2)}, u32[]{:S(2)}) collective-permute-start(f32[2,2,64,256]{3,2,1,0:T(8,128)S(1)} %dynamic-slice_bitcast_fusion.2), channel_id=1, source_target_pairs={{0,4},{4,0},{8,12},{12,8},{16,20},{20,16},{24,28},{28,24},{1,5},{5... | collective-permute-start | bytes 786440 | tf_op jit(solution)/shard_map/ppermute | solution.py:145
  190.2 8.5 %collective-permute-start.19 = (f32[2,64,256]{2,1,0:T(8,128)S(1)}, f32[2,64,256]{2,1,0:T(8,128)S(1)}, u32[]{:S(2)}, u32[]{:S(2)}) collective-permute-start(f32[2,64,256]{2,1,0:T(8,128)S(1)} %dynamic-slice_bitcast_fusion.4), channel_id=1, source_target_pairs={{0,16},{4,20},{8,24},{12,28},{16,0},{20,4},{24,8},{28,12},{1,17},{... | collective-permute-start | bytes 393224 | tf_op jit(solution)/shard_map/ppermute | solution.py:145
  192.7 6.7 %collective-permute-start.16 = (f32[2,64,256]{2,1,0:T(8,128)S(1)}, f32[2,64,256]{2,1,0:T(8,128)S(1)}, u32[]{:S(2)}, u32[]{:S(2)}) collective-permute-start(f32[2,64,256]{2,1,0:T(8,128)S(1)} %dynamic-slice_bitcast_fusion.5), channel_id=1, source_target_pairs={{0,8},{4,12},{8,0},{12,4},{16,24},{20,28},{24,16},{28,20},{1,9},{5... | collective-permute-start | bytes 393224 | tf_op jit(solution)/shard_map/ppermute | solution.py:145
  198.8 4.3 %collective-permute-start.20 = (f32[64,256]{1,0:T(8,128)S(1)}, f32[64,256]{1,0:T(8,128)S(1)}, u32[]{:S(2)}, u32[]{:S(2)}) collective-permute-start(f32[64,256]{1,0:T(8,128)S(1)} %dynamic-slice_bitcast_fusion.7), channel_id=1, source_target_pairs={{0,4},{4,0},{8,12},{12,8},{16,20},{20,16},{24,28},{28,24},{1,5},{5... | collective-permute-start | bytes 196616 | tf_op jit(solution)/shard_map/ppermute | solution.py:145
  199.4 5.9 %collective-permute-start.17 = (f32[64,256]{1,0:T(8,128)S(1)}, f32[64,256]{1,0:T(8,128)S(1)}, u32[]{:S(2)}, u32[]{:S(2)}) collective-permute-start(f32[64,256]{1,0:T(8,128)S(1)} %dynamic-slice_bitcast_fusion.8), channel_id=1, source_target_pairs={{0,16},{4,20},{8,24},{12,28},{16,0},{20,4},{24,8},{28,12},{1,17},{... | collective-permute-start | bytes 196616 | tf_op jit(solution)/shard_map/ppermute | solution.py:145
  206.3 11.0 %all-to-all-start.1 = ((f32[32,1,64]{2,1,0:T(1,128)}), f32[32,1,64]{2,1,0:T(1,128)S(1)}, u32[]{:S(2)}, u32[]{:S(2)}) async-start(f32[32,1,64]{2,1,0:T(1,128)} %broadcast_in_dim.18), calls=%async_computation.1 | async-start | bytes 32768 | tf_op jit(solution)/shard_map/all_to_all | solution.py:185
  (10 other events, 67.6 us)

commit v4 on v3

--- a/solution.py
+++ b/solution.py
@@ -215,7 +215,6 @@
     row3 = shift(row2, "rep", 1)
     rows_in = row2.reshape(mine.shape)
     near = [take_blocks(rows_in, p1 ^ d, 1) for d in (0, 1, 2, 3, 4)]
-    near[1] = shift(near[1], "blk", 1)
     col0 = after(col0, row3, *near)
     late0 = take_blocks(
         col0.reshape((1, nb, rows * rows) + amplitudes.shape[2:]),
@@ -224,6 +223,7 @@
     )
     late2 = shift(late0.reshape((3,) + col0.shape[1:]), "rep", 2)
     col1 = shift(col0, "rep", 1)
+    near[1] = shift(after(near[1], col1), "blk", 1)
     near[2] = shift(after(near[2], late0), "blk", 2)
     near[3] = shift(after(near[3], late0), "blk", 3)
     far2 = shift(after(near[4], late0), "blk", 4)
@@ -243,7 +243,7 @@
     begun = [part for part, _, _ in sums0]
     far3 = shift(after(far2, part0), "rep", 1)
     late3 = shift(after(late2, far3, *begun), "rep", 1)
-    early2 = jnp.concatenate(near[:2] + [after(near[2], part0), after(near[3], part0)])
+    early2 = jnp.concatenate(near[:1] + [after(part, part0) for part in near[1:4]])
     early3 = shift(early2, "rep", 1)
     sources = []
     for base, early, far, late in ((0, early2, far2, late2), (half, early3, far3, late3)):

time: 221 us -> 216 us (0.977)
  starting transfers between devices: 33.2 us -> 27.2 us
    ppermute x21, starting transfers between devices: 23.6 us -> 18 us  [shift(): return lax.ppermute(value, axis, [(i, i ^ d) for i in range(size)])]
    all_to_all x1, waiting for transfers between devices: 0.01 us -> 3.43 us  [parts_small(): col0 = lax.all_to_all(own, 'blk', 0, 0, tiled=True)]
    ppermute x21, waiting for transfers between devices: 77.8 us -> 75.3 us  [shift(): return lax.ppermute(value, axis, [(i, i ^ d) for i in range(size)])]
  transfers between devices with their start and end apart: 23 -> 23, of which waited for: 11 -> 12; matrix products, arithmetic and copies ran while one was open for 3% -> 3% of each run, Pallas kernels for 36% -> 37%
where the time goes in v4:
time: 216 us; the launch traced here: 215 us
  waiting for transfers between devices  84.8 us (39%)
  Pallas kernels  80.5 us (37%)
  starting transfers between devices  27.2 us (13%)
  local copies, waits for them, and re-layouts  13 us (6%)
  other arithmetic  6.82 us (3%)
  between operations  2.92 us (1%)
    ppermute x21, waiting for transfers between devices, shift(): return lax.ppermute(value, axis, [(i, i ^ d) for i in range(size)])  75.3 us
    pallas_call x4, Pallas kernels, product(): pl.pallas_call(functools.partial(product_kernel, places, start is None, w...  49 us
    ppermute x21, starting transfers between devices, shift(): return lax.ppermute(value, axis, [(i, i ^ d) for i in range(size)])  18 us
    pallas_call x2, Pallas kernels, split_integrals(): pl.pallas_call(split_kernel, grid=(i // tile,), in_specs=[pl.BlockSpec((a...  17.4 us
    pallas_call x7, Pallas kernels, take_blocks(): pl.pallas_call(functools.partial(take_kernel, count), grid_spec=pltpu.Pre...  14.2 us
    unnamed x22, local copies, waits for them, and re-layouts  11.2 us
    all_to_all x1, waiting for transfers between devices, all_sum(): return jnp.sum(lax.all_to_all(copies, ('blk', 'rep'), 0, 0, tiled=True))  6.07 us
    all_to_all x1, starting transfers between devices, parts_small(): col0 = lax.all_to_all(own, 'blk', 0, 0, tiled=True)  5.81 us
  transfers between devices with their start and end apart: 23, of which 12 were waited for; matrix products, arithmetic and copies ran while one was open for 3% of the time, Pallas kernels for 37%

profile of v4, /device:TPU:0, one launch (start us, length us, event | category | flops | bytes accessed | tf_op | source)
XLA Modules:
  0.0 215.3 jit_solution(16809193331859084124)
XLA Ops:
  1.1 2.6 %collective-permute-start = (f32[1,8,64,4,512]{4,3,2,1,0:T(4,128)}, f32[1,8,64,4,512]{4,3,2,1,0:T(4,128)}, u32[]{:S(2)}, u32[]{:S(2)}) collective-permute-start(f32[1,8,64,4,512]{4,3,2,1,0:T(4,128)} %bitcast.70), channel_id=1, source_target_pairs={{0,2},{1,3},{2,0},{3,1},{4,6},{5,7},{6,4},{7,5},{8,10},{9,11},{10,... | collective-permute-start | bytes 12582920 | tf_op jit(solution)/shard_map/ppermute | solution.py:145
  3.7 2.9 %shard_map.86 = f32[8,8,8,4,512]{4,3,2,1,0:T(4,128)S(1)} custom-call(s32[8]{0:T(128)S(1)} %iota.3.where_ref, f32[8,8,8,4,512]{4,3,2,1,0:T(4,128)} %bitcast.71), custom_call_target="tpu_custom_call" | custom-call | flops 1024 | bytes 1024 | tf_op jit(solution)/shard_map/pallas_call | solution.py:62
  8.6 5.8 %all-to-all-start = ((f32[8,8,8,4,512]{4,3,2,1,0:T(4,128)}), f32[8,8,8,4,512]{4,3,2,1,0:T(4,128)}, u32[]{:S(2)}, u32[]{:S(2)}) async-start(f32[8,8,8,4,512]{4,3,2,1,0:T(4,128)} %copy-done.3), calls=%async_computation | async-start | bytes 8388608 | tf_op jit(solution)/shard_map/all_to_all | solution.py:202
  14.4 8.7 %shard_map.87 = (bf16[8,512,512]{2,1,0:T(8,128)(2,1)S(1)}, bf16[8,512,512]{2,1,0:T(8,128)(2,1)}) custom-call(f32[8,64,8,512]{3,2,1,0:T(8,128)} %in_ref.1), custom_call_target="tpu_custom_call" | custom-call | flops 1024 | bytes 1024 | tf_op jit(solution)/shard_map/pallas_call | solution.py:31
  25.1 2.2 %copy-done.1 = bf16[8,512,512]{2,1,0:T(8,128)(2,1)S(1)} copy-done((bf16[8,512,512]{2,1,0:T(8,128)(2,1)S(1)}, bf16[8,512,512]{2,1,0:T(8,128)(2,1)}, u32[]{:S(2)}) %copy-start.1) | copy-done | bytes 4194328
  27.3 12.0 %shard_map.88.refs_2_ = f32[512,512]{1,0:T(8,128)S(1)} custom-call(s32[1]{0:T(128)} %bitcast.p_ref.where_ref, bf16[8,512,512]{2,1,0:T(8,128)(2,1)S(1)} %copy-done.1, bf16[8,512,512]{2,1,0:T(8,128)(2,1)} %get-tuple-element.25.low_ref, f32[1,8,64,4,512]{4,3,2,1,0:T(4,128)} %bitcast.72, f32[1,8,64,4,512]{4,3,2,1,0:T(4,128)} %collective-permute-done.1.refs_1_), custom_call_target="tpu_custom_call" | custom-call | flops 1024 | bytes 1024 | tf_op jit(solution)/shard_map/pallas_call | solution.py:128
  39.4 8.7 %shard_map.89 = (bf16[8,512,512]{2,1,0:T(8,128)(2,1)S(1)}, bf16[8,512,512]{2,1,0:T(8,128)(2,1)}) custom-call(f32[8,64,8,512]{3,2,1,0:T(8,128)} %in_ref.2), custom_call_target="tpu_custom_call" | custom-call | flops 1024 | bytes 1024 | tf_op jit(solution)/shard_map/pallas_call | solution.py:31
  50.1 45.1 %collective-permute-done.refs_0_ = f32[1,8,64,4,512]{4,3,2,1,0:T(4,128)} collective-permute-done((f32[1,8,64,4,512]{4,3,2,1,0:T(4,128)}, f32[1,8,64,4,512]{4,3,2,1,0:T(4,128)}, u32[]{:S(2)}, u32[]{:S(2)}) %collective-permute-start) | collective-permute-done | bytes 4194336 | tf_op jit(solution)/shard_map/ppermute | solution.py:145
  104.6 3.4 %all-to-all-done = f32[8,8,8,4,512]{4,3,2,1,0:T(4,128)} async-done(((f32[8,8,8,4,512]{4,3,2,1,0:T(4,128)}), f32[8,8,8,4,512]{4,3,2,1,0:T(4,128)}, u32[]{:S(2)}, u32[]{:S(2)}) %all-to-all-start) | async-done | bytes 4194336 | tf_op jit(solution)/shard_map/all_to_all | solution.py:202
  108.0 2.8 %shard_map.95 = f32[3,1,64,4,512]{4,3,2,1,0:T(4,128)} custom-call(s32[3]{0:T(128)S(1)} %broadcast_xor_fusion.where_ref, f32[1,8,64,4,512]{4,3,2,1,0:T(4,128)} %bitcast.4.in_ref), custom_call_target="tpu_custom_call" | custom-call | flops 1024 | bytes 1024 | tf_op jit(solution)/shard_map/pallas_call | solution.py:62
  117.0 2.2 %copy-done.2 = bf16[8,512,512]{2,1,0:T(8,128)(2,1)S(1)} copy-done((bf16[8,512,512]{2,1,0:T(8,128)(2,1)S(1)}, bf16[8,512,512]{2,1,0:T(8,128)(2,1)}, u32[]{:S(2)}) %copy-start.2) | copy-done | bytes 4194328
  119.2 12.0 %shard_map.96.refs_6_ = f32[512,512]{1,0:T(8,128)S(1)} custom-call(s32[1]{0:T(128)} %bitcast.p_ref.where_ref, bf16[8,512,512]{2,1,0:T(8,128)(2,1)S(1)} %copy-done.2, bf16[8,512,512]{2,1,0:T(8,128)(2,1)} %get-tuple-element.25.low_ref, f32[1,8,64,4,512]{4,3,2,1,0:T(4,128)} %collective-permute-done.refs_0_, f32[1,8,64,4,512]{4,3,2,1,0:T(4,128)} %collective-permute-done.2.refs_1_), custom_call_target="tpu_custom_call" | custom-call | flops 1024 | bytes 1024 | tf_op jit(solution)/shard_map/pallas_call | solution.py:128
  131.2 12.5 %shard_map.97 = f32[512,512]{1,0:T(8,128)S(1)} custom-call(s32[1]{0:T(128)} %bitcast.p_ref.where_ref, bf16[8,512,512]{2,1,0:T(8,128)(2,1)} %copy-done.4, bf16[8,512,512]{2,1,0:T(8,128)(2,1)} %get-tuple-element.32.low_ref, f32[1,64,8,4,512]{4,3,2,1,0:T(4,128)} %bitcast.5.refs_0_, f32[1,64,8,4,512]{4,3,2,1,0:T(4,128)} %bitcast.6.refs_1_, ...), custom_call_target="tpu_custom_call" | custom-call | flops 1024 | bytes 1024 | tf_op jit(solution)/shard_map/pallas_call | solution.py:128
  144.5 4.7 %collective-permute-done.7 = f32[1,8,8,4,512]{4,3,2,1,0:T(4,128)} collective-permute-done((f32[1,8,8,4,512]{4,3,2,1,0:T(4,128)}, f32[1,8,8,4,512]{4,3,2,1,0:T(4,128)}, u32[]{:S(2)}, u32[]{:S(2)}) %collective-permute-start.7) | collective-permute-done | bytes 524320 | tf_op jit(solution)/shard_map/ppermute | solution.py:145
  149.2 3.6 %pad_maximum_fusion.refs_0_ = f32[4,8,8,4,512]{4,3,2,1,0:T(4,128)} fusion(f32[1,8,8,4,512]{4,3,2,1,0:T(4,128)} %collective-permute-done.8, f32[1,8,8,4,512]{4,3,2,1,0:T(4,128)} %collective-permute-done.7, f32[1,8,8,4,512]{4,3,2,1,0:T(4,128)} %collective-permute-done.6, f32[1,8,8,4,512]{4,3,2,1,0:T(4,128)S(1)} %copy-done.6), kind=kLoop, calls=%fused_computation | loop fusion | flops 1572864 | bytes 4194304 | tf_op jit(solution)/shard_map/concatenate | solution.py:246
  153.3 4.4 %collective-permute-done.4 = f32[2,2,64,512]{3,2,1,0:T(8,128)} collective-permute-done((f32[2,2,64,512]{3,2,1,0:T(8,128)S(1)}, f32[2,2,64,512]{3,2,1,0:T(8,128)}, u32[]{:S(2)}, u32[]{:S(2)}) %collective-permute-start.4) | collective-permute-done | bytes 524320 | tf_op jit(solution)/shard_map/ppermute | solution.py:145
  159.4 3.3 %collective-permute-done.13.refs_5_ = f32[3,8,8,4,512]{4,3,2,1,0:T(4,128)} collective-permute-done((f32[3,8,8,4,512]{4,3,2,1,0:T(4,128)}, f32[3,8,8,4,512]{4,3,2,1,0:T(4,128)}, u32[]{:S(2)}, u32[]{:S(2)}) %collective-permute-start.13) | collective-permute-done | bytes 1572896 | tf_op jit(solution)/shard_map/ppermute | solution.py:145
  162.7 12.4 %shard_map.98 = f32[512,512]{1,0:T(8,128)S(1)} custom-call(s32[1]{0:T(128)} %bitcast.p_ref.where_ref, bf16[8,512,512]{2,1,0:T(8,128)(2,1)} %copy-done.4, bf16[8,512,512]{2,1,0:T(8,128)(2,1)} %get-tuple-element.32.low_ref, f32[4,8,8,4,512]{4,3,2,1,0:T(4,128)} %pad_maximum_fusion.refs_0_, f32[1,8,8,4,512]{4,3,2,1,0:T(4,128)} %collective-permute-done.9.refs_1_, ...), custom_call_target="tpu_custom_call" | custom-call | flops 1024 | bytes 1024 | tf_op jit(solution)/shard_map/pallas_call | solution.py:128
  178.9 5.2 %collective-permute-done.14 = f32[64,512]{1,0:T(8,128)S(1)} collective-permute-done((f32[64,512]{1,0:T(8,128)S(1)}, f32[64,512]{1,0:T(8,128)S(1)}, u32[]{:S(2)}, u32[]{:S(2)}) %collective-permute-start.14) | collective-permute-done | bytes 131104 | tf_op jit(solution)/shard_map/ppermute | solution.py:145
  187.5 2.2 %collective-permute-start.16 = (f32[2,64,256]{2,1,0:T(8,128)S(1)}, f32[2,64,256]{2,1,0:T(8,128)S(1)}, u32[]{:S(2)}, u32[]{:S(2)}) collective-permute-start(f32[2,64,256]{2,1,0:T(8,128)S(1)} %dynamic-slice_bitcast_fusion.5), channel_id=1, source_target_pairs={{0,8},{4,12},{8,0},{12,4},{16,24},{20,28},{24,16},{28,20},{1,9},{5... | collective-permute-start | bytes 393224 | tf_op jit(solution)/shard_map/ppermute | solution.py:145
  189.7 5.4 %collective-permute-done.19 = f32[2,64,256]{2,1,0:T(8,128)S(1)} collective-permute-done((f32[2,64,256]{2,1,0:T(8,128)S(1)}, f32[2,64,256]{2,1,0:T(8,128)S(1)}, u32[]{:S(2)}, u32[]{:S(2)}) %collective-permute-start.19) | collective-permute-done | bytes 131104 | tf_op jit(solution)/shard_map/ppermute | solution.py:145
  196.2 3.3 %collective-permute-done.20 = f32[64,256]{1,0:T(8,128)S(1)} collective-permute-done((f32[64,256]{1,0:T(8,128)S(1)}, f32[64,256]{1,0:T(8,128)S(1)}, u32[]{:S(2)}, u32[]{:S(2)}) %collective-permute-start.20) | collective-permute-done | bytes 65568 | tf_op jit(solution)/shard_map/ppermute | solution.py:145
  202.3 3.5 %all-to-all-start.1 = ((f32[32,1,64]{2,1,0:T(1,128)}), f32[32,1,64]{2,1,0:T(1,128)S(1)}, u32[]{:S(2)}, u32[]{:S(2)}) async-start(f32[32,1,64]{2,1,0:T(1,128)} %broadcast_in_dim.18), calls=%async_computation.1 | async-start | bytes 32768 | tf_op jit(solution)/shard_map/all_to_all | solution.py:185
  206.8 6.1 %all-to-all-done.1 = f32[32,1,64]{2,1,0:T(1,128)S(1)} async-done(((f32[32,1,64]{2,1,0:T(1,128)}), f32[32,1,64]{2,1,0:T(1,128)S(1)}, u32[]{:S(2)}, u32[]{:S(2)}) %all-to-all-start.1) | async-done | bytes 8224 | tf_op jit(solution)/shard_map/all_to_all | solution.py:185
  (101 shorter events, 37.5 us)
Async XLA Ops:
  0.6 24.5 %collective-permute-start.1 = (f32[1,8,64,4,512]{4,3,2,1,0:T(4,128)}, f32[1,8,64,4,512]{4,3,2,1,0:T(4,128)}, u32[]{:S(2)}, u32[]{:S(2)}) collective-permute-start(f32[1,8,64,4,512]{4,3,2,1,0:T(4,128)} %bitcast.69), channel_id=1, source_target_pairs={{0,1},{1,0},{2,3},{3,2},{4,5},{5,4},{6,7},{7,6},{8,9},{9,8},{10,11... | collective-permute-start | bytes 12582920 | tf_op jit(solution)/shard_map/ppermute | solution.py:145
  1.1 94.1 %collective-permute-start = (f32[1,8,64,4,512]{4,3,2,1,0:T(4,128)}, f32[1,8,64,4,512]{4,3,2,1,0:T(4,128)}, u32[]{:S(2)}, u32[]{:S(2)}) collective-permute-start(f32[1,8,64,4,512]{4,3,2,1,0:T(4,128)} %bitcast.70), channel_id=1, source_target_pairs={{0,2},{1,3},{2,0},{3,1},{4,6},{5,7},{6,4},{7,5},{8,10},{9,11},{10,... | collective-permute-start | bytes 12582920 | tf_op jit(solution)/shard_map/ppermute | solution.py:145
  8.6 99.4 %all-to-all-start = ((f32[8,8,8,4,512]{4,3,2,1,0:T(4,128)}), f32[8,8,8,4,512]{4,3,2,1,0:T(4,128)}, u32[]{:S(2)}, u32[]{:S(2)}) async-start(f32[8,8,8,4,512]{4,3,2,1,0:T(4,128)} %copy-done.3), calls=%async_computation | async-start | bytes 8388608 | tf_op jit(solution)/shard_map/all_to_all | solution.py:202
  95.2 12.8 %collective-permute-start.2 = (f32[1,8,64,4,512]{4,3,2,1,0:T(4,128)}, f32[1,8,64,4,512]{4,3,2,1,0:T(4,128)}, u32[]{:S(2)}, u32[]{:S(2)}) collective-permute-start(f32[1,8,64,4,512]{4,3,2,1,0:T(4,128)} %collective-permute-done.refs_0_), channel_id=1, source_target_pairs={{0,1},{1,0},{2,3},{3,2},{4,5},{5,4},{6,7},{7,6},{8,9},{9,8},{10,11... | collective-permute-start | bytes 12582920 | tf_op jit(solution)/shard_map/ppermute | solution.py:145
  108.0 7.5 %collective-permute-start.3 = (f32[8,8,8,4,512]{4,3,2,1,0:T(4,128)}, f32[8,8,8,4,512]{4,3,2,1,0:T(4,128)}, u32[]{:S(2)}, u32[]{:S(2)}) collective-permute-start(f32[8,8,8,4,512]{4,3,2,1,0:T(4,128)} %all-to-all-done), channel_id=1, source_target_pairs={{0,1},{1,0},{2,3},{3,2},{4,5},{5,4},{6,7},{7,6},{8,9},{9,8},{10,11... | collective-permute-start | bytes 12582920 | tf_op jit(solution)/shard_map/ppermute | solution.py:145
  110.8 48.0 %collective-permute-start.10 = (f32[3,8,8,4,512]{4,3,2,1,0:T(4,128)}, f32[3,8,8,4,512]{4,3,2,1,0:T(4,128)}, u32[]{:S(2)}, u32[]{:S(2)}) collective-permute-start(f32[3,8,8,4,512]{4,3,2,1,0:T(4,128)} %bitcast.12), channel_id=1, source_target_pairs={{0,2},{1,3},{2,0},{3,1},{4,6},{5,7},{6,4},{7,5},{8,10},{9,11},{10,... | collective-permute-start | bytes 4718600 | tf_op jit(solution)/shard_map/ppermute | solution.py:145
  111.4 32.4 %collective-permute-start.8 = (f32[1,8,8,4,512]{4,3,2,1,0:T(4,128)}, f32[1,8,8,4,512]{4,3,2,1,0:T(4,128)}, u32[]{:S(2)}, u32[]{:S(2)}) collective-permute-start(f32[1,8,8,4,512]{4,3,2,1,0:T(4,128)} %shard_map.93), channel_id=1, source_target_pairs={{0,12},{4,8},{8,4},{12,0},{16,28},{20,24},{24,20},{28,16},{1,13},{... | collective-permute-start | bytes 1572872 | tf_op jit(solution)/shard_map/ppermute | solution.py:145
  112.3 36.9 %collective-permute-start.7 = (f32[1,8,8,4,512]{4,3,2,1,0:T(4,128)}, f32[1,8,8,4,512]{4,3,2,1,0:T(4,128)}, u32[]{:S(2)}, u32[]{:S(2)}) collective-permute-start(f32[1,8,8,4,512]{4,3,2,1,0:T(4,128)} %shard_map.92), channel_id=1, source_target_pairs={{0,8},{4,12},{8,0},{12,4},{16,24},{20,28},{24,16},{28,20},{1,9},{5... | collective-permute-start | bytes 1572872 | tf_op jit(solution)/shard_map/ppermute | solution.py:145
  114.3 34.8 %collective-permute-start.9 = (f32[1,8,8,4,512]{4,3,2,1,0:T(4,128)}, f32[1,8,8,4,512]{4,3,2,1,0:T(4,128)}, u32[]{:S(2)}, u32[]{:S(2)}) collective-permute-start(f32[1,8,8,4,512]{4,3,2,1,0:T(4,128)} %shard_map.94), channel_id=1, source_target_pairs={{0,16},{4,20},{8,24},{12,28},{16,0},{20,4},{24,8},{28,12},{1,17},{... | collective-permute-start | bytes 1572872 | tf_op jit(solution)/shard_map/ppermute | solution.py:145
  115.5 33.7 %collective-permute-start.6 = (f32[1,8,8,4,512]{4,3,2,1,0:T(4,128)}, f32[1,8,8,4,512]{4,3,2,1,0:T(4,128)}, u32[]{:S(2)}, u32[]{:S(2)}) collective-permute-start(f32[1,8,8,4,512]{4,3,2,1,0:T(4,128)} %shard_map.91), channel_id=1, source_target_pairs={{0,4},{4,0},{8,12},{12,8},{16,20},{20,16},{24,28},{28,24},{1,5},{5... | collective-permute-start | bytes 1572872 | tf_op jit(solution)/shard_map/ppermute | solution.py:145
  143.8 13.9 %collective-permute-start.4 = (f32[2,2,64,512]{3,2,1,0:T(8,128)S(1)}, f32[2,2,64,512]{3,2,1,0:T(8,128)}, u32[]{:S(2)}, u32[]{:S(2)}) collective-permute-start(f32[2,2,64,512]{3,2,1,0:T(8,128)S(1)} %dynamic-slice_bitcast_fusion), channel_id=1, source_target_pairs={{0,4},{4,0},{8,12},{12,8},{16,20},{20,16},{24,28},{28,24},{1,5},{5... | collective-permute-start | bytes 1572872 | tf_op jit(solution)/shard_map/ppermute | solution.py:145
  149.2 9.6 %collective-permute-start.12 = (f32[1,8,8,4,512]{4,3,2,1,0:T(4,128)}, f32[1,8,8,4,512]{4,3,2,1,0:T(4,128)S(1)}, u32[]{:S(2)}, u32[]{:S(2)}) collective-permute-start(f32[1,8,8,4,512]{4,3,2,1,0:T(4,128)} %collective-permute-done.9.refs_1_), channel_id=1, source_target_pairs={{0,1},{1,0},{2,3},{3,2},{4,5},{5,4},{6,7},{7,6},{8,9},{9,8},{10,11... | collective-permute-start | bytes 1572872 | tf_op jit(solution)/shard_map/ppermute | solution.py:145
  152.8 9.9 %collective-permute-start.11 = (f32[4,8,8,4,512]{4,3,2,1,0:T(4,128)}, f32[4,8,8,4,512]{4,3,2,1,0:T(4,128)}, u32[]{:S(2)}, u32[]{:S(2)}) collective-permute-start(f32[4,8,8,4,512]{4,3,2,1,0:T(4,128)} %pad_maximum_fusion.refs_0_), channel_id=1, source_target_pairs={{0,1},{1,0},{2,3},{3,2},{4,5},{5,4},{6,7},{7,6},{8,9},{9,8},{10,11... | collective-permute-start | bytes 6291464 | tf_op jit(solution)/shard_map/ppermute | solution.py:145
  158.8 3.8 %collective-permute-start.13 = (f32[3,8,8,4,512]{4,3,2,1,0:T(4,128)}, f32[3,8,8,4,512]{4,3,2,1,0:T(4,128)}, u32[]{:S(2)}, u32[]{:S(2)}) collective-permute-start(f32[3,8,8,4,512]{4,3,2,1,0:T(4,128)} %collective-permute-done.10.refs_2_), channel_id=1, source_target_pairs={{0,1},{1,0},{2,3},{3,2},{4,5},{5,4},{6,7},{7,6},{8,9},{9,8},{10,11... | collective-permute-start | bytes 4718600 | tf_op jit(solution)/shard_map/ppermute | solution.py:145
  159.3 15.9 %collective-permute-start.5 = (f32[2,64,512]{2,1,0:T(8,128)S(1)}, f32[2,64,512]{2,1,0:T(8,128)S(1)}, u32[]{:S(2)}, u32[]{:S(2)}) collective-permute-start(f32[2,64,512]{2,1,0:T(8,128)S(1)} %dynamic-slice_bitcast_fusion.3), channel_id=1, source_target_pairs={{0,8},{4,12},{8,0},{12,4},{16,24},{20,28},{24,16},{28,20},{1,9},{5... | collective-permute-start | bytes 786440 | tf_op jit(solution)/shard_map/ppermute | solution.py:145
  175.2 8.8 %collective-permute-start.14 = (f32[64,512]{1,0:T(8,128)S(1)}, f32[64,512]{1,0:T(8,128)S(1)}, u32[]{:S(2)}, u32[]{:S(2)}) collective-permute-start(f32[64,512]{1,0:T(8,128)S(1)} %dynamic-slice_bitcast_fusion.6), channel_id=1, source_target_pairs={{0,16},{4,20},{8,24},{12,28},{16,0},{20,4},{24,8},{28,12},{1,17},{... | collective-permute-start | bytes 393224 | tf_op jit(solution)/shard_map/ppermute | solution.py:145
  175.4 11.2 %collective-permute-start.18 = (f32[2,2,64,256]{3,2,1,0:T(8,128)S(1)}, f32[2,2,64,256]{3,2,1,0:T(8,128)S(1)}, u32[]{:S(2)}, u32[]{:S(2)}) collective-permute-start(f32[2,2,64,256]{3,2,1,0:T(8,128)S(1)} %dynamic-slice_bitcast_fusion.1), channel_id=1, source_target_pairs={{0,8},{4,12},{8,0},{12,4},{16,24},{20,28},{24,16},{28,20},{1,9},{5... | collective-permute-start | bytes 786440 | tf_op jit(solution)/shard_map/ppermute | solution.py:145
  177.4 28.4 %copy-start.7 = (f32[16]{0:T(128)S(1)}, f32[16]{0:T(128)}, u32[]{:S(2)}) copy-start(f32[16]{0:T(128)} %param.12) | copy-start | bytes 196
  177.4 10.0 %collective-permute-start.15 = (f32[2,2,64,256]{3,2,1,0:T(8,128)S(1)}, f32[2,2,64,256]{3,2,1,0:T(8,128)S(1)}, u32[]{:S(2)}, u32[]{:S(2)}) collective-permute-start(f32[2,2,64,256]{3,2,1,0:T(8,128)S(1)} %dynamic-slice_bitcast_fusion.2), channel_id=1, source_target_pairs={{0,4},{4,0},{8,12},{12,8},{16,20},{20,16},{24,28},{28,24},{1,5},{5... | collective-permute-start | bytes 786440 | tf_op jit(solution)/shard_map/ppermute | solution.py:145
  186.6 8.5 %collective-permute-start.19 = (f32[2,64,256]{2,1,0:T(8,128)S(1)}, f32[2,64,256]{2,1,0:T(8,128)S(1)}, u32[]{:S(2)}, u32[]{:S(2)}) collective-permute-start(f32[2,64,256]{2,1,0:T(8,128)S(1)} %dynamic-slice_bitcast_fusion.4), channel_id=1, source_target_pairs={{0,16},{4,20},{8,24},{12,28},{16,0},{20,4},{24,8},{28,12},{1,17},{... | collective-permute-start | bytes 393224 | tf_op jit(solution)/shard_map/ppermute | solution.py:145
  187.5 8.5 %collective-permute-start.16 = (f32[2,64,256]{2,1,0:T(8,128)S(1)}, f32[2,64,256]{2,1,0:T(8,128)S(1)}, u32[]{:S(2)}, u32[]{:S(2)}) collective-permute-start(f32[2,64,256]{2,1,0:T(8,128)S(1)} %dynamic-slice_bitcast_fusion.5), channel_id=1, source_target_pairs={{0,8},{4,12},{8,0},{12,4},{16,24},{20,28},{24,16},{28,20},{1,9},{5... | collective-permute-start | bytes 393224 | tf_op jit(solution)/shard_map/ppermute | solution.py:145
  195.2 4.3 %collective-permute-start.20 = (f32[64,256]{1,0:T(8,128)S(1)}, f32[64,256]{1,0:T(8,128)S(1)}, u32[]{:S(2)}, u32[]{:S(2)}) collective-permute-start(f32[64,256]{1,0:T(8,128)S(1)} %dynamic-slice_bitcast_fusion.7), channel_id=1, source_target_pairs={{0,4},{4,0},{8,12},{12,8},{16,20},{20,16},{24,28},{28,24},{1,5},{5... | collective-permute-start | bytes 196616 | tf_op jit(solution)/shard_map/ppermute | solution.py:145
  196.1 5.2 %collective-permute-start.17 = (f32[64,256]{1,0:T(8,128)S(1)}, f32[64,256]{1,0:T(8,128)S(1)}, u32[]{:S(2)}, u32[]{:S(2)}) collective-permute-start(f32[64,256]{1,0:T(8,128)S(1)} %dynamic-slice_bitcast_fusion.8), channel_id=1, source_target_pairs={{0,16},{4,20},{8,24},{12,28},{16,0},{20,4},{24,8},{28,12},{1,17},{... | collective-permute-start | bytes 196616 | tf_op jit(solution)/shard_map/ppermute | solution.py:145
  202.3 10.6 %all-to-all-start.1 = ((f32[32,1,64]{2,1,0:T(1,128)}), f32[32,1,64]{2,1,0:T(1,128)S(1)}, u32[]{:S(2)}, u32[]{:S(2)}) async-start(f32[32,1,64]{2,1,0:T(1,128)} %broadcast_in_dim.18), calls=%async_computation.1 | async-start | bytes 32768 | tf_op jit(solution)/shard_map/all_to_all | solution.py:185
  (10 other events, 66.8 us)

commit v5 on v4

--- a/solution.py
+++ b/solution.py
@@ -167,7 +167,7 @@
     left = list(reversed(bits))
     return [
         (part[:, at : at + half].reshape((2,) * len(bits) + (-1, half)), left, order)
-        for at, order in ((0, bits), (half, bits[1:] + bits[:1]))[:pieces]
+        for at, order in ((0, bits), (half, bits[1:2] + bits[:1] + bits[2:]))[:pieces]
     ]
 
 

time: 216 us -> 214 us (level)
  waiting for transfers between devices: 84.8 us -> 81.9 us
    ppermute x21, waiting for transfers between devices: 75.3 us -> 72.4 us  [shift(): return lax.ppermute(value, axis, [(i, i ^ d) for i in range(size)])]
  transfers between devices with their start and end apart: 23 -> 23, of which waited for: 12 -> 13; matrix products, arithmetic and copies ran while one was open for 3% -> 3% of each run, Pallas kernels for 37% -> 38%
where the time goes in v5:
time: 214 us; the launch traced here: 213 us
  waiting for transfers between devices  81.9 us (38%)
  Pallas kernels  80.5 us (38%)
  starting transfers between devices  27.7 us (13%)
  local copies, waits for them, and re-layouts  13 us (6%)
  other arithmetic  6.82 us (3%)
  between operations  2.91 us (1%)
    ppermute x21, waiting for transfers between devices, shift(): return lax.ppermute(value, axis, [(i, i ^ d) for i in range(size)])  72.4 us
    pallas_call x4, Pallas kernels, product(): pl.pallas_call(functools.partial(product_kernel, places, start is None, w...  49 us
    ppermute x21, starting transfers between devices, shift(): return lax.ppermute(value, axis, [(i, i ^ d) for i in range(size)])  18 us
    pallas_call x2, Pallas kernels, split_integrals(): pl.pallas_call(split_kernel, grid=(i // tile,), in_specs=[pl.BlockSpec((a...  17.4 us
    pallas_call x7, Pallas kernels, take_blocks(): pl.pallas_call(functools.partial(take_kernel, count), grid_spec=pltpu.Pre...  14.2 us
    unnamed x22, local copies, waits for them, and re-layouts  11.2 us
    all_to_all x1, waiting for transfers between devices, all_sum(): return jnp.sum(lax.all_to_all(copies, ('blk', 'rep'), 0, 0, tiled=True))  6.07 us
    all_to_all x1, starting transfers between devices, parts_small(): col0 = lax.all_to_all(own, 'blk', 0, 0, tiled=True)  5.81 us
  transfers between devices with their start and end apart: 23, of which 13 were waited for; matrix products, arithmetic and copies ran while one was open for 3% of the time, Pallas kernels for 38%

profile of v5, /device:TPU:0, one launch (start us, length us, event | category | flops | bytes accessed | tf_op | source)
XLA Modules:
  0.0 212.9 jit_solution(5509136050535649975)
XLA Ops:
  1.1 2.6 %collective-permute-start = (f32[1,8,64,4,512]{4,3,2,1,0:T(4,128)}, f32[1,8,64,4,512]{4,3,2,1,0:T(4,128)}, u32[]{:S(2)}, u32[]{:S(2)}) collective-permute-start(f32[1,8,64,4,512]{4,3,2,1,0:T(4,128)} %bitcast.70), channel_id=1, source_target_pairs={{0,2},{1,3},{2,0},{3,1},{4,6},{5,7},{6,4},{7,5},{8,10},{9,11},{10,... | collective-permute-start | bytes 12582920 | tf_op jit(solution)/shard_map/ppermute | solution.py:145
  3.7 2.9 %shard_map.86 = f32[8,8,8,4,512]{4,3,2,1,0:T(4,128)S(1)} custom-call(s32[8]{0:T(128)S(1)} %iota.3.where_ref, f32[8,8,8,4,512]{4,3,2,1,0:T(4,128)} %bitcast.71), custom_call_target="tpu_custom_call" | custom-call | flops 1024 | bytes 1024 | tf_op jit(solution)/shard_map/pallas_call | solution.py:62
  8.6 5.8 %all-to-all-start = ((f32[8,8,8,4,512]{4,3,2,1,0:T(4,128)}), f32[8,8,8,4,512]{4,3,2,1,0:T(4,128)}, u32[]{:S(2)}, u32[]{:S(2)}) async-start(f32[8,8,8,4,512]{4,3,2,1,0:T(4,128)} %copy-done.3), calls=%async_computation | async-start | bytes 8388608 | tf_op jit(solution)/shard_map/all_to_all | solution.py:202
  14.4 8.7 %shard_map.87 = (bf16[8,512,512]{2,1,0:T(8,128)(2,1)S(1)}, bf16[8,512,512]{2,1,0:T(8,128)(2,1)}) custom-call(f32[8,64,8,512]{3,2,1,0:T(8,128)} %in_ref.1), custom_call_target="tpu_custom_call" | custom-call | flops 1024 | bytes 1024 | tf_op jit(solution)/shard_map/pallas_call | solution.py:31
  25.1 2.2 %copy-done.1 = bf16[8,512,512]{2,1,0:T(8,128)(2,1)S(1)} copy-done((bf16[8,512,512]{2,1,0:T(8,128)(2,1)S(1)}, bf16[8,512,512]{2,1,0:T(8,128)(2,1)}, u32[]{:S(2)}) %copy-start.1) | copy-done | bytes 4194328
  27.3 12.0 %shard_map.88.refs_2_ = f32[512,512]{1,0:T(8,128)S(1)} custom-call(s32[1]{0:T(128)} %bitcast.p_ref.where_ref, bf16[8,512,512]{2,1,0:T(8,128)(2,1)S(1)} %copy-done.1, bf16[8,512,512]{2,1,0:T(8,128)(2,1)} %get-tuple-element.25.low_ref, f32[1,8,64,4,512]{4,3,2,1,0:T(4,128)} %bitcast.72, f32[1,8,64,4,512]{4,3,2,1,0:T(4,128)} %collective-permute-done.1.refs_1_), custom_call_target="tpu_custom_call" | custom-call | flops 1024 | bytes 1024 | tf_op jit(solution)/shard_map/pallas_call | solution.py:128
  39.4 8.7 %shard_map.89 = (bf16[8,512,512]{2,1,0:T(8,128)(2,1)S(1)}, bf16[8,512,512]{2,1,0:T(8,128)(2,1)}) custom-call(f32[8,64,8,512]{3,2,1,0:T(8,128)} %in_ref.2), custom_call_target="tpu_custom_call" | custom-call | flops 1024 | bytes 1024 | tf_op jit(solution)/shard_map/pallas_call | solution.py:31
  50.1 45.1 %collective-permute-done.refs_0_ = f32[1,8,64,4,512]{4,3,2,1,0:T(4,128)} collective-permute-done((f32[1,8,64,4,512]{4,3,2,1,0:T(4,128)}, f32[1,8,64,4,512]{4,3,2,1,0:T(4,128)}, u32[]{:S(2)}, u32[]{:S(2)}) %collective-permute-start) | collective-permute-done | bytes 4194336 | tf_op jit(solution)/shard_map/ppermute | solution.py:145
  104.6 3.4 %all-to-all-done = f32[8,8,8,4,512]{4,3,2,1,0:T(4,128)} async-done(((f32[8,8,8,4,512]{4,3,2,1,0:T(4,128)}), f32[8,8,8,4,512]{4,3,2,1,0:T(4,128)}, u32[]{:S(2)}, u32[]{:S(2)}) %all-to-all-start) | async-done | bytes 4194336 | tf_op jit(solution)/shard_map/all_to_all | solution.py:202
  108.0 2.8 %shard_map.95 = f32[3,1,64,4,512]{4,3,2,1,0:T(4,128)} custom-call(s32[3]{0:T(128)S(1)} %broadcast_xor_fusion.where_ref, f32[1,8,64,4,512]{4,3,2,1,0:T(4,128)} %bitcast.4.in_ref), custom_call_target="tpu_custom_call" | custom-call | flops 1024 | bytes 1024 | tf_op jit(solution)/shard_map/pallas_call | solution.py:62
  117.0 2.2 %copy-done.2 = bf16[8,512,512]{2,1,0:T(8,128)(2,1)S(1)} copy-done((bf16[8,512,512]{2,1,0:T(8,128)(2,1)S(1)}, bf16[8,512,512]{2,1,0:T(8,128)(2,1)}, u32[]{:S(2)}) %copy-start.2) | copy-done | bytes 4194328
  119.2 12.0 %shard_map.96.refs_6_ = f32[512,512]{1,0:T(8,128)S(1)} custom-call(s32[1]{0:T(128)} %bitcast.p_ref.where_ref, bf16[8,512,512]{2,1,0:T(8,128)(2,1)S(1)} %copy-done.2, bf16[8,512,512]{2,1,0:T(8,128)(2,1)} %get-tuple-element.25.low_ref, f32[1,8,64,4,512]{4,3,2,1,0:T(4,128)} %collective-permute-done.refs_0_, f32[1,8,64,4,512]{4,3,2,1,0:T(4,128)} %collective-permute-done.2.refs_1_), custom_call_target="tpu_custom_call" | custom-call | flops 1024 | bytes 1024 | tf_op jit(solution)/shard_map/pallas_call | solution.py:128
  131.2 12.5 %shard_map.97 = f32[512,512]{1,0:T(8,128)S(1)} custom-call(s32[1]{0:T(128)} %bitcast.p_ref.where_ref, bf16[8,512,512]{2,1,0:T(8,128)(2,1)} %copy-done.4, bf16[8,512,512]{2,1,0:T(8,128)(2,1)} %get-tuple-element.32.low_ref, f32[1,64,8,4,512]{4,3,2,1,0:T(4,128)} %bitcast.5.refs_0_, f32[1,64,8,4,512]{4,3,2,1,0:T(4,128)} %bitcast.6.refs_1_, ...), custom_call_target="tpu_custom_call" | custom-call | flops 1024 | bytes 1024 | tf_op jit(solution)/shard_map/pallas_call | solution.py:128
  144.5 4.7 %collective-permute-done.7 = f32[1,8,8,4,512]{4,3,2,1,0:T(4,128)} collective-permute-done((f32[1,8,8,4,512]{4,3,2,1,0:T(4,128)}, f32[1,8,8,4,512]{4,3,2,1,0:T(4,128)}, u32[]{:S(2)}, u32[]{:S(2)}) %collective-permute-start.7) | collective-permute-done | bytes 524320 | tf_op jit(solution)/shard_map/ppermute | solution.py:145
  149.2 3.6 %pad_maximum_fusion.refs_0_ = f32[4,8,8,4,512]{4,3,2,1,0:T(4,128)} fusion(f32[1,8,8,4,512]{4,3,2,1,0:T(4,128)} %collective-permute-done.8, f32[1,8,8,4,512]{4,3,2,1,0:T(4,128)} %collective-permute-done.7, f32[1,8,8,4,512]{4,3,2,1,0:T(4,128)} %collective-permute-done.6, f32[1,8,8,4,512]{4,3,2,1,0:T(4,128)S(1)} %copy-done.6), kind=kLoop, calls=%fused_computation | loop fusion | flops 1572864 | bytes 4194304 | tf_op jit(solution)/shard_map/concatenate | solution.py:246
  153.3 4.4 %collective-permute-done.4 = f32[2,2,64,512]{3,2,1,0:T(8,128)} collective-permute-done((f32[2,2,64,512]{3,2,1,0:T(8,128)S(1)}, f32[2,2,64,512]{3,2,1,0:T(8,128)}, u32[]{:S(2)}, u32[]{:S(2)}) %collective-permute-start.4) | collective-permute-done | bytes 524320 | tf_op jit(solution)/shard_map/ppermute | solution.py:145
  159.4 3.3 %collective-permute-done.13.refs_5_ = f32[3,8,8,4,512]{4,3,2,1,0:T(4,128)} collective-permute-done((f32[3,8,8,4,512]{4,3,2,1,0:T(4,128)}, f32[3,8,8,4,512]{4,3,2,1,0:T(4,128)}, u32[]{:S(2)}, u32[]{:S(2)}) %collective-permute-start.13) | collective-permute-done | bytes 1572896 | tf_op jit(solution)/shard_map/ppermute | solution.py:145
  162.7 12.4 %shard_map.98 = f32[512,512]{1,0:T(8,128)S(1)} custom-call(s32[1]{0:T(128)} %bitcast.p_ref.where_ref, bf16[8,512,512]{2,1,0:T(8,128)(2,1)} %copy-done.4, bf16[8,512,512]{2,1,0:T(8,128)(2,1)} %get-tuple-element.32.low_ref, f32[4,8,8,4,512]{4,3,2,1,0:T(4,128)} %pad_maximum_fusion.refs_0_, f32[1,8,8,4,512]{4,3,2,1,0:T(4,128)} %collective-permute-done.9.refs_1_, ...), custom_call_target="tpu_custom_call" | custom-call | flops 1024 | bytes 1024 | tf_op jit(solution)/shard_map/pallas_call | solution.py:128
  175.4 2.0 collective-permute-start.18
  178.9 5.2 %collective-permute-done.14 = f32[64,512]{1,0:T(8,128)S(1)} collective-permute-done((f32[64,512]{1,0:T(8,128)S(1)}, f32[64,512]{1,0:T(8,128)S(1)}, u32[]{:S(2)}, u32[]{:S(2)}) %collective-permute-start.14) | collective-permute-done | bytes 131104 | tf_op jit(solution)/shard_map/ppermute | solution.py:145
  188.3 3.4 %collective-permute-done.19 = f32[2,64,256]{2,1,0:T(8,128)S(1)} collective-permute-done((f32[2,64,256]{2,1,0:T(8,128)S(1)}, f32[2,64,256]{2,1,0:T(8,128)S(1)}, u32[]{:S(2)}, u32[]{:S(2)}) %collective-permute-start.19) | collective-permute-done | bytes 131104 | tf_op jit(solution)/shard_map/ppermute | solution.py:145
  194.8 3.0 %collective-permute-done.20 = f32[64,256]{1,0:T(8,128)S(1)} collective-permute-done((f32[64,256]{1,0:T(8,128)S(1)}, f32[64,256]{1,0:T(8,128)S(1)}, u32[]{:S(2)}, u32[]{:S(2)}) %collective-permute-start.20) | collective-permute-done | bytes 65568 | tf_op jit(solution)/shard_map/ppermute | solution.py:145
  199.4 3.9 %all-to-all-start.1 = ((f32[32,1,64]{2,1,0:T(1,128)}), f32[32,1,64]{2,1,0:T(1,128)S(1)}, u32[]{:S(2)}, u32[]{:S(2)}) async-start(f32[32,1,64]{2,1,0:T(1,128)} %broadcast_in_dim.18), calls=%async_computation.1 | async-start | bytes 32768 | tf_op jit(solution)/shard_map/all_to_all | solution.py:185
  204.4 6.1 %all-to-all-done.1 = f32[32,1,64]{2,1,0:T(1,128)S(1)} async-done(((f32[32,1,64]{2,1,0:T(1,128)}), f32[32,1,64]{2,1,0:T(1,128)S(1)}, u32[]{:S(2)}, u32[]{:S(2)}) %all-to-all-start.1) | async-done | bytes 8224 | tf_op jit(solution)/shard_map/all_to_all | solution.py:185
  (101 shorter events, 37.1 us)
Async XLA Ops:
  0.6 24.5 %collective-permute-start.1 = (f32[1,8,64,4,512]{4,3,2,1,0:T(4,128)}, f32[1,8,64,4,512]{4,3,2,1,0:T(4,128)}, u32[]{:S(2)}, u32[]{:S(2)}) collective-permute-start(f32[1,8,64,4,512]{4,3,2,1,0:T(4,128)} %bitcast.69), channel_id=1, source_target_pairs={{0,1},{1,0},{2,3},{3,2},{4,5},{5,4},{6,7},{7,6},{8,9},{9,8},{10,11... | collective-permute-start | bytes 12582920 | tf_op jit(solution)/shard_map/ppermute | solution.py:145
  1.1 94.1 %collective-permute-start = (f32[1,8,64,4,512]{4,3,2,1,0:T(4,128)}, f32[1,8,64,4,512]{4,3,2,1,0:T(4,128)}, u32[]{:S(2)}, u32[]{:S(2)}) collective-permute-start(f32[1,8,64,4,512]{4,3,2,1,0:T(4,128)} %bitcast.70), channel_id=1, source_target_pairs={{0,2},{1,3},{2,0},{3,1},{4,6},{5,7},{6,4},{7,5},{8,10},{9,11},{10,... | collective-permute-start | bytes 12582920 | tf_op jit(solution)/shard_map/ppermute | solution.py:145
  8.6 99.4 %all-to-all-start = ((f32[8,8,8,4,512]{4,3,2,1,0:T(4,128)}), f32[8,8,8,4,512]{4,3,2,1,0:T(4,128)}, u32[]{:S(2)}, u32[]{:S(2)}) async-start(f32[8,8,8,4,512]{4,3,2,1,0:T(4,128)} %copy-done.3), calls=%async_computation | async-start | bytes 8388608 | tf_op jit(solution)/shard_map/all_to_all | solution.py:202
  95.2 12.8 %collective-permute-start.2 = (f32[1,8,64,4,512]{4,3,2,1,0:T(4,128)}, f32[1,8,64,4,512]{4,3,2,1,0:T(4,128)}, u32[]{:S(2)}, u32[]{:S(2)}) collective-permute-start(f32[1,8,64,4,512]{4,3,2,1,0:T(4,128)} %collective-permute-done.refs_0_), channel_id=1, source_target_pairs={{0,1},{1,0},{2,3},{3,2},{4,5},{5,4},{6,7},{7,6},{8,9},{9,8},{10,11... | collective-permute-start | bytes 12582920 | tf_op jit(solution)/shard_map/ppermute | solution.py:145
  108.0 7.5 %collective-permute-start.3 = (f32[8,8,8,4,512]{4,3,2,1,0:T(4,128)}, f32[8,8,8,4,512]{4,3,2,1,0:T(4,128)}, u32[]{:S(2)}, u32[]{:S(2)}) collective-permute-start(f32[8,8,8,4,512]{4,3,2,1,0:T(4,128)} %all-to-all-done), channel_id=1, source_target_pairs={{0,1},{1,0},{2,3},{3,2},{4,5},{5,4},{6,7},{7,6},{8,9},{9,8},{10,11... | collective-permute-start | bytes 12582920 | tf_op jit(solution)/shard_map/ppermute | solution.py:145
  110.8 48.0 %collective-permute-start.10 = (f32[3,8,8,4,512]{4,3,2,1,0:T(4,128)}, f32[3,8,8,4,512]{4,3,2,1,0:T(4,128)}, u32[]{:S(2)}, u32[]{:S(2)}) collective-permute-start(f32[3,8,8,4,512]{4,3,2,1,0:T(4,128)} %bitcast.12), channel_id=1, source_target_pairs={{0,2},{1,3},{2,0},{3,1},{4,6},{5,7},{6,4},{7,5},{8,10},{9,11},{10,... | collective-permute-start | bytes 4718600 | tf_op jit(solution)/shard_map/ppermute | solution.py:145
  111.4 32.4 %collective-permute-start.8 = (f32[1,8,8,4,512]{4,3,2,1,0:T(4,128)}, f32[1,8,8,4,512]{4,3,2,1,0:T(4,128)}, u32[]{:S(2)}, u32[]{:S(2)}) collective-permute-start(f32[1,8,8,4,512]{4,3,2,1,0:T(4,128)} %shard_map.93), channel_id=1, source_target_pairs={{0,12},{4,8},{8,4},{12,0},{16,28},{20,24},{24,20},{28,16},{1,13},{... | collective-permute-start | bytes 1572872 | tf_op jit(solution)/shard_map/ppermute | solution.py:145
  112.3 36.9 %collective-permute-start.7 = (f32[1,8,8,4,512]{4,3,2,1,0:T(4,128)}, f32[1,8,8,4,512]{4,3,2,1,0:T(4,128)}, u32[]{:S(2)}, u32[]{:S(2)}) collective-permute-start(f32[1,8,8,4,512]{4,3,2,1,0:T(4,128)} %shard_map.92), channel_id=1, source_target_pairs={{0,8},{4,12},{8,0},{12,4},{16,24},{20,28},{24,16},{28,20},{1,9},{5... | collective-permute-start | bytes 1572872 | tf_op jit(solution)/shard_map/ppermute | solution.py:145
  114.3 34.8 %collective-permute-start.9 = (f32[1,8,8,4,512]{4,3,2,1,0:T(4,128)}, f32[1,8,8,4,512]{4,3,2,1,0:T(4,128)}, u32[]{:S(2)}, u32[]{:S(2)}) collective-permute-start(f32[1,8,8,4,512]{4,3,2,1,0:T(4,128)} %shard_map.94), channel_id=1, source_target_pairs={{0,16},{4,20},{8,24},{12,28},{16,0},{20,4},{24,8},{28,12},{1,17},{... | collective-permute-start | bytes 1572872 | tf_op jit(solution)/shard_map/ppermute | solution.py:145
  115.5 33.7 %collective-permute-start.6 = (f32[1,8,8,4,512]{4,3,2,1,0:T(4,128)}, f32[1,8,8,4,512]{4,3,2,1,0:T(4,128)}, u32[]{:S(2)}, u32[]{:S(2)}) collective-permute-start(f32[1,8,8,4,512]{4,3,2,1,0:T(4,128)} %shard_map.91), channel_id=1, source_target_pairs={{0,4},{4,0},{8,12},{12,8},{16,20},{20,16},{24,28},{28,24},{1,5},{5... | collective-permute-start | bytes 1572872 | tf_op jit(solution)/shard_map/ppermute | solution.py:145
  143.8 13.9 %collective-permute-start.4 = (f32[2,2,64,512]{3,2,1,0:T(8,128)S(1)}, f32[2,2,64,512]{3,2,1,0:T(8,128)}, u32[]{:S(2)}, u32[]{:S(2)}) collective-permute-start(f32[2,2,64,512]{3,2,1,0:T(8,128)S(1)} %dynamic-slice_bitcast_fusion), channel_id=1, source_target_pairs={{0,4},{4,0},{8,12},{12,8},{16,20},{20,16},{24,28},{28,24},{1,5},{5... | collective-permute-start | bytes 1572872 | tf_op jit(solution)/shard_map/ppermute | solution.py:145
  149.2 9.6 %collective-permute-start.12 = (f32[1,8,8,4,512]{4,3,2,1,0:T(4,128)}, f32[1,8,8,4,512]{4,3,2,1,0:T(4,128)S(1)}, u32[]{:S(2)}, u32[]{:S(2)}) collective-permute-start(f32[1,8,8,4,512]{4,3,2,1,0:T(4,128)} %collective-permute-done.9.refs_1_), channel_id=1, source_target_pairs={{0,1},{1,0},{2,3},{3,2},{4,5},{5,4},{6,7},{7,6},{8,9},{9,8},{10,11... | collective-permute-start | bytes 1572872 | tf_op jit(solution)/shard_map/ppermute | solution.py:145
  152.8 9.9 %collective-permute-start.11 = (f32[4,8,8,4,512]{4,3,2,1,0:T(4,128)}, f32[4,8,8,4,512]{4,3,2,1,0:T(4,128)}, u32[]{:S(2)}, u32[]{:S(2)}) collective-permute-start(f32[4,8,8,4,512]{4,3,2,1,0:T(4,128)} %pad_maximum_fusion.refs_0_), channel_id=1, source_target_pairs={{0,1},{1,0},{2,3},{3,2},{4,5},{5,4},{6,7},{7,6},{8,9},{9,8},{10,11... | collective-permute-start | bytes 6291464 | tf_op jit(solution)/shard_map/ppermute | solution.py:145
  158.8 3.8 %collective-permute-start.13 = (f32[3,8,8,4,512]{4,3,2,1,0:T(4,128)}, f32[3,8,8,4,512]{4,3,2,1,0:T(4,128)}, u32[]{:S(2)}, u32[]{:S(2)}) collective-permute-start(f32[3,8,8,4,512]{4,3,2,1,0:T(4,128)} %collective-permute-done.10.refs_2_), channel_id=1, source_target_pairs={{0,1},{1,0},{2,3},{3,2},{4,5},{5,4},{6,7},{7,6},{8,9},{9,8},{10,11... | collective-permute-start | bytes 4718600 | tf_op jit(solution)/shard_map/ppermute | solution.py:145
  159.3 15.9 %collective-permute-start.5 = (f32[2,64,512]{2,1,0:T(8,128)S(1)}, f32[2,64,512]{2,1,0:T(8,128)S(1)}, u32[]{:S(2)}, u32[]{:S(2)}) collective-permute-start(f32[2,64,512]{2,1,0:T(8,128)S(1)} %dynamic-slice_bitcast_fusion.3), channel_id=1, source_target_pairs={{0,8},{4,12},{8,0},{12,4},{16,24},{20,28},{24,16},{28,20},{1,9},{5... | collective-permute-start | bytes 786440 | tf_op jit(solution)/shard_map/ppermute | solution.py:145
  175.2 8.8 %collective-permute-start.14 = (f32[64,512]{1,0:T(8,128)S(1)}, f32[64,512]{1,0:T(8,128)S(1)}, u32[]{:S(2)}, u32[]{:S(2)}) collective-permute-start(f32[64,512]{1,0:T(8,128)S(1)} %dynamic-slice_bitcast_fusion.6), channel_id=1, source_target_pairs={{0,16},{4,20},{8,24},{12,28},{16,0},{20,4},{24,8},{28,12},{1,17},{... | collective-permute-start | bytes 393224 | tf_op jit(solution)/shard_map/ppermute | solution.py:145
  175.4 11.2 %collective-permute-start.18 = (f32[2,2,64,256]{3,2,1,0:T(8,128)S(1)}, f32[2,2,64,256]{3,2,1,0:T(8,128)S(1)}, u32[]{:S(2)}, u32[]{:S(2)}) collective-permute-start(f32[2,2,64,256]{3,2,1,0:T(8,128)S(1)} %dynamic-slice_bitcast_fusion.1), channel_id=1, source_target_pairs={{0,8},{4,12},{8,0},{12,4},{16,24},{20,28},{24,16},{28,20},{1,9},{5... | collective-permute-start | bytes 786440 | tf_op jit(solution)/shard_map/ppermute | solution.py:145
  177.4 26.0 %copy-start.7 = (f32[16]{0:T(128)S(1)}, f32[16]{0:T(128)}, u32[]{:S(2)}) copy-start(f32[16]{0:T(128)} %param.12) | copy-start | bytes 196
  177.4 10.6 %collective-permute-start.15 = (f32[2,2,64,256]{3,2,1,0:T(8,128)S(1)}, f32[2,2,64,256]{3,2,1,0:T(8,128)S(1)}, u32[]{:S(2)}, u32[]{:S(2)}) collective-permute-start(f32[2,2,64,256]{3,2,1,0:T(8,128)S(1)} %dynamic-slice_bitcast_fusion.2), channel_id=1, source_target_pairs={{0,4},{4,0},{8,12},{12,8},{16,20},{20,16},{24,28},{28,24},{1,5},{5... | collective-permute-start | bytes 786440 | tf_op jit(solution)/shard_map/ppermute | solution.py:145
  186.6 5.0 %collective-permute-start.19 = (f32[2,64,256]{2,1,0:T(8,128)S(1)}, f32[2,64,256]{2,1,0:T(8,128)S(1)}, u32[]{:S(2)}, u32[]{:S(2)}) collective-permute-start(f32[2,64,256]{2,1,0:T(8,128)S(1)} %dynamic-slice_bitcast_fusion.4), channel_id=1, source_target_pairs={{0,4},{4,0},{8,12},{12,8},{16,20},{20,16},{24,28},{28,24},{1,5},{5... | collective-permute-start | bytes 393224 | tf_op jit(solution)/shard_map/ppermute | solution.py:145
  188.1 5.0 %collective-permute-start.16 = (f32[2,64,256]{2,1,0:T(8,128)S(1)}, f32[2,64,256]{2,1,0:T(8,128)S(1)}, u32[]{:S(2)}, u32[]{:S(2)}) collective-permute-start(f32[2,64,256]{2,1,0:T(8,128)S(1)} %dynamic-slice_bitcast_fusion.5), channel_id=1, source_target_pairs={{0,8},{4,12},{8,0},{12,4},{16,24},{20,28},{24,16},{28,20},{1,9},{5... | collective-permute-start | bytes 393224 | tf_op jit(solution)/shard_map/ppermute | solution.py:145
  191.7 6.1 %collective-permute-start.20 = (f32[64,256]{1,0:T(8,128)S(1)}, f32[64,256]{1,0:T(8,128)S(1)}, u32[]{:S(2)}, u32[]{:S(2)}) collective-permute-start(f32[64,256]{1,0:T(8,128)S(1)} %dynamic-slice_bitcast_fusion.7), channel_id=1, source_target_pairs={{0,16},{4,20},{8,24},{12,28},{16,0},{20,4},{24,8},{28,12},{1,17},{... | collective-permute-start | bytes 196616 | tf_op jit(solution)/shard_map/ppermute | solution.py:145
  193.2 5.3 %collective-permute-start.17 = (f32[64,256]{1,0:T(8,128)S(1)}, f32[64,256]{1,0:T(8,128)S(1)}, u32[]{:S(2)}, u32[]{:S(2)}) collective-permute-start(f32[64,256]{1,0:T(8,128)S(1)} %dynamic-slice_bitcast_fusion.8), channel_id=1, source_target_pairs={{0,16},{4,20},{8,24},{12,28},{16,0},{20,4},{24,8},{28,12},{1,17},{... | collective-permute-start | bytes 196616 | tf_op jit(solution)/shard_map/ppermute | solution.py:145
  199.4 11.1 %all-to-all-start.1 = ((f32[32,1,64]{2,1,0:T(1,128)}), f32[32,1,64]{2,1,0:T(1,128)S(1)}, u32[]{:S(2)}, u32[]{:S(2)}) async-start(f32[32,1,64]{2,1,0:T(1,128)} %broadcast_in_dim.18), calls=%async_computation.1 | async-start | bytes 32768 | tf_op jit(solution)/shard_map/all_to_all | solution.py:185
  (10 other events, 66.8 us)
